TPU v7x, 512 devices: a whole 4x8x8 slice. The times are simulated.
512 devices in a mesh: sec: 2 (over core), grp: 16 (over y_hi, x), dev: 16 (over y_lo, z).
Axes of the slice: x: 4, y: 8 (y_hi: 4, y_lo: 2; y = y_hi * 2 + y_lo), z: 8, core: 2. Of those that a mesh axis runs over, the one named last changes fastest.
Arguments:
- q_latent: bfloat16 [256, 128, 512], P(('grp', 'dev')), may hold values from -16 to 16
- q_rope: bfloat16 [256, 8192], P(('grp', 'dev')), may hold values from -6 to 6
- cache_latent: bfloat16 [256, 2048, 512], P(('grp', 'dev'), 'sec'), may hold values from -6 to 6
- cache_rope: bfloat16 [256, 64, 2048], P(('grp', 'dev'), None, 'sec'), may hold values from -6 to 6
- lengths: int32 [256], P(('grp', 'dev')), may hold values from 2 to 2048
- w_uv: bfloat16 [128, 512, 128], P(('sec', 'grp')), may hold values from -1 to 1
- w_out: bfloat16 [16384, 7168], P(('sec', 'grp'), 'dev'), may hold values from -0.046875 to 0.046875
- resid: bfloat16 [256, 7168], P(('sec', 'grp'), 'dev'), may hold values from -6 to 6
- norm_gain: float32 [7168], P('dev'), may hold values from 0.1 to 1.9
- router: float32 [7168, 16], P('dev'), may hold values from -0.0625 to 0.0625
- routes: int32 [256, 8], P(('sec', 'grp')), may hold values from 0 to 15, as said below
- slots: int32 [256, 8], P(('sec', 'grp')), may hold values from 0 to 7, as said below
- w_gateup: bfloat16 [16, 7168, 2, 2048], P('grp', 'dev', None, 'sec'), may hold values from -0.0625 to 0.0625
- w_down: bfloat16 [16, 2048, 7168], P('grp', 'sec', 'dev'), may hold values from -0.125 to 0.125
Outputs:
- layer_out: bfloat16 [256, 7168], P(('sec', 'grp'), 'dev')
Inputs may be any that keep to these rules, and one draw needn't show every extreme that they name: `routes`: each row names 8 different experts; one expert is named by every row. Within each aligned block of 8 rows, the routes that name one expert hold the slots 0, 1, ... up to their number less one, each once.
All inputs are finite; a program needn't handle non-finite values.
Results may differ from a plain program's by a relative error of at most 0.033.
Values may be sent and summed in bfloat16 or wider, within the bound.
No kernel may reach another device: no remote copies, remote signals or barrier semaphores. Data moves between devices by JAX's collectives and lax.ppermute only.
A program may use at most 64 MiB of HBM per device.

v0:
```python
import jax
import jax.numpy as jnp
from jax import lax
from jax.sharding import PartitionSpec as P

score_scale = 0.07216878364870323
route_scale = 2.5
norm_eps = 1e-06
masked_floor = -1e30


def merged_2(value, axis, join):
    gathered = jax.tree.map(
        lambda a, kind: lax.all_gather(a.astype(kind), axis),
        value,
        (jnp.bfloat16, jnp.bfloat16, jnp.bfloat16),
    )

    def take(source):
        return jax.tree.map(
            lambda a, own: lax.dynamic_index_in_dim(a, source, 0, False).astype(own.dtype),
            gathered,
            value,
        )

    return lax.fori_loop(
        1, lax.axis_size(axis), lambda source, state: join(state, take(source)), take(0)
    )


def join_parts(former, latter):
    top_former, mass_former, weighted_former = former
    top_latter, mass_latter, weighted_latter = latter
    top_both = jnp.maximum(top_former, top_latter)
    factor_former = jnp.exp(top_former - top_both)
    factor_latter = jnp.exp(top_latter - top_both)
    return (
        top_both,
        mass_former * factor_former + mass_latter * factor_latter,
        weighted_former * factor_former[..., None] + weighted_latter * factor_latter[..., None],
    )


def body(
    q_latent,
    q_rope,
    cache_latent,
    cache_rope,
    lengths,
    w_uv,
    w_out,
    resid,
    norm_gain,
    router,
    routes,
    slots,
    w_gateup,
    w_down,
):
    sections = lax.axis_size("sec")
    groups = lax.axis_size("grp")
    members = lax.axis_size("dev")
    section = lax.axis_index("sec")
    row_count, head_total, latent = q_latent.shape
    hist_local = cache_latent.shape[1]
    rope_width = cache_rope.shape[1]
    half_heads = head_total // sections
    head_block = w_uv.shape[0]
    rope_query = q_rope.reshape(row_count, head_total, rope_width)
    scores = (
        jnp.einsum("rhc,rpc->rhp", q_latent, cache_latent, preferred_element_type=jnp.float32)
        + jnp.einsum("rhj,rjp->rhp", rope_query, cache_rope, preferred_element_type=jnp.float32)
    ) * score_scale
    positions = section * hist_local + jnp.arange(hist_local, dtype=jnp.int32)
    usable = (positions[None, :] < lengths[:, None])[:, None, :]
    masked = jnp.where(usable, scores, masked_floor)
    top_score = jnp.max(masked, axis=-1)
    expon = jnp.where(usable, jnp.exp(masked - top_score[..., None]), 0.0)
    mass_sum = jnp.sum(expon, axis=-1)
    weighted = jnp.einsum(
        "rhp,rpc->rhc", expon.astype(jnp.bfloat16), cache_latent, preferred_element_type=jnp.float32
    )
    mine_start = section * half_heads
    merged = merged_2((top_score, mass_sum, weighted), "sec", join_parts)
    top_mine, mass_mine, weighted_mine = [
        lax.dynamic_slice_in_dim(quantity, mine_start, half_heads, 1) for quantity in merged
    ]
    latent_out = (weighted_mine / mass_mine[..., None]).astype(jnp.bfloat16)
    outgoing_heads = latent_out.reshape(row_count, groups, head_block, latent)
    arrived = lax.all_to_all(outgoing_heads, "grp", split_axis=1, concat_axis=0, tiled=True)
    arrived = arrived.reshape(groups * row_count, head_block, latent)
    values = jnp.einsum("nhc,hcv->nhv", arrived, w_uv, preferred_element_type=jnp.float32).astype(
        jnp.bfloat16
    )
    width_heads = head_block * w_uv.shape[2]
    values = values.reshape(groups * row_count, width_heads)
    gathered = lax.all_gather(values, "dev", axis=0, tiled=True)
    natural = gathered.reshape(members, groups, row_count, width_heads).transpose(1, 0, 2, 3)
    natural = natural.reshape(members * groups * row_count, width_heads)
    block_rows = resid.shape[0]
    attention = lax.psum_scatter(
        jnp.dot(natural, w_out, preferred_element_type=jnp.float32).astype(jnp.bfloat16),
        ("sec", "grp"),
        scatter_dimension=0,
        tiled=True,
    ).astype(jnp.float32)
    hidden_state = resid.astype(jnp.float32) + attention
    gained = hidden_state * norm_gain
    square_sum = jnp.sum(hidden_state * hidden_state, axis=-1)
    router_part = jnp.dot(gained, router, precision=lax.Precision.HIGHEST)
    square_total, logit_total = lax.psum((square_sum, router_part), "dev")
    model_width = norm_gain.shape[0] * members
    inverse_rms = lax.rsqrt(square_total / model_width + norm_eps)
    logits = logit_total * inverse_rms[:, None]
    normed = (gained * inverse_rms[:, None]).astype(jnp.bfloat16)
    expert_total = router.shape[1]
    capacity = max(2, 3 * block_rows // 4)
    expert_ids = jnp.arange(expert_total, dtype=jnp.int32)
    chosen_mask = routes[:, :, None] == expert_ids[None, None, :]
    sigmoid_scores = jax.nn.sigmoid(logits)
    picked = jnp.sum(jnp.where(chosen_mask, sigmoid_scores[:, None, :], 0.0), axis=-1)
    route_weight = route_scale * picked / jnp.sum(picked, axis=-1, keepdims=True)
    kept = slots < capacity
    route_weight = jnp.where(kept, route_weight, 0.0)
    slot_index = routes * capacity + slots
    slot_ids = jnp.arange(expert_total * capacity, dtype=jnp.int32)
    placement_matrix = jnp.any(
        (slot_index[:, :, None] == slot_ids[None, None, :]) & kept[:, :, None], axis=1
    ).astype(jnp.bfloat16)
    width_local = normed.shape[1]
    buffer = jnp.einsum("be,bd->ed", placement_matrix, normed, preferred_element_type=jnp.float32)
    buffer = buffer.astype(jnp.bfloat16).reshape(expert_total, capacity, width_local)
    received = lax.all_to_all(buffer, "grp", split_axis=0, concat_axis=1, tiled=True)
    received = lax.all_gather(received, "sec", axis=1, tiled=True)
    incoming_rows = received[0]
    padded_rows = incoming_rows.shape[0]
    gate_weights = w_gateup[0]
    partial_gate = jnp.einsum(
        "pd,dtf->ptf", incoming_rows, gate_weights, preferred_element_type=jnp.float32
    )
    gate_total = lax.psum(partial_gate.astype(jnp.bfloat16), "dev").astype(jnp.float32)
    activated = (jax.nn.silu(gate_total[:, 0]) * gate_total[:, 1]).astype(jnp.bfloat16)
    down_part = jnp.dot(activated, w_down[0], preferred_element_type=jnp.float32)
    down_total = lax.psum_scatter(
        down_part.reshape(sections, padded_rows // sections, width_local).astype(jnp.bfloat16),
        "sec",
        scatter_dimension=0,
        tiled=True,
    )
    expert_rows = down_total.reshape(groups, capacity, width_local)
    returned = lax.all_to_all(expert_rows, "grp", split_axis=0, concat_axis=0, tiled=True)
    returned = returned.reshape(expert_total * capacity, width_local)
    safe_index = jnp.where(kept, slot_index, 0)
    fetched = returned[safe_index]
    mixture = jnp.sum(route_weight[:, :, None] * fetched.astype(jnp.float32), axis=1)
    return (hidden_state + mixture).astype(jnp.bfloat16)


def solution(mesh):
    in_specs = (
        P(("grp", "dev"), None, None),
        P(("grp", "dev"), None),
        P(("grp", "dev"), "sec", None),
        P(("grp", "dev"), None, "sec"),
        P(("grp", "dev")),
        P(("sec", "grp"), None, None),
        P(("sec", "grp"), "dev"),
        P(("sec", "grp"), "dev"),
        P("dev"),
        P("dev", None),
        P(("sec", "grp"), None),
        P(("sec", "grp"), None),
        P("grp", "dev", None, "sec"),
        P("grp", "sec", "dev"),
    )
    out_specs = P(("sec", "grp"), "dev")
    return jax.shard_map(body, mesh=mesh, in_specs=in_specs, out_specs=out_specs, check_vma=False)
```

profile of v0, /device:TPU:1, one launch (start us, length us, event | category | flops | bytes accessed | tf_op | source)
XLA Modules:
  0.0 402.9 jit_solution(10967352460992047660)
XLA Ops:
  7.3 0.9 reduce.5
  8.2 0.1 reshape.317
  8.3 1.1 fusion.23
  9.4 1.9 fusion.46
  11.3 0.2 fusion.12
  11.6 0.4 convolution_convert_fusion.2
  12.0 8.5 %all-gather.3 = bf16[2,1,128]{2,1,0:T(2,128)(2,1)S(1)} all-gather(bf16[1,1,128]{2,1,0:T(2,128)(2,1)S(1)} %convert_bitcast_fusion.1), channel_id=3, replica_groups=mesh['sec'=2,'grp'=16,'dev'=16] {'sec'}, dimensions={0}, use_global_device_ids=true | all-gather | bytes 768 | tf_op jit(solution)/shard_map/all_gather | solution.py:14
  20.4 1.8 all-gather.4
  22.2 0.1 fusion.41
  22.3 0.1 dynamic-slice
  22.4 0.1 dynamic-slice.1
  22.4 2.0 all-gather
  24.5 0.1 fusion.22
  24.6 12.8 %all_to_all.26 = bf16[1,16,4,512]{3,2,0,1:T(4,128)(2,1)S(1)} all-to-all(bf16[1,16,4,512]{3,2,0,1:T(4,128)(2,1)S(1)} %bitcast.106), channel_id=1, replica_groups=mesh['sec'=2,'grp'=16,'dev'=16] {'grp'}, dimensions={1} | all-to-all | bytes 131072 | tf_op jit(solution)/shard_map/all_to_all | solution.py:90
  37.4 0.2 fusion.7
  37.6 32.9 %all_gather.24 = bf16[256,512]{1,0:T(8,128)(2,1)S(1)} all-gather(bf16[16,512]{1,0:T(8,128)(2,1)S(1)} %bitcast.107), channel_id=1, replica_groups=mesh['sec'=2,'grp'=16,'dev'=16] {'dev'}, dimensions={0}, use_global_device_ids=true | all-gather | bytes 278528 | tf_op jit(solution)/shard_map/all_gather | solution.py:97
  70.5 0.1 copy.29
  70.6 1.0 convolution_convert_fusion
  71.6 0.0 reduce-scatter.3.cloned.1.call-update
  71.7 0.0 all-reduce.3.cloned.1.call-start
  71.7 92.9 %reduce-scatter.3.cloned.1.call-done = bf16[8,448]{1,0:T(8,128)(2,1)} async-done(((bf16[256,448]{1,0:T(8,128)(2,1)}), bf16[8,448]{1,0:T(8,128)(2,1)}) %reduce-scatter.3.cloned.1.call-update) | async-done | bytes 7184 | tf_op jit(solution)/shard_map/reduce_scatter | solution.py:101
  164.7 0.8 fusion.30
  165.5 0.8 multiply_reduce_fusion
  166.3 28.1 %all-reduce = (f32[8]{0:T(128)S(1)}, f32[8,16]{1,0:T(8,128)S(1)}) all-reduce(f32[8]{0:T(128)S(1)} %multiply_reduce_fusion, f32[8,16]{1,0:T(8,128)S(1)} %fusion.30), channel_id=1, replica_groups=mesh['sec'=2,'grp'=16,'dev'=16] {'dev'}, use_global_device_ids=true, to_apply=%region_5.6 | all-reduce | flops 136 | bytes 1088 | tf_op jit(solution)/shard_map/psum | solution.py:111
  194.5 0.1 add_divide_fusion
  194.6 0.2 select_reduce_fusion
  194.8 0.1 divide_select_fusion
  194.9 0.1 fusion.29
  195.0 1.0 convolution_convert_fusion.3
  195.9 0.1 reshape.324
  196.0 14.3 %all_to_all.27 = bf16[16,6,448]{2,1,0:T(8,128)(2,1)S(1)} all-to-all(bf16[16,6,448]{2,1,0:T(8,128)(2,1)S(1)} %reshape.324), channel_id=1, replica_groups=mesh['sec'=2,'grp'=16,'dev'=16] {'grp'}, dimensions={0} | all-to-all | bytes 172032 | tf_op jit(solution)/shard_map/all_to_all | solution.py:133
  210.3 0.1 all_to_all.10
  210.4 13.1 %all_gather.25 = bf16[1,192,448]{2,1,0:T(8,128)(2,1)S(1)} all-gather(bf16[1,96,448]{2,1,0:T(8,128)(2,1)S(1)} %all_to_all.10), channel_id=1, replica_groups=mesh['sec'=2,'grp'=16,'dev'=16] {'sec'}, dimensions={1}, use_global_device_ids=true | all-gather | bytes 258048 | tf_op jit(solution)/shard_map/all_gather | solution.py:134
  223.5 1.7 fusion.2
  225.2 0.0 reduce-scatter.5.cloned.1.call-start
  225.3 122.5 %all-reduce.3.cloned.1.call-done = bf16[192,2,1024]{2,0,1:T(8,128)(2,1)} async-done(((bf16[192,2,1024]{2,0,1:T(8,128)(2,1)}), bf16[192,2,1024]{2,0,1:T(8,128)(2,1)}) %all-reduce.3.cloned.1.call-update) | async-done | bytes 786448 | tf_op jit(solution)/shard_map/psum | solution.py:141
  347.8 1.3 convert_element_type.231
  349.1 0.2 fusion.11
  349.4 1.1 convolution_convert_fusion.1
  350.5 25.5 %reduce-scatter.5.cloned.1.call-done = bf16[1,96,448]{2,1,0:T(8,128)(2,1)} async-done(((bf16[2,96,448]{2,1,0:T(8,128)(2,1)}), bf16[1,96,448]{2,1,0:T(8,128)(2,1)}) %reduce-scatter.5.cloned.1.call-update) | async-done | bytes 86032 | tf_op jit(solution)/shard_map/reduce_scatter | solution.py:144
  376.0 1.6 reshape.325
  377.5 8.0 %all-to-all-start.2 = ((bf16[16,6,448]{2,1,0:T(8,128)(2,1)}), bf16[16,6,448]{2,1,0:T(8,128)(2,1)S(1)}, u32[]{:S(2)}, u32[]{:S(2)}) async-start(bf16[16,6,448]{2,1,0:T(8,128)(2,1)} %reshape.325), calls=%async_computation.4 | async-start | bytes 262144 | tf_op jit(solution)/shard_map/all_to_all | solution.py:151
  385.5 0.1 reshape.337
  385.6 9.2 %all-to-all-done.2 = bf16[16,6,448]{2,1,0:T(8,128)(2,1)S(1)} async-done(((bf16[16,6,448]{2,1,0:T(8,128)(2,1)}), bf16[16,6,448]{2,1,0:T(8,128)(2,1)S(1)}, u32[]{:S(2)}, u32[]{:S(2)}) %all-to-all-start.2) | async-done | bytes 86048 | tf_op jit(solution)/shard_map/all_to_all | solution.py:151
  394.9 0.1 reshape.326
  394.9 0.7 gather_fusion
  395.6 0.1 fusion.19
  395.8 0.6 add_convert_fusion
  (35 shorter events, 0.2 us)
Async XLA Ops:
  6.5 217.0 %copy-start = (bf16[1,448,2,1024]{3,2,1,0:T(2,128)(2,1)S(1)}, bf16[1,448,2,1024]{3,2,1,0:T(2,128)(2,1)}, u32[]{:S(2)}) copy-start(bf16[1,448,2,1024]{3,2,1,0:T(2,128)(2,1)} %param.26) | copy-start | bytes 5505028
  6.5 5.0 %copy-start.1 = (bf16[1,1024,512]{2,1,0:T(8,128)(2,1)S(1)}, bf16[1,1024,512]{2,1,0:T(8,128)(2,1)}, u32[]{:S(2)}) copy-start(bf16[1,1024,512]{2,1,0:T(8,128)(2,1)} %param.16) | copy-start | bytes 3145732
  6.5 158.1 %reduce-scatter.3.cloned.1.call-start = ((), (), s32[]{:S(2)}) async-start(), calls=%async_computation.5 | async-start | bytes 270336 | tf_op jit(solution)/shard_map/reduce_scatter | solution.py:101
  11.3 26.1 %copy-start.3 = (bf16[4,512,128]{2,1,0:T(8,128)(2,1)S(1)}, bf16[4,512,128]{2,1,0:T(8,128)(2,1)}, u32[]{:S(2)}) copy-start(bf16[4,512,128]{2,1,0:T(8,128)(2,1)} %param.19) | copy-start | bytes 1572868
  11.9 58.7 %copy-start.4 = (bf16[512,448]{0,1:T(8,128)(2,1)S(1)}, bf16[512,448]{0,1:T(8,128)(2,1)}, u32[]{:S(2)}) copy-start(bf16[512,448]{0,1:T(8,128)(2,1)} %param.20) | copy-start | bytes 1376260
  24.4 140.2 %copy-start.5 = (bf16[8,448]{1,0:T(8,128)(2,1)S(1)}, bf16[8,448]{1,0:T(8,128)(2,1)}, u32[]{:S(2)}) copy-start(bf16[8,448]{1,0:T(8,128)(2,1)} %param.21) | copy-start | bytes 21508
  24.4 140.2 %copy-start.7 = (f32[448,16]{0,1:T(8,128)S(1)}, f32[448,16]{0,1:T(8,128)}, u32[]{:S(2)}) copy-start(f32[448,16]{0,1:T(8,128)} %param.23) | copy-start | bytes 86020
  24.4 140.2 %copy-start.10 = (f32[448]{0:T(512)S(1)}, f32[448]{0:T(512)}, u32[]{:S(2)}) copy-start(f32[448]{0:T(512)} %param.22) | copy-start | bytes 5380
  24.4 170.1 %copy-start.8 = (s32[8,8]{1,0:T(8,128)S(1)}, s32[8,8]{1,0:T(8,128)}, u32[]{:S(2)}) copy-start(s32[8,8]{1,0:T(8,128)} %param.24) | copy-start | bytes 772
  24.4 170.3 %copy-start.9 = (s32[8,8]{1,0:T(8,128)S(1)}, s32[8,8]{1,0:T(8,128)}, u32[]{:S(2)}) copy-start(s32[8,8]{1,0:T(8,128)} %param.25) | copy-start | bytes 772
  71.7 276.1 %all-reduce.3.cloned.1.call-start = ((), (), s32[]{:S(2)}) async-start(), calls=%async_computation.6 | async-start | bytes 1572864 | tf_op jit(solution)/shard_map/psum | solution.py:141
  225.2 124.1 %copy-start.2 = (bf16[1,1024,448]{1,2,0:T(8,128)(2,1)S(1)}, bf16[1,1024,448]{1,2,0:T(8,128)(2,1)}, u32[]{:S(2)}) copy-start(bf16[1,1024,448]{1,2,0:T(8,128)(2,1)} %param.27) | copy-start | bytes 2752516
  225.2 150.8 %reduce-scatter.5.cloned.1.call-start = ((), (), s32[]{:S(2)}) async-start(), calls=%async_computation.7 | async-start | bytes 294912 | tf_op jit(solution)/shard_map/reduce_scatter | solution.py:144
  349.3 46.4 %copy-start.6 = (bf16[8,448]{1,0:T(8,128)(2,1)S(1)}, bf16[8,448]{1,0:T(8,128)(2,1)}, u32[]{:S(2)}) copy-start(bf16[8,448]{1,0:T(8,128)(2,1)} %reduce-scatter.3.cloned.1.call-done) | copy-start | bytes 21508
  377.5 17.3 %all-to-all-start.2 = ((bf16[16,6,448]{2,1,0:T(8,128)(2,1)}), bf16[16,6,448]{2,1,0:T(8,128)(2,1)S(1)}, u32[]{:S(2)}, u32[]{:S(2)}) async-start(bf16[16,6,448]{2,1,0:T(8,128)(2,1)} %reshape.325), calls=%async_computation.4 | async-start | bytes 262144 | tf_op jit(solution)/shard_map/all_to_all | solution.py:151
Sparse Core Ops, SparseCore 0:
  71.8 92.8 reduce-scatter.2
  225.3 122.4 all-reduce.2
  350.8 25.1 reduce-scatter.4
where the time goes:
time: 404 us; the launch traced here: 403 us
  waiting for transfers between devices  250 us (62%)
  blocking collectives  113 us (28%)
  between operations  14.1 us (3%)
  matrix products  9.13 us (2%)
  starting transfers between devices  8.08 us (2%)
  other arithmetic  4.83 us (1%)
    psum x1, waiting for transfers between devices, body(): lax.psum(partial_gate.astype(jnp.bfloat16), 'dev').astype(jnp.float32)  123 us
    reduce_scatter x1, waiting for transfers between devices, body(): lax.psum_scatter(jnp.dot(natural, w_out, preferred_element_type=jnp.float...  92.9 us
    all_gather x1, blocking collectives, body(): gathered = lax.all_gather(values, 'dev', axis=0, tiled=True)  32.9 us
    psum x1, blocking collectives, body(): square_total, logit_total = lax.psum((square_sum, router_part), 'dev')  28.1 us
    reduce_scatter x1, waiting for transfers between devices, body(): lax.psum_scatter(down_part.reshape(sections, padded_rows // sections, wid...  25.5 us
    all_to_all x1, blocking collectives, body(): lax.all_to_all(buffer, 'grp', split_axis=0, concat_axis=1, tiled=True)  14.3 us
    all_gather x1, blocking collectives, body(): received = lax.all_gather(received, 'sec', axis=1, tiled=True)  13.1 us
    all_to_all x1, blocking collectives, body(): lax.all_to_all(outgoing_heads, 'grp', split_axis=1, concat_axis=0, tiled=...  12.8 us
  transfers between devices with their start and end apart: 4, of which 4 were waited for; matrix products, arithmetic and copies ran while one was open for 0% of the time, Pallas kernels for 0%

commit v1 on v0

v1 whole, which is shorter than its diff:
```python
import jax
import jax.numpy as jnp
from jax import lax
from jax.sharding import PartitionSpec as P

score_scale = 0.07216878364870323
route_scale = 2.5
norm_eps = 1e-06
masked_floor = -1e30
f32 = jnp.float32
bf16 = jnp.bfloat16


def split_2(value):
    high = value.astype(bf16)
    low = (value - high.astype(f32)).astype(bf16)
    return high, low


def spread(value, axis):
    copies = jnp.broadcast_to(value[None], (lax.axis_size(axis),) + value.shape)
    return lax.all_to_all(copies, axis, split_axis=0, concat_axis=0, tiled=True)


def body(
    q_latent,
    q_rope,
    cache_latent,
    cache_rope,
    lengths,
    w_uv,
    w_out,
    resid,
    norm_gain,
    router,
    routes,
    slots,
    w_gateup,
    w_down,
):
    sections = lax.axis_size("sec")
    groups = lax.axis_size("grp")
    members = lax.axis_size("dev")
    section = lax.axis_index("sec")
    _, head_total, latent = q_latent.shape
    hist_local = cache_latent.shape[1]
    rope_width = cache_rope.shape[1]
    half_heads = head_total // sections
    head_block, _, value_width = w_uv.shape
    block_rows, width_local = resid.shape
    choices = routes.shape[1]
    expert_total = router.shape[1]
    capacity = max(2, 3 * block_rows // 4)
    pair_rows = sections * block_rows

    query = q_latent[0]
    rope_query = q_rope.reshape(head_total, rope_width)
    scores = (
        jnp.einsum("hc,pc->hp", query, cache_latent[0], preferred_element_type=f32)
        + jnp.einsum("hj,jp->hp", rope_query, cache_rope[0], preferred_element_type=f32)
    ) * score_scale
    positions = section * hist_local + jnp.arange(hist_local, dtype=jnp.int32)
    usable = (positions < lengths[0])[None, :]
    masked = jnp.where(usable, scores, masked_floor)
    top = jnp.max(masked, axis=-1, keepdims=True).astype(bf16)
    expon = jnp.where(usable, jnp.exp(masked - top.astype(f32)), 0.0)
    mass = jnp.sum(expon, axis=-1, keepdims=True)
    weighted = jnp.dot(expon.astype(bf16), cache_latent[0], preferred_element_type=f32)

    mass_high, mass_low = split_2(mass)
    route_part = jnp.concatenate([routes, slots], axis=1).astype(bf16)
    route_part = jnp.pad(route_part, ((0, half_heads - block_rows), (0, 0)))

    def half(value, which):
        return lax.dynamic_slice_in_dim(value, which * half_heads, half_heads, 0)

    other = 1 - section
    spare = 128 - 3 - 2 * choices
    outgoing = jnp.concatenate(
        [
            half(weighted, other).astype(bf16),
            half(top, other),
            half(mass_high, other),
            half(mass_low, other),
            route_part,
            jnp.zeros((half_heads, spare), bf16),
        ],
        axis=1,
    )
    both = lax.all_gather(outgoing, "sec", axis=0)
    theirs = lax.dynamic_index_in_dim(both, other, 0, False)
    top_mine = half(top, section).astype(f32)
    top_theirs = theirs[:, latent : latent + 1].astype(f32)
    mass_theirs = (
        theirs[:, latent + 1 : latent + 2].astype(f32)
        + theirs[:, latent + 2 : latent + 3].astype(f32)
    )
    top_both = jnp.maximum(top_mine, top_theirs)
    factor_mine = jnp.exp(top_mine - top_both)
    factor_theirs = jnp.exp(top_theirs - top_both)
    mass_both = half(mass, section) * factor_mine + mass_theirs * factor_theirs
    latent_out = (
        half(weighted, section) * factor_mine + theirs[:, :latent].astype(f32) * factor_theirs
    ) / mass_both
    latent_out = latent_out.astype(bf16)
    pair_table = both[:, :block_rows, latent + 3 : latent + 3 + 2 * choices]
    pair_table = pair_table.reshape(pair_rows, 2 * choices).astype(jnp.int32)
    pair_routes, pair_slots = pair_table[:, :choices], pair_table[:, choices:]

    outgoing_heads = latent_out.reshape(groups, head_block, latent)
    arrived = lax.all_to_all(outgoing_heads, "grp", split_axis=0, concat_axis=0, tiled=True)
    values = jnp.einsum("nhc,hcv->nhv", arrived, w_uv, preferred_element_type=f32).astype(bf16)
    width_heads = head_block * value_width
    gathered = spread(values.reshape(groups, width_heads), "dev")
    rows_by_block = gathered.transpose(1, 0, 2).reshape(sections, groups, block_rows, width_heads)
    rows_by_block = rows_by_block.transpose(1, 0, 2, 3).reshape(-1, width_heads)
    partial = jnp.dot(rows_by_block, w_out, preferred_element_type=f32).astype(bf16)
    partial = partial.reshape(groups, pair_rows, width_local)
    partial = lax.all_to_all(partial, "grp", split_axis=0, concat_axis=0, tiled=True)
    summed = jnp.sum(partial.astype(f32), axis=0).reshape(sections, block_rows, width_local)
    is_mine = (jnp.arange(sections) == section)[:, None, None]
    summed = summed + jnp.where(is_mine, resid.astype(f32)[None], 0.0)
    hidden = jnp.sum(lax.all_gather(summed, "sec", axis=0), axis=0)
    hidden_mine = lax.dynamic_index_in_dim(hidden, section, 0, False)
    hidden = hidden.reshape(pair_rows, width_local)

    gained = hidden * norm_gain
    square_high, square_low = split_2(jnp.sum(hidden * hidden, axis=-1, keepdims=True))
    logit_high, logit_low = split_2(jnp.dot(gained, router, precision=lax.Precision.HIGHEST))
    expert_ids = jnp.arange(expert_total, dtype=jnp.int32)
    named = jnp.any(pair_routes[:, :, None] == expert_ids[None, None, :], axis=1)
    extra = 3 * expert_total + 2
    tail = -(width_local + extra) % 128
    content = jnp.concatenate(
        [
            gained.astype(bf16),
            logit_high,
            logit_low,
            named.astype(bf16),
            square_high,
            square_low,
            jnp.zeros((pair_rows, tail), bf16),
        ],
        axis=1,
    )
    pair_slot_count = sections * capacity
    block_of_row = jnp.arange(pair_rows, dtype=jnp.int32)[:, None] // block_rows
    kept = pair_slots < capacity
    slot_index = pair_routes * pair_slot_count + block_of_row * capacity + pair_slots
    slot_index = jnp.where(kept, slot_index, -1)
    slot_ids = jnp.arange(expert_total * pair_slot_count, dtype=jnp.int32)
    placement = jnp.any(slot_index[:, :, None] == slot_ids[None, None, :], axis=1).astype(bf16)
    buffer = jnp.einsum("be,bd->ed", placement, content, preferred_element_type=f32).astype(bf16)
    buffer = buffer.reshape(expert_total, pair_slot_count, content.shape[1])
    received = lax.all_to_all(buffer, "grp", split_axis=0, concat_axis=0, tiled=True)
    received = received.reshape(groups * pair_slot_count, content.shape[1])

    own_slots = received.shape[0] // members
    unit = w_gateup.shape[3]
    gate_up = jnp.dot(
        received[:, :width_local],
        w_gateup[0].reshape(width_local, 2 * unit),
        preferred_element_type=f32,
    ).astype(bf16)
    sums_out = jnp.concatenate(
        [gate_up, received[:, width_local : width_local + extra], jnp.zeros((received.shape[0], 128 - extra), bf16)],
        axis=1,
    ).reshape(members, own_slots, 2 * unit + 128)
    sums_in = lax.all_to_all(sums_out, "dev", split_axis=0, concat_axis=0, tiled=True)
    total = jnp.sum(sums_in.astype(f32), axis=0)
    side = total[:, 2 * unit :]
    logits = side[:, :expert_total] + side[:, expert_total : 2 * expert_total]
    chosen = side[:, 2 * expert_total : 3 * expert_total] > 0.5
    squares = side[:, 3 * expert_total : 3 * expert_total + 1] + side[:, 3 * expert_total + 1 : 3 * expert_total + 2]
    inverse_rms = lax.rsqrt(squares / (width_local * members) + norm_eps)
    sigmoid_scores = jax.nn.sigmoid(logits * inverse_rms)
    own_expert = (expert_ids == lax.axis_index("grp"))[None, :]
    picked = jnp.sum(jnp.where(own_expert, sigmoid_scores, 0.0), axis=-1, keepdims=True)
    denominator = jnp.sum(jnp.where(chosen, sigmoid_scores, 0.0), axis=-1, keepdims=True)
    occupied = jnp.any(chosen, axis=-1, keepdims=True)
    route_weight = jnp.where(occupied, route_scale * picked / jnp.where(occupied, denominator, 1.0), 0.0)
    gate = total[:, :unit] * inverse_rms
    up = total[:, unit : 2 * unit] * inverse_rms
    activated = (jax.nn.silu(gate) * up * route_weight).astype(bf16)

    everyone = spread(activated, "dev").reshape(members * own_slots, unit)
    down = jnp.dot(everyone, w_down[0], preferred_element_type=f32).astype(bf16)
    down = down.reshape(groups, pair_slot_count, width_local)
    returned = lax.all_to_all(down, "grp", split_axis=0, concat_axis=0, tiled=True)
    returned = returned.reshape(expert_total * pair_slot_count, width_local)
    mixture = jnp.dot(placement, returned, preferred_element_type=f32)
    mixture = mixture.reshape(sections, block_rows, width_local)
    both_halves = lax.all_gather(
        lax.dynamic_index_in_dim(mixture, other, 0, False), "sec", axis=0
    )
    from_other = lax.dynamic_index_in_dim(both_halves, other, 0, False)
    mine = lax.dynamic_index_in_dim(mixture, section, 0, False)
    return (hidden_mine + mine + from_other).astype(bf16)


def solution(mesh):
    in_specs = (
        P(("grp", "dev"), None, None),
        P(("grp", "dev"), None),
        P(("grp", "dev"), "sec", None),
        P(("grp", "dev"), None, "sec"),
        P(("grp", "dev")),
        P(("sec", "grp"), None, None),
        P(("sec", "grp"), "dev"),
        P(("sec", "grp"), "dev"),
        P("dev"),
        P("dev", None),
        P(("sec", "grp"), None),
        P(("sec", "grp"), None),
        P("grp", "dev", None, "sec"),
        P("grp", "sec", "dev"),
    )
    out_specs = P(("sec", "grp"), "dev")
    return jax.shard_map(body, mesh=mesh, in_specs=in_specs, out_specs=out_specs, check_vma=False)
```

time: 404 us -> 165 us (0.41)
  waiting for transfers between devices: 250 us -> 63.3 us
  blocking collectives: 113 us -> 52.4 us
  starting transfers between devices: 8.08 us -> 28.5 us
  between operations: 14.1 us -> 1.13 us
  local copies, waits for them, and re-layouts: 3.1 us -> 9.58 us
    psum x1 -> x0, waiting for transfers between devices: 123 us -> none  [body(): lax.psum(partial_gate.astype(jnp.bfloat16), 'dev').astype(jnp.float32)]
    reduce_scatter x2 -> x0, waiting for transfers between devices: 118 us -> none  [the longest x1 92.9 us: body(): lax.psum_scatter(jnp.dot(natural, w_out, preferred_element_type=jnp.float...]
    all_to_all x1 -> x5, waiting for transfers between devices: 9.22 us -> 63.3 us  [the longest x1 26.9 us: body(): lax.all_to_all(sums_out, 'dev', split_axis=0, concat_axis=0, tiled=True)]
    all_gather x5 -> x3, blocking collectives: 58.2 us -> 21.3 us  [the longest x1 8.45 us: body(): both = lax.all_gather(outgoing, 'sec', axis=0)]
    psum x1 -> x0, blocking collectives: 28.1 us -> none  [body(): square_total, logit_total = lax.psum((square_sum, router_part), 'dev')]
    all_to_all x1 -> x5, starting transfers between devices: 7.99 us -> 28.5 us  [the longest x1 10.4 us: spread(): return lax.all_to_all(copies, axis, split_axis=0, concat_axis=0, tiled=True)]
    all_to_all x2, blocking collectives: 27.1 us -> 31.1 us  [the longest x1 18.4 us: spread(): return lax.all_to_all(copies, axis, split_axis=0, concat_axis=0, tiled=True)]
    dot_general x9 -> x10, matrix products: 9.13 us -> 5.87 us  [the longest x1 1.47 us: body(): jnp.einsum('hc,pc->hp', query, cache_latent[0], preferred_element_type=f32)]
  transfers between devices with their start and end apart: 4 -> 5, of which waited for: 4 -> 5; matrix products, arithmetic and copies ran while one was open for 0% -> 1% of each run, Pallas kernels for 0% -> 0%
where the time goes in v1:
time: 165 us; the launch traced here: 164 us
  waiting for transfers between devices  63.3 us (38%)
  blocking collectives  52.4 us (32%)
  starting transfers between devices  28.5 us (17%)
  local copies, waits for them, and re-layouts  9.58 us (6%)
  matrix products  5.87 us (4%)
  other arithmetic  3.39 us (2%)
    all_to_all x1, waiting for transfers between devices, body(): lax.all_to_all(sums_out, 'dev', split_axis=0, concat_axis=0, tiled=True)  26.9 us
    all_to_all x1, blocking collectives, spread(): return lax.all_to_all(copies, axis, split_axis=0, concat_axis=0, tiled=True)  18.4 us
    all_to_all x1, blocking collectives, body(): lax.all_to_all(outgoing_heads, 'grp', split_axis=0, concat_axis=0, tiled=...  12.7 us
    all_to_all x1, starting transfers between devices, spread(): return lax.all_to_all(copies, axis, split_axis=0, concat_axis=0, tiled=True)  10.4 us
    all_to_all x1, waiting for transfers between devices, body(): lax.all_to_all(partial, 'grp', split_axis=0, concat_axis=0, tiled=True)  10.2 us
    all_to_all x1, waiting for transfers between devices, body(): lax.all_to_all(down, 'grp', split_axis=0, concat_axis=0, tiled=True)  9.94 us
    all_to_all x1, waiting for transfers between devices, body(): lax.all_to_all(buffer, 'grp', split_axis=0, concat_axis=0, tiled=True)  8.69 us
    all_gather x1, blocking collectives, body(): both = lax.all_gather(outgoing, 'sec', axis=0)  8.45 us
  transfers between devices with their start and end apart: 5, of which 5 were waited for; matrix products, arithmetic and copies ran while one was open for 1% of the time, Pallas kernels for 0%

profile of v1, /device:TPU:1, one launch (start us, length us, event | category | flops | bytes accessed | tf_op | source)
XLA Modules:
  0.0 164.1 jit_solution(2002551671927479829)
XLA Ops:
  0.7 0.8 reduce.1
  1.7 1.1 fusion.14
  2.8 1.5 fusion.54
  4.3 0.2 fusion.7
  4.6 0.4 fusion.3
  5.1 0.1 copy.92
  5.2 0.1 copy.93
  5.4 0.1 copy.91
  5.6 0.1 concatenate.14
  5.7 8.4 %all-gather = bf16[128,640]{1,0:T(8,128)(2,1)S(1)} all-gather(bf16[64,640]{1,0:T(8,128)(2,1)S(1)} %concatenate.14), channel_id=2, replica_groups=mesh['sec'=2,'grp'=16,'dev'=16] {'sec'}, dimensions={0}, use_global_device_ids=true | all-gather | bytes 245760 | tf_op jit(solution)/shard_map/all_gather | solution.py:90
  14.2 0.2 copy.104
  14.4 0.1 copy.103
  14.8 12.7 %all_to_all.35 = bf16[16,4,512]{2,1,0:T(4,128)(2,1)S(1)} all-to-all(bf16[16,4,512]{2,1,0:T(4,128)(2,1)S(1)} %reshape.211), channel_id=1, replica_groups=mesh['sec'=2,'grp'=16,'dev'=16] {'grp'}, dimensions={0} | all-to-all | bytes 131072 | tf_op jit(solution)/shard_map/all_to_all | solution.py:111
  27.5 0.2 fusion.2
  27.7 0.7 broadcast_in_dim.106
  28.5 10.4 %all-to-all-start.1 = ((bf16[16,16,512]{2,1,0:T(8,128)(2,1)}), bf16[16,16,512]{2,1,0:T(8,128)(2,1)S(1)}, u32[]{:S(2)}, u32[]{:S(2)}) async-start(bf16[16,16,512]{2,1,0:T(8,128)(2,1)} %broadcast_in_dim.106), calls=%async_computation.1 | async-start | bytes 524288 | tf_op jit(solution)/shard_map/all_to_all | solution.py:22
  38.9 7.6 %all-to-all-done.1 = bf16[16,16,512]{2,1,0:T(8,128)(2,1)S(1)} async-done(((bf16[16,16,512]{2,1,0:T(8,128)(2,1)}), bf16[16,16,512]{2,1,0:T(8,128)(2,1)S(1)}, u32[]{:S(2)}, u32[]{:S(2)}) %all-to-all-start.1) | async-done | bytes 262176 | tf_op jit(solution)/shard_map/all_to_all | solution.py:22
  46.5 0.1 copy.98
  46.7 0.3 convolution_convert_fusion.1
  47.0 0.8 copy.100
  47.9 3.5 %all-to-all-start.2 = ((bf16[16,16,448]{2,1,0:T(8,128)(2,1)}), bf16[16,16,448]{2,1,0:T(8,128)(2,1)S(1)}, u32[]{:S(2)}, u32[]{:S(2)}) async-start(bf16[16,16,448]{2,1,0:T(8,128)(2,1)} %bitcast.19), calls=%async_computation.2 | async-start | bytes 524288 | tf_op jit(solution)/shard_map/all_to_all | solution.py:119
  51.6 0.1 fusion.17
  51.7 10.2 %all-to-all-done.2 = bf16[16,16,448]{2,1,0:T(8,128)(2,1)S(1)} async-done(((bf16[16,16,448]{2,1,0:T(8,128)(2,1)}), bf16[16,16,448]{2,1,0:T(8,128)(2,1)S(1)}, u32[]{:S(2)}, u32[]{:S(2)}) %all-to-all-start.2) | async-done | bytes 229408 | tf_op jit(solution)/shard_map/all_to_all | solution.py:119
  62.1 6.1 %all_gather.16 = f32[2,2,8,448]{3,2,1,0:T(8,128)S(1)} all-gather(f32[1,2,8,448]{3,2,1,0:T(8,128)S(1)} %bitcast_add_fusion), channel_id=1, replica_groups=mesh['sec'=2,'grp'=16,'dev'=16] {'sec'}, dimensions={0}, use_global_device_ids=true | all-gather | bytes 86016 | tf_op jit(solution)/shard_map/all_gather | solution.py:123
  68.2 0.1 subtract_convert_fusion
  68.8 0.3 convolution_convert_fusion.2
  69.1 0.7 reshape.217
  69.8 3.5 %all-to-all-start.3 = ((bf16[16,12,512]{2,1,0:T(8,128)(2,1)}), bf16[16,12,512]{2,1,0:T(8,128)(2,1)S(1)}, u32[]{:S(2)}, u32[]{:S(2)}) async-start(bf16[16,12,512]{2,1,0:T(8,128)(2,1)} %reshape.217), calls=%async_computation.3 | async-start | bytes 524288 | tf_op jit(solution)/shard_map/all_to_all | solution.py:155
  73.3 2.0 %copy.106 = bf16[56,8,2,1024]{3,1,2,0:T(8,128)(2,1)S(1)} copy(bf16[56,8,2,1024]{3,2,1,0:T(2,128)(2,1)} %bitcast.93) | data formatting | bytes 3670016
  75.4 8.7 %all-to-all-done.3 = bf16[16,12,512]{2,1,0:T(8,128)(2,1)S(1)} async-done(((bf16[16,12,512]{2,1,0:T(8,128)(2,1)}), bf16[16,12,512]{2,1,0:T(8,128)(2,1)S(1)}, u32[]{:S(2)}, u32[]{:S(2)}) %all-to-all-start.3) | async-done | bytes 196640 | tf_op jit(solution)/shard_map/all_to_all | solution.py:155
  84.2 1.5 convolution_convert_fusion
  85.6 1.2 concatenate.16
  86.9 1.2 reshape.219
  88.1 6.4 %all-to-all-start.4 = ((bf16[16,12,2176]{2,1,0:T(8,128)(2,1)}), bf16[16,12,2176]{2,1,0:T(8,128)(2,1)S(1)}, u32[]{:S(2)}, u32[]{:S(2)}) async-start(bf16[16,12,2176]{2,1,0:T(8,128)(2,1)} %reshape.219), calls=%async_computation.4 | async-start | bytes 2228224 | tf_op jit(solution)/shard_map/all_to_all | solution.py:169
  94.5 26.9 %all-to-all-done.4 = bf16[16,12,2176]{2,1,0:T(8,128)(2,1)S(1)} async-done(((bf16[16,12,2176]{2,1,0:T(8,128)(2,1)}), bf16[16,12,2176]{2,1,0:T(8,128)(2,1)S(1)}, u32[]{:S(2)}, u32[]{:S(2)}) %all-to-all-start.4) | async-done | bytes 835616 | tf_op jit(solution)/shard_map/all_to_all | solution.py:169
  121.3 0.2 convert_reduce_fusion
  121.5 0.2 fusion.40
  121.7 0.2 select_reduce_fusion.1
  121.9 0.1 reduce_or.29
  122.1 0.1 fusion.20
  122.2 18.4 %all_to_all.36 = bf16[16,12,1024]{2,1,0:T(8,128)(2,1)S(1)} all-to-all(bf16[16,12,1024]{2,1,0:T(8,128)(2,1)S(1)} %broadcast_in_dim.117), channel_id=1, replica_groups=mesh['sec'=2,'grp'=16,'dev'=16] {'dev'}, dimensions={0} | all-to-all | bytes 786432 | tf_op jit(solution)/shard_map/all_to_all | solution.py:22
  140.7 0.4 convolution_convert_fusion.3
  141.1 0.8 reshape.221
  141.9 4.7 %all-to-all-start.6 = ((bf16[16,12,448]{2,1,0:T(8,128)(2,1)}), bf16[16,12,448]{2,1,0:T(8,128)(2,1)S(1)}, u32[]{:S(2)}, u32[]{:S(2)}) async-start(bf16[16,12,448]{2,1,0:T(8,128)(2,1)} %reshape.221), calls=%async_computation.6 | async-start | bytes 524288 | tf_op jit(solution)/shard_map/all_to_all | solution.py:189
  146.6 9.9 %all-to-all-done.6 = bf16[16,12,448]{2,1,0:T(8,128)(2,1)S(1)} async-done(((bf16[16,12,448]{2,1,0:T(8,128)(2,1)}), bf16[16,12,448]{2,1,0:T(8,128)(2,1)S(1)}, u32[]{:S(2)}, u32[]{:S(2)}) %all-to-all-start.6) | async-done | bytes 172064 | tf_op jit(solution)/shard_map/all_to_all | solution.py:189
  156.6 0.1 fusion.29
  156.7 6.8 %all_gather.17 = f32[2,8,448]{2,1,0:T(8,128)S(1)} all-gather(f32[1,8,448]{2,1,0:T(8,128)S(1)} %constant_dynamic-slice_fusion), channel_id=1, replica_groups=mesh['sec'=2,'grp'=16,'dev'=16] {'sec'}, dimensions={0}, use_global_device_ids=true | all-gather | bytes 43008 | tf_op jit(solution)/shard_map/all_gather | solution.py:193
  163.5 0.6 fusion.31
  (65 shorter events, 2.0 us)
Async XLA Ops:
  0.0 2.8 %copy-start = (bf16[1,1024,512]{2,1,0:T(8,128)(2,1)S(1)}, bf16[1,1024,512]{2,1,0:T(8,128)(2,1)}, u32[]{:S(2)}) copy-start(bf16[1,1024,512]{2,1,0:T(8,128)(2,1)} %param.16) | copy-start | bytes 3145732
  4.3 1.2 copy-start.7
  4.3 1.2 copy-start.8
  4.9 22.6 %copy-start.2 = (bf16[4,512,128]{2,1,0:T(8,128)(2,1)S(1)}, bf16[4,512,128]{2,1,0:T(8,128)(2,1)}, u32[]{:S(2)}) copy-start(bf16[4,512,128]{2,1,0:T(8,128)(2,1)} %param.19) | copy-start | bytes 1572868
  14.6 32.1 %copy-start.3 = (bf16[512,448]{0,1:T(8,128)(2,1)S(1)}, bf16[512,448]{0,1:T(8,128)(2,1)}, u32[]{:S(2)}) copy-start(bf16[512,448]{0,1:T(8,128)(2,1)} %param.20) | copy-start | bytes 1376260
  28.4 23.0 %copy-start.5 = (bf16[8,448]{1,0:T(8,128)(2,1)S(1)}, bf16[8,448]{1,0:T(8,128)(2,1)}, u32[]{:S(2)}) copy-start(bf16[8,448]{1,0:T(8,128)(2,1)} %param.21) | copy-start | bytes 21508
  28.5 18.1 %all-to-all-start.1 = ((bf16[16,16,512]{2,1,0:T(8,128)(2,1)}), bf16[16,16,512]{2,1,0:T(8,128)(2,1)S(1)}, u32[]{:S(2)}, u32[]{:S(2)}) async-start(bf16[16,16,512]{2,1,0:T(8,128)(2,1)} %broadcast_in_dim.106), calls=%async_computation.1 | async-start | bytes 524288 | tf_op jit(solution)/shard_map/all_to_all | solution.py:22
  38.9 29.3 %copy-start.6 = (f32[448]{0:T(512)S(1)}, f32[448]{0:T(512)}, u32[]{:S(2)}) copy-start(f32[448]{0:T(512)} %param.22) | copy-start | bytes 5380
  38.9 29.3 %copy-start.4 = (f32[448,16]{0,1:T(8,128)S(1)}, f32[448,16]{0,1:T(8,128)}, u32[]{:S(2)}) copy-start(f32[448,16]{0,1:T(8,128)} %param.23) | copy-start | bytes 86020
  47.9 14.1 %all-to-all-start.2 = ((bf16[16,16,448]{2,1,0:T(8,128)(2,1)}), bf16[16,16,448]{2,1,0:T(8,128)(2,1)S(1)}, u32[]{:S(2)}, u32[]{:S(2)}) async-start(bf16[16,16,448]{2,1,0:T(8,128)(2,1)} %bitcast.19), calls=%async_computation.2 | async-start | bytes 524288 | tf_op jit(solution)/shard_map/all_to_all | solution.py:119
  69.8 14.2 %all-to-all-start.3 = ((bf16[16,12,512]{2,1,0:T(8,128)(2,1)}), bf16[16,12,512]{2,1,0:T(8,128)(2,1)S(1)}, u32[]{:S(2)}, u32[]{:S(2)}) async-start(bf16[16,12,512]{2,1,0:T(8,128)(2,1)} %reshape.217), calls=%async_computation.3 | async-start | bytes 524288 | tf_op jit(solution)/shard_map/all_to_all | solution.py:155
  88.1 33.3 %all-to-all-start.4 = ((bf16[16,12,2176]{2,1,0:T(8,128)(2,1)}), bf16[16,12,2176]{2,1,0:T(8,128)(2,1)S(1)}, u32[]{:S(2)}, u32[]{:S(2)}) async-start(bf16[16,12,2176]{2,1,0:T(8,128)(2,1)} %reshape.219), calls=%async_computation.4 | async-start | bytes 2228224 | tf_op jit(solution)/shard_map/all_to_all | solution.py:169
  94.5 46.2 %copy-start.1 = (bf16[1,1024,448]{1,2,0:T(8,128)(2,1)S(1)}, bf16[1,1024,448]{1,2,0:T(8,128)(2,1)}, u32[]{:S(2)}) copy-start(bf16[1,1024,448]{1,2,0:T(8,128)(2,1)} %param.27) | copy-start | bytes 2752516
  141.9 14.6 %all-to-all-start.6 = ((bf16[16,12,448]{2,1,0:T(8,128)(2,1)}), bf16[16,12,448]{2,1,0:T(8,128)(2,1)S(1)}, u32[]{:S(2)}, u32[]{:S(2)}) async-start(bf16[16,12,448]{2,1,0:T(8,128)(2,1)} %reshape.221), calls=%async_computation.6 | async-start | bytes 524288 | tf_op jit(solution)/shard_map/all_to_all | solution.py:189

commit v2 on v1

--- a/solution.py
+++ b/solution.py
@@ -1,6 +1,10 @@
+import functools
+
 import jax
 import jax.numpy as jnp
 from jax import lax
+from jax.experimental import pallas as pl
+from jax.experimental.pallas import tpu as pltpu
 from jax.sharding import PartitionSpec as P
 
 score_scale = 0.07216878364870323
@@ -20,6 +24,129 @@
 def spread(value, axis):
     copies = jnp.broadcast_to(value[None], (lax.axis_size(axis),) + value.shape)
     return lax.all_to_all(copies, axis, split_axis=0, concat_axis=0, tiled=True)
+
+
+def in_vmem(count):
+    return [pl.BlockSpec(memory_space=pltpu.VMEM) for _ in range(count)]
+
+
+def iota(shape, axis):
+    return lax.broadcasted_iota(jnp.int32, shape, axis)
+
+
+def one_hot(condition):
+    return jnp.where(condition, 1.0, 0.0).astype(bf16)
+
+
+def select_rows(selection, rows):
+    return jnp.dot(selection, rows, preferred_element_type=f32).astype(bf16)
+
+
+def dot_nt(left, right):
+    return lax.dot_general(left, right, (((1,), (1,)), ((), ())), preferred_element_type=f32)
+
+
+def project_kernel(gathered_ref, weight_ref, out_ref):
+    members, groups, width = gathered_ref.shape
+    total = members * groups
+    rows = gathered_ref[...].reshape(total, width)
+    target = iota((total, total), 0)
+    source = iota((total, total), 1)
+    wanted = (target >> 3 & 1) * (total // 2) + (target >> 4) * 8 + (target & 7)
+    found = (source & (groups - 1)) * members + (source >> 4)
+    rows = select_rows(one_hot(wanted == found), rows)
+    out = dot_nt(rows, weight_ref[...]).astype(bf16)
+    out_ref[...] = out.reshape(out_ref.shape)
+
+
+def gate_up_kernel(received_ref, weight_ref, out_ref):
+    members, chunk, width = received_ref.shape
+    total = members * chunk
+    rows = received_ref[...].reshape(total, width)
+    shape = (24 * members, total)
+    target = iota(shape, 0)
+    source = iota(shape, 1)
+    base = 24 * (source >> 4)
+    slot = source & 15
+    gate_rows = select_rows(one_hot((target == base + slot) & (slot < 12)), rows)
+    place = base + jnp.where(slot < 8, slot + 16, slot + 4)
+    up_rows = select_rows(one_hot((target == place) & (slot < 12)), rows)
+    left = jnp.concatenate([gate_rows, up_rows], axis=1)
+    sums = jnp.dot(left, weight_ref[...], preferred_element_type=f32)
+    side = received_ref[:, :, width - 128 :].astype(f32)
+    first = iota((8, 128), 1) < 64
+    columns = sums.shape[1] // 128
+    for member in range(members):
+        tiles = [
+            sums[24 * member + 8 * row : 24 * member + 8 * row + 8, 128 * col : 128 * col + 128]
+            for row in range(3)
+            for col in range(columns)
+        ]
+        turned = pltpu.roll(side[member, :8], 64, 1)
+        tiles.append(jnp.where(first, turned, side[member, 8:]))
+        out_ref[member] = jnp.concatenate(tiles, axis=0).astype(bf16)
+
+
+def activate_kernel(model_width, expert_total, sums_ref, expert_ref, out_ref):
+    members, height, _ = sums_ref.shape
+    columns = height // 24
+    total = sums_ref[0].astype(f32)
+    for member in range(1, members):
+        total = total + sums_ref[member].astype(f32)
+
+    def block(row):
+        first = 8 * columns * row
+        return jnp.concatenate(
+            [total[first + 8 * col : first + 8 * col + 8] for col in range(columns)], axis=1
+        )
+
+    side = total[24 * columns :]
+    side = jnp.concatenate([side, pltpu.roll(side, 64, 1)], axis=0)
+    lane = iota(side.shape, 1)
+    logits = side + pltpu.roll(side, 128 - expert_total, 1)
+    named = pltpu.roll(side, 128 - 2 * expert_total, 1)
+    square_lane = 3 * expert_total
+    is_square = (lane == square_lane) | (lane == square_lane + 1)
+    squares = jnp.sum(jnp.where(is_square, side, 0.0), axis=1, keepdims=True)
+    inverse_rms = lax.rsqrt(squares / model_width + norm_eps)
+    scores = 1.0 / (1.0 + jnp.exp(-jnp.where(lane < expert_total, logits * inverse_rms, 0.0)))
+    chosen = (named > 0.5) & (lane < expert_total)
+    picked = jnp.sum(jnp.where(lane == expert_ref[0], scores, 0.0), axis=1, keepdims=True)
+    denominator = jnp.sum(jnp.where(chosen, scores, 0.0), axis=1, keepdims=True)
+    occupied = denominator > 0.0
+    weight = route_scale * picked / jnp.where(occupied, denominator, 1.0)
+    weight = jnp.where(occupied, weight, 0.0)
+
+    def activation(gate, up, scale, share):
+        gate = gate * scale
+        return gate / (1.0 + jnp.exp(-gate)) * (up * scale) * share
+
+    early = activation(block(0), block(2), inverse_rms[:8], weight[:8])
+    mixed = block(1)
+    late = activation(mixed, pltpu.roll(mixed, 4, 0), inverse_rms[8:], weight[8:])
+    half = early.shape[1] // 2
+    last = jnp.where(
+        iota((8, half), 0) < 4, late[:, :half], pltpu.roll(late[:, half:], 4, 0)
+    )
+    packed = jnp.concatenate([early[:, :half], early[:, half:], last], axis=0).astype(bf16)
+    for member in range(out_ref.shape[0]):
+        out_ref[member] = packed
+
+
+def down_kernel(packed_ref, weight_ref, out_ref):
+    members, height, half = packed_ref.shape
+    rows = packed_ref[...].reshape(members * height, half)
+    shape = (16 * members, members * height)
+    target = iota(shape, 0)
+    source = iota(shape, 1)
+    base = 24 * (target >> 4)
+    slot = target & 15
+    low_place = base + jnp.where(slot < 8, slot, slot + 8)
+    high_place = base + jnp.where(slot < 8, slot + 8, slot + 12)
+    low = select_rows(one_hot((source == low_place) & (slot < 12)), rows)
+    high = select_rows(one_hot((source == high_place) & (slot < 12)), rows)
+    out = dot_nt(jnp.concatenate([low, high], axis=1), weight_ref[...]).astype(bf16)
+    out_ref[...] = out.reshape(out_ref.shape)
 
 
 def body(
@@ -52,6 +179,7 @@
     expert_total = router.shape[1]
     capacity = max(2, 3 * block_rows // 4)
     pair_rows = sections * block_rows
+    vmem = pltpu.CompilerParams(vmem_limit_bytes=32 * 2**20)
 
     query = q_latent[0]
     rope_query = q_rope.reshape(head_total, rope_width)
@@ -112,10 +240,13 @@
     values = jnp.einsum("nhc,hcv->nhv", arrived, w_uv, preferred_element_type=f32).astype(bf16)
     width_heads = head_block * value_width
     gathered = spread(values.reshape(groups, width_heads), "dev")
-    rows_by_block = gathered.transpose(1, 0, 2).reshape(sections, groups, block_rows, width_heads)
-    rows_by_block = rows_by_block.transpose(1, 0, 2, 3).reshape(-1, width_heads)
-    partial = jnp.dot(rows_by_block, w_out, preferred_element_type=f32).astype(bf16)
-    partial = partial.reshape(groups, pair_rows, width_local)
+    partial = pl.pallas_call(
+        project_kernel,
+        out_shape=jax.ShapeDtypeStruct((groups, pair_rows, width_local), bf16),
+        in_specs=in_vmem(2),
+        out_specs=in_vmem(1)[0],
+        compiler_params=vmem,
+    )(gathered, w_out.T)
     partial = lax.all_to_all(partial, "grp", split_axis=0, concat_axis=0, tiled=True)
     summed = jnp.sum(partial.astype(f32), axis=0).reshape(sections, block_rows, width_local)
     is_mine = (jnp.arange(sections) == section)[:, None, None]
@@ -143,51 +274,47 @@
         ],
         axis=1,
     )
-    pair_slot_count = sections * capacity
+    chunk = 16
     block_of_row = jnp.arange(pair_rows, dtype=jnp.int32)[:, None] // block_rows
     kept = pair_slots < capacity
-    slot_index = pair_routes * pair_slot_count + block_of_row * capacity + pair_slots
+    slot_index = pair_routes * chunk + block_of_row * capacity + pair_slots
     slot_index = jnp.where(kept, slot_index, -1)
-    slot_ids = jnp.arange(expert_total * pair_slot_count, dtype=jnp.int32)
+    slot_ids = jnp.arange(expert_total * chunk, dtype=jnp.int32)
     placement = jnp.any(slot_index[:, :, None] == slot_ids[None, None, :], axis=1).astype(bf16)
     buffer = jnp.einsum("be,bd->ed", placement, content, preferred_element_type=f32).astype(bf16)
-    buffer = buffer.reshape(expert_total, pair_slot_count, content.shape[1])
+    buffer = buffer.reshape(expert_total, chunk, content.shape[1])
     received = lax.all_to_all(buffer, "grp", split_axis=0, concat_axis=0, tiled=True)
-    received = received.reshape(groups * pair_slot_count, content.shape[1])
-
-    own_slots = received.shape[0] // members
+
     unit = w_gateup.shape[3]
-    gate_up = jnp.dot(
-        received[:, :width_local],
-        w_gateup[0].reshape(width_local, 2 * unit),
-        preferred_element_type=f32,
-    ).astype(bf16)
-    sums_out = jnp.concatenate(
-        [gate_up, received[:, width_local : width_local + extra], jnp.zeros((received.shape[0], 128 - extra), bf16)],
-        axis=1,
-    ).reshape(members, own_slots, 2 * unit + 128)
-    sums_in = lax.all_to_all(sums_out, "dev", split_axis=0, concat_axis=0, tiled=True)
-    total = jnp.sum(sums_in.astype(f32), axis=0)
-    side = total[:, 2 * unit :]
-    logits = side[:, :expert_total] + side[:, expert_total : 2 * expert_total]
-    chosen = side[:, 2 * expert_total : 3 * expert_total] > 0.5
-    squares = side[:, 3 * expert_total : 3 * expert_total + 1] + side[:, 3 * expert_total + 1 : 3 * expert_total + 2]
-    inverse_rms = lax.rsqrt(squares / (width_local * members) + norm_eps)
-    sigmoid_scores = jax.nn.sigmoid(logits * inverse_rms)
-    own_expert = (expert_ids == lax.axis_index("grp"))[None, :]
-    picked = jnp.sum(jnp.where(own_expert, sigmoid_scores, 0.0), axis=-1, keepdims=True)
-    denominator = jnp.sum(jnp.where(chosen, sigmoid_scores, 0.0), axis=-1, keepdims=True)
-    occupied = jnp.any(chosen, axis=-1, keepdims=True)
-    route_weight = jnp.where(occupied, route_scale * picked / jnp.where(occupied, denominator, 1.0), 0.0)
-    gate = total[:, :unit] * inverse_rms
-    up = total[:, unit : 2 * unit] * inverse_rms
-    activated = (jax.nn.silu(gate) * up * route_weight).astype(bf16)
-
-    everyone = spread(activated, "dev").reshape(members * own_slots, unit)
-    down = jnp.dot(everyone, w_down[0], preferred_element_type=f32).astype(bf16)
-    down = down.reshape(groups, pair_slot_count, width_local)
+    weight = jnp.pad(
+        w_gateup[0].transpose(1, 0, 2), ((0, 0), (0, content.shape[1] - width_local), (0, 0))
+    ).reshape(2 * content.shape[1], unit)
+    sums = pl.pallas_call(
+        gate_up_kernel,
+        out_shape=jax.ShapeDtypeStruct((members, 24 * unit // 128 + 8, 128), bf16),
+        in_specs=in_vmem(2),
+        out_specs=in_vmem(1)[0],
+        compiler_params=vmem,
+    )(received, weight)
+    sums = lax.all_to_all(sums, "dev", split_axis=0, concat_axis=0, tiled=True)
+    packed = pl.pallas_call(
+        functools.partial(activate_kernel, width_local * members, expert_total),
+        out_shape=jax.ShapeDtypeStruct((members, 24, unit // 2), bf16),
+        in_specs=[in_vmem(1)[0], pl.BlockSpec(memory_space=pltpu.SMEM)],
+        out_specs=in_vmem(1)[0],
+        compiler_params=vmem,
+    )(sums, lax.axis_index("grp").reshape(1))
+
+    everyone = lax.all_to_all(packed, "dev", split_axis=0, concat_axis=0, tiled=True)
+    down = pl.pallas_call(
+        down_kernel,
+        out_shape=jax.ShapeDtypeStruct((groups, chunk, width_local), bf16),
+        in_specs=in_vmem(2),
+        out_specs=in_vmem(1)[0],
+        compiler_params=vmem,
+    )(everyone, w_down[0].T)
     returned = lax.all_to_all(down, "grp", split_axis=0, concat_axis=0, tiled=True)
-    returned = returned.reshape(expert_total * pair_slot_count, width_local)
+    returned = returned.reshape(expert_total * chunk, width_local)
     mixture = jnp.dot(placement, returned, preferred_element_type=f32)
     mixture = mixture.reshape(sections, block_rows, width_local)
     both_halves = lax.all_gather(

time: 165 us -> 153 us (0.927)
  waiting for transfers between devices: 63.3 us -> 56.6 us
  local copies, waits for them, and re-layouts: 9.58 us -> 3.93 us
  Pallas kernels: 0 us -> 4.03 us
    all_to_all x1, waiting for transfers between devices: 26.9 us -> 18.9 us  [body(): sums = lax.all_to_all(sums, 'dev', split_axis=0, concat_axis=0, tiled=True)]
    pallas_call x0 -> x4, Pallas kernels: none -> 4.03 us  [the longest x1 1.42 us: body(): pl.pallas_call(down_kernel, out_shape=jax.ShapeDtypeStruct((groups, chunk...]
    reshape x6 -> x0, local copies, waits for them, and re-layouts: 2.88 us -> none  [the longest x1 1.17 us: body(): sums_out = jnp.concatenate([gate_up, received[:, width_local:width_local...]
    dot_general x3 -> x0, matrix products: 2.22 us -> none  [the longest x1 1.46 us: body(): jnp.dot(received[:, :width_local], w_gateup[0].reshape(width_local, 2 * u...]
where the time goes in v2:
time: 153 us; the launch traced here: 152 us
  waiting for transfers between devices  56.6 us (37%)
  blocking collectives  52.3 us (34%)
  starting transfers between devices  27.5 us (18%)
  matrix products  4.39 us (3%)
  Pallas kernels  4.03 us (3%)
  local copies, waits for them, and re-layouts  3.93 us (3%)
  other arithmetic  2.58 us (2%)
    all_to_all x1, waiting for transfers between devices, body(): sums = lax.all_to_all(sums, 'dev', split_axis=0, concat_axis=0, tiled=True)  18.9 us
    all_to_all x1, blocking collectives, body(): lax.all_to_all(packed, 'dev', split_axis=0, concat_axis=0, tiled=True)  17.5 us
    all_to_all x1, blocking collectives, body(): lax.all_to_all(outgoing_heads, 'grp', split_axis=0, concat_axis=0, tiled=...  12.7 us
    all_to_all x1, starting transfers between devices, spread(): return lax.all_to_all(copies, axis, split_axis=0, concat_axis=0, tiled=True)  10.3 us
    all_to_all x1, waiting for transfers between devices, body(): lax.all_to_all(partial, 'grp', split_axis=0, concat_axis=0, tiled=True)  10.2 us
    all_to_all x1, waiting for transfers between devices, body(): lax.all_to_all(buffer, 'grp', split_axis=0, concat_axis=0, tiled=True)  9.99 us
    all_to_all x1, waiting for transfers between devices, body(): lax.all_to_all(down, 'grp', split_axis=0, concat_axis=0, tiled=True)  9.97 us
    all_gather x1, blocking collectives, body(): both = lax.all_gather(outgoing, 'sec', axis=0)  8.59 us
  transfers between devices with their start and end apart: 5, of which 5 were waited for; matrix products, arithmetic and copies ran while one was open for 1% of the time, Pallas kernels for 0%

profile of v2, /device:TPU:1, one launch (start us, length us, event | category | flops | bytes accessed | tf_op | source)
XLA Modules:
  0.0 152.4 jit_solution(12123879055909029812)
XLA Ops:
  0.7 0.8 reduce.1
  1.6 0.1 reshape.176
  1.7 1.1 fusion.12
  2.8 1.5 fusion.40
  4.3 0.2 fusion.6
  4.6 0.4 fusion.3
  5.1 0.1 copy.75
  5.3 0.1 copy.77
  5.4 0.1 copy.76
  5.7 0.1 concatenate.11
  5.8 8.6 %all-gather = bf16[128,640]{1,0:T(8,128)(2,1)S(1)} all-gather(bf16[64,640]{1,0:T(8,128)(2,1)S(1)} %concatenate.11), channel_id=2, replica_groups=mesh['sec'=2,'grp'=16,'dev'=16] {'sec'}, dimensions={0}, use_global_device_ids=true | all-gather | bytes 245760 | tf_op jit(solution)/shard_map/all_gather | solution.py:218
  14.4 0.2 copy.89
  14.5 0.1 fusion.35
  14.6 0.1 copy.88
  14.8 0.1 copy.79
  15.0 12.7 %all_to_all.35 = bf16[16,4,512]{2,1,0:T(4,128)(2,1)S(1)} all-to-all(bf16[16,4,512]{2,1,0:T(4,128)(2,1)S(1)} %reshape.177), channel_id=1, replica_groups=mesh['sec'=2,'grp'=16,'dev'=16] {'grp'}, dimensions={0} | all-to-all | bytes 131072 | tf_op jit(solution)/shard_map/all_to_all | solution.py:239
  27.7 0.2 fusion.2
  27.9 0.7 broadcast_in_dim.72
  28.6 10.3 %all-to-all-start.1 = ((bf16[16,16,512]{2,1,0:T(8,128)(2,1)}), bf16[16,16,512]{2,1,0:T(8,128)(2,1)S(1)}, u32[]{:S(2)}, u32[]{:S(2)}) async-start(bf16[16,16,512]{2,1,0:T(8,128)(2,1)} %broadcast_in_dim.72), calls=%async_computation.1 | async-start | bytes 524288 | tf_op jit(solution)/shard_map/all_to_all | solution.py:26
  39.0 7.6 %all-to-all-done.1.gathered_ref = bf16[16,16,512]{2,1,0:T(8,128)(2,1)S(1)} async-done(((bf16[16,16,512]{2,1,0:T(8,128)(2,1)}), bf16[16,16,512]{2,1,0:T(8,128)(2,1)S(1)}, u32[]{:S(2)}, u32[]{:S(2)}) %all-to-all-start.1) | async-done | bytes 262176 | tf_op jit(solution)/shard_map/all_to_all | solution.py:26
  46.6 1.1 shard_map.136
  47.7 3.7 %all-to-all-start.2 = ((bf16[16,16,448]{2,1,0:T(8,128)(2,1)}), bf16[16,16,448]{2,1,0:T(8,128)(2,1)S(1)}, u32[]{:S(2)}, u32[]{:S(2)}) async-start(bf16[16,16,448]{2,1,0:T(8,128)(2,1)} %shard_map.136), calls=%async_computation.2 | async-start | bytes 524288 | tf_op jit(solution)/shard_map/all_to_all | solution.py:250
  51.5 0.1 fusion.17
  51.6 0.1 fusion.15
  51.7 10.2 %all-to-all-done.2 = bf16[16,16,448]{2,1,0:T(8,128)(2,1)S(1)} async-done(((bf16[16,16,448]{2,1,0:T(8,128)(2,1)}), bf16[16,16,448]{2,1,0:T(8,128)(2,1)S(1)}, u32[]{:S(2)}, u32[]{:S(2)}) %all-to-all-start.2) | async-done | bytes 229408 | tf_op jit(solution)/shard_map/all_to_all | solution.py:250
  62.0 6.1 %all_gather.16 = f32[2,2,8,448]{3,2,1,0:T(8,128)S(1)} all-gather(f32[1,2,8,448]{3,2,1,0:T(8,128)S(1)} %bitcast_add_fusion), channel_id=1, replica_groups=mesh['sec'=2,'grp'=16,'dev'=16] {'sec'}, dimensions={0}, use_global_device_ids=true | all-gather | bytes 86016 | tf_op jit(solution)/shard_map/all_gather | solution.py:254
  68.1 0.1 multiply_reduce_fusion
  68.3 0.1 copy.83
  68.4 0.1 copy.82
  68.5 0.1 subtract_convert_fusion
  68.7 0.1 concatenate.12
  68.8 1.0 convolution_convert_fusion
  69.7 3.5 %all-to-all-start.3 = ((bf16[16,16,512]{2,1,0:T(8,128)(2,1)}), bf16[16,16,512]{2,1,0:T(8,128)(2,1)S(1)}, u32[]{:S(2)}, u32[]{:S(2)}) async-start(bf16[16,16,512]{2,1,0:T(8,128)(2,1)} %bitcast.21), calls=%async_computation.3 | async-start | bytes 524288 | tf_op jit(solution)/shard_map/all_to_all | solution.py:286
  73.3 0.5 copy.90
  73.8 0.2 pad.9.clone
  74.0 10.0 %all-to-all-done.3.received_ref = bf16[16,16,512]{2,1,0:T(8,128)(2,1)S(1)} async-done(((bf16[16,16,512]{2,1,0:T(8,128)(2,1)}), bf16[16,16,512]{2,1,0:T(8,128)(2,1)S(1)}, u32[]{:S(2)}, u32[]{:S(2)}) %all-to-all-start.3) | async-done | bytes 262176 | tf_op jit(solution)/shard_map/all_to_all | solution.py:286
  84.0 1.2 shard_map.137
  85.2 0.9 copy-done.1
  86.1 6.5 %all-to-all-start.4 = ((bf16[16,200,128]{2,1,0:T(8,128)(2,1)}), bf16[16,200,128]{2,1,0:T(8,128)(2,1)S(1)}, u32[]{:S(2)}, u32[]{:S(2)}) async-start(bf16[16,200,128]{2,1,0:T(8,128)(2,1)} %copy-done.1), calls=%async_computation.4 | async-start | bytes 1638400 | tf_op jit(solution)/shard_map/all_to_all | solution.py:299
  92.6 18.9 %all-to-all-done.4.sums_ref = bf16[16,200,128]{2,1,0:T(8,128)(2,1)S(1)} async-done(((bf16[16,200,128]{2,1,0:T(8,128)(2,1)}), bf16[16,200,128]{2,1,0:T(8,128)(2,1)S(1)}, u32[]{:S(2)}, u32[]{:S(2)}) %all-to-all-start.4) | async-done | bytes 819232 | tf_op jit(solution)/shard_map/all_to_all | solution.py:299
  111.5 0.3 shard_map.138
  111.8 17.5 %all_to_all.36.packed_ref = bf16[16,24,512]{2,1,0:T(8,128)(2,1)S(1)} all-to-all(bf16[16,24,512]{2,1,0:T(8,128)(2,1)S(1)} %shard_map.138), channel_id=1, replica_groups=mesh['sec'=2,'grp'=16,'dev'=16] {'dev'}, dimensions={0} | all-to-all | bytes 786432 | tf_op jit(solution)/shard_map/all_to_all | solution.py:308
  129.3 1.4 shard_map.139
  130.7 3.6 %all-to-all-start.6 = ((bf16[16,16,448]{2,1,0:T(8,128)(2,1)}), bf16[16,16,448]{2,1,0:T(8,128)(2,1)S(1)}, u32[]{:S(2)}, u32[]{:S(2)}) async-start(bf16[16,16,448]{2,1,0:T(8,128)(2,1)} %shard_map.139), calls=%async_computation.6 | async-start | bytes 524288 | tf_op jit(solution)/shard_map/all_to_all | solution.py:316
  134.3 10.0 %all-to-all-done.6 = bf16[16,16,448]{2,1,0:T(8,128)(2,1)S(1)} async-done(((bf16[16,16,448]{2,1,0:T(8,128)(2,1)}), bf16[16,16,448]{2,1,0:T(8,128)(2,1)S(1)}, u32[]{:S(2)}, u32[]{:S(2)}) %all-to-all-start.6) | async-done | bytes 229408 | tf_op jit(solution)/shard_map/all_to_all | solution.py:316
  144.3 0.1 fusion.24
  144.4 7.4 %all_gather.17 = f32[2,8,448]{2,1,0:T(8,128)S(1)} all-gather(f32[1,8,448]{2,1,0:T(8,128)S(1)} %constant_dynamic-slice_fusion), channel_id=1, replica_groups=mesh['sec'=2,'grp'=16,'dev'=16] {'sec'}, dimensions={0}, use_global_device_ids=true | all-gather | bytes 43008 | tf_op jit(solution)/shard_map/all_gather | solution.py:320
  151.8 0.6 fusion.26
  (51 shorter events, 0.9 us)
Async XLA Ops:
  0.0 2.8 %copy-start = (bf16[1,1024,512]{2,1,0:T(8,128)(2,1)S(1)}, bf16[1,1024,512]{2,1,0:T(8,128)(2,1)}, u32[]{:S(2)}) copy-start(bf16[1,1024,512]{2,1,0:T(8,128)(2,1)} %param.16) | copy-start | bytes 3145732
  2.8 2.2 %copy-start.9 = (s32[8,8]{1,0:T(8,128)S(1)}, s32[8,8]{1,0:T(8,128)}, u32[]{:S(2)}) copy-start(s32[8,8]{1,0:T(8,128)} %param.24) | copy-start | bytes 772
  2.8 2.2 %copy-start.10 = (s32[8,8]{1,0:T(8,128)S(1)}, s32[8,8]{1,0:T(8,128)}, u32[]{:S(2)}) copy-start(s32[8,8]{1,0:T(8,128)} %param.25) | copy-start | bytes 772
  4.9 22.8 %copy-start.5 = (bf16[4,512,128]{2,1,0:T(8,128)(2,1)S(1)}, bf16[4,512,128]{2,1,0:T(8,128)(2,1)}, u32[]{:S(2)}) copy-start(bf16[4,512,128]{2,1,0:T(8,128)(2,1)} %param.19) | copy-start | bytes 1572868
  5.6 40.9 %copy-start.3 = (bf16[512,448]{0,1:T(8,128)(2,1)S(1)}, bf16[512,448]{0,1:T(8,128)(2,1)}, u32[]{:S(2)}) copy-start(bf16[512,448]{0,1:T(8,128)(2,1)} %param.20) | copy-start | bytes 1376260
  14.8 36.6 %copy-start.7 = (bf16[8,448]{1,0:T(8,128)(2,1)S(1)}, bf16[8,448]{1,0:T(8,128)(2,1)}, u32[]{:S(2)}) copy-start(bf16[8,448]{1,0:T(8,128)(2,1)} %param.21) | copy-start | bytes 21508
  27.7 40.8 %copy-start.8 = (f32[448]{0:T(512)S(1)}, f32[448]{0:T(512)}, u32[]{:S(2)}) copy-start(f32[448]{0:T(512)} %param.22) | copy-start | bytes 5380
  27.7 40.8 %copy-start.6 = (f32[448,16]{0,1:T(8,128)S(1)}, f32[448,16]{0,1:T(8,128)}, u32[]{:S(2)}) copy-start(f32[448,16]{0,1:T(8,128)} %param.23) | copy-start | bytes 86020
  28.6 18.0 %all-to-all-start.1 = ((bf16[16,16,512]{2,1,0:T(8,128)(2,1)}), bf16[16,16,512]{2,1,0:T(8,128)(2,1)S(1)}, u32[]{:S(2)}, u32[]{:S(2)}) async-start(bf16[16,16,512]{2,1,0:T(8,128)(2,1)} %broadcast_in_dim.72), calls=%async_computation.1 | async-start | bytes 524288 | tf_op jit(solution)/shard_map/all_to_all | solution.py:26
  47.7 25.6 %copy-start.4 = (bf16[1,448,2,1024]{3,2,1,0:T(2,128)(2,1)S(1)}, bf16[1,448,2,1024]{3,2,1,0:T(2,128)(2,1)}, u32[]{:S(2)}) copy-start(bf16[1,448,2,1024]{3,2,1,0:T(2,128)(2,1)} %param.26) | copy-start | bytes 5505028
  47.7 14.2 %all-to-all-start.2 = ((bf16[16,16,448]{2,1,0:T(8,128)(2,1)}), bf16[16,16,448]{2,1,0:T(8,128)(2,1)S(1)}, u32[]{:S(2)}, u32[]{:S(2)}) async-start(bf16[16,16,448]{2,1,0:T(8,128)(2,1)} %shard_map.136), calls=%async_computation.2 | async-start | bytes 524288 | tf_op jit(solution)/shard_map/all_to_all | solution.py:250
  69.7 14.3 %all-to-all-start.3 = ((bf16[16,16,512]{2,1,0:T(8,128)(2,1)}), bf16[16,16,512]{2,1,0:T(8,128)(2,1)S(1)}, u32[]{:S(2)}, u32[]{:S(2)}) async-start(bf16[16,16,512]{2,1,0:T(8,128)(2,1)} %bitcast.21), calls=%async_computation.3 | async-start | bytes 524288 | tf_op jit(solution)/shard_map/all_to_all | solution.py:286
  85.2 0.9 copy-start.1
  86.1 43.2 %copy-start.2 = (bf16[1,1024,448]{1,2,0:T(8,128)(2,1)S(1)}, bf16[1,1024,448]{1,2,0:T(8,128)(2,1)}, u32[]{:S(2)}) copy-start(bf16[1,1024,448]{1,2,0:T(8,128)(2,1)} %param.27) | copy-start | bytes 2752516
  86.1 25.4 %all-to-all-start.4 = ((bf16[16,200,128]{2,1,0:T(8,128)(2,1)}), bf16[16,200,128]{2,1,0:T(8,128)(2,1)S(1)}, u32[]{:S(2)}, u32[]{:S(2)}) async-start(bf16[16,200,128]{2,1,0:T(8,128)(2,1)} %copy-done.1), calls=%async_computation.4 | async-start | bytes 1638400 | tf_op jit(solution)/shard_map/all_to_all | solution.py:299
  130.7 13.5 %all-to-all-start.6 = ((bf16[16,16,448]{2,1,0:T(8,128)(2,1)}), bf16[16,16,448]{2,1,0:T(8,128)(2,1)S(1)}, u32[]{:S(2)}, u32[]{:S(2)}) async-start(bf16[16,16,448]{2,1,0:T(8,128)(2,1)} %shard_map.139), calls=%async_computation.6 | async-start | bytes 524288 | tf_op jit(solution)/shard_map/all_to_all | solution.py:316

commit v3 on v2

--- a/solution.py
+++ b/solution.py
@@ -15,12 +15,6 @@
 bf16 = jnp.bfloat16
 
 
-def split_2(value):
-    high = value.astype(bf16)
-    low = (value - high.astype(f32)).astype(bf16)
-    return high, low
-
-
 def spread(value, axis):
     copies = jnp.broadcast_to(value[None], (lax.axis_size(axis),) + value.shape)
     return lax.all_to_all(copies, axis, split_axis=0, concat_axis=0, tiled=True)
@@ -44,6 +38,81 @@
 
 def dot_nt(left, right):
     return lax.dot_general(left, right, (((1,), (1,)), ((), ())), preferred_element_type=f32)
+
+
+def attend_kernel(
+    place_ref, latent_ref, rope_ref, cache_ref, cache_rope_ref, routes_ref, slots_ref, sent_ref, kept_ref
+):
+    heads = latent_ref.shape[0]
+    half = heads // 2
+    latent = latent_ref.shape[1]
+    mine = pl.multiple_of(place_ref[0] * half, half)
+    other = pl.multiple_of(half - place_ref[0] * half, half)
+
+    def other_first(ref):
+        return jnp.concatenate([ref[pl.ds(other, half), :], ref[pl.ds(mine, half), :]], axis=0)
+
+    cache = cache_ref[...]
+    scores = dot_nt(other_first(latent_ref), cache) + jnp.dot(
+        other_first(rope_ref), cache_rope_ref[...], preferred_element_type=f32
+    )
+    usable = iota(scores.shape, 1) < place_ref[1]
+    masked = jnp.where(usable, scores * score_scale, masked_floor)
+    top = jnp.max(masked, axis=1, keepdims=True).astype(bf16).astype(f32)
+    expon = jnp.where(usable, jnp.exp(masked - top), 0.0)
+    mass = jnp.sum(expon, axis=1, keepdims=True)
+    weighted = jnp.dot(expon.astype(bf16), cache, preferred_element_type=f32)
+    mass_high = mass.astype(bf16).astype(f32)
+    lane = iota((heads, 128), 1)
+    side = jnp.where(lane == 0, top, 0.0)
+    side = jnp.where(lane == 1, mass_high, side)
+    side = jnp.where(lane == 2, mass - mass_high, side)
+    kept_ref[:, :latent] = weighted[half:]
+    kept_ref[:, latent:] = side[half:]
+    choices = routes_ref.shape[1]
+    spot = iota((choices, 128), 1) - iota((choices, 128), 0)
+    table = jnp.dot(
+        routes_ref[...].astype(f32), jnp.where(spot == 16, 1.0, 0.0), preferred_element_type=f32
+    ) + jnp.dot(
+        slots_ref[...].astype(f32), jnp.where(spot == 16 + choices, 1.0, 0.0), preferred_element_type=f32
+    )
+    block_rows = table.shape[0]
+    side = jnp.concatenate([side[:block_rows] + table, side[block_rows:half]], axis=0)
+    sent_ref[:, :latent] = weighted[:half].astype(bf16)
+    sent_ref[:, latent:] = side.astype(bf16)
+
+
+def dispatch_kernel(
+    expert_total, sums_ref, gain_ref, router_ref, named_ref, placement_ref, buffer_ref, hidden_ref
+):
+    hidden = sums_ref[0] + sums_ref[1]
+    hidden_ref[...] = hidden
+    rows, width = hidden.shape
+    gained = hidden * gain_ref[...]
+    squares = jnp.sum(hidden * hidden, axis=1, keepdims=True)
+    square_high = squares.astype(bf16).astype(f32)
+    logits = lax.dot_general(
+        gained,
+        router_ref[...],
+        (((1,), (1,)), ((), ())),
+        preferred_element_type=f32,
+        precision=lax.Precision.HIGHEST,
+    )
+    spread_out = jnp.concatenate([logits, jnp.zeros((rows, 128 - expert_total), f32)], axis=1)
+    logit_high = spread_out.astype(bf16).astype(f32)
+    lane = iota((rows, 128), 1)
+    first = width % 128
+    side = pltpu.roll(logit_high, first, 1) + pltpu.roll(
+        spread_out - logit_high, first + expert_total, 1
+    )
+    side = side + pltpu.roll(named_ref[...], first + 2 * expert_total, 1)
+    side = jnp.where(lane == first + 3 * expert_total, square_high, side)
+    side = jnp.where(lane == first + 3 * expert_total + 1, squares - square_high, side)
+    full = width - first
+    last = jnp.concatenate([gained[:, full:], jnp.zeros((rows, 128 - first), f32)], axis=1)
+    content = jnp.concatenate([gained[:, :full], jnp.where(lane < first, last, side)], axis=1)
+    out = jnp.dot(placement_ref[...], content.astype(bf16), preferred_element_type=f32)
+    buffer_ref[...] = out.astype(bf16).reshape(buffer_ref.shape)
 
 
 def project_kernel(gathered_ref, weight_ref, out_ref):
@@ -181,43 +250,31 @@
     pair_rows = sections * block_rows
     vmem = pltpu.CompilerParams(vmem_limit_bytes=32 * 2**20)
 
-    query = q_latent[0]
-    rope_query = q_rope.reshape(head_total, rope_width)
-    scores = (
-        jnp.einsum("hc,pc->hp", query, cache_latent[0], preferred_element_type=f32)
-        + jnp.einsum("hj,jp->hp", rope_query, cache_rope[0], preferred_element_type=f32)
-    ) * score_scale
-    positions = section * hist_local + jnp.arange(hist_local, dtype=jnp.int32)
-    usable = (positions < lengths[0])[None, :]
-    masked = jnp.where(usable, scores, masked_floor)
-    top = jnp.max(masked, axis=-1, keepdims=True).astype(bf16)
-    expon = jnp.where(usable, jnp.exp(masked - top.astype(f32)), 0.0)
-    mass = jnp.sum(expon, axis=-1, keepdims=True)
-    weighted = jnp.dot(expon.astype(bf16), cache_latent[0], preferred_element_type=f32)
-
-    mass_high, mass_low = split_2(mass)
-    route_part = jnp.concatenate([routes, slots], axis=1).astype(bf16)
-    route_part = jnp.pad(route_part, ((0, half_heads - block_rows), (0, 0)))
-
-    def half(value, which):
-        return lax.dynamic_slice_in_dim(value, which * half_heads, half_heads, 0)
+    place = jnp.stack([section, lengths[0] - section * hist_local]).astype(jnp.int32)
+    sent, kept_part = pl.pallas_call(
+        attend_kernel,
+        out_shape=(
+            jax.ShapeDtypeStruct((half_heads, latent + 128), bf16),
+            jax.ShapeDtypeStruct((half_heads, latent + 128), f32),
+        ),
+        in_specs=[pl.BlockSpec(memory_space=pltpu.SMEM)] + in_vmem(6),
+        out_specs=tuple(in_vmem(2)),
+        compiler_params=vmem,
+    )(
+        place,
+        q_latent[0],
+        q_rope.reshape(head_total, rope_width),
+        cache_latent[0],
+        cache_rope[0],
+        routes,
+        slots,
+    )
 
     other = 1 - section
-    spare = 128 - 3 - 2 * choices
-    outgoing = jnp.concatenate(
-        [
-            half(weighted, other).astype(bf16),
-            half(top, other),
-            half(mass_high, other),
-            half(mass_low, other),
-            route_part,
-            jnp.zeros((half_heads, spare), bf16),
-        ],
-        axis=1,
-    )
-    both = lax.all_gather(outgoing, "sec", axis=0)
+    both = lax.all_gather(sent, "sec", axis=0)
     theirs = lax.dynamic_index_in_dim(both, other, 0, False)
-    top_mine = half(top, section).astype(f32)
+    top_mine = kept_part[:, latent : latent + 1]
+    mass_mine = kept_part[:, latent + 1 : latent + 2] + kept_part[:, latent + 2 : latent + 3]
     top_theirs = theirs[:, latent : latent + 1].astype(f32)
     mass_theirs = (
         theirs[:, latent + 1 : latent + 2].astype(f32)
@@ -226,12 +283,12 @@
     top_both = jnp.maximum(top_mine, top_theirs)
     factor_mine = jnp.exp(top_mine - top_both)
     factor_theirs = jnp.exp(top_theirs - top_both)
-    mass_both = half(mass, section) * factor_mine + mass_theirs * factor_theirs
+    mass_both = mass_mine * factor_mine + mass_theirs * factor_theirs
     latent_out = (
-        half(weighted, section) * factor_mine + theirs[:, :latent].astype(f32) * factor_theirs
+        kept_part[:, :latent] * factor_mine + theirs[:, :latent].astype(f32) * factor_theirs
     ) / mass_both
     latent_out = latent_out.astype(bf16)
-    pair_table = both[:, :block_rows, latent + 3 : latent + 3 + 2 * choices]
+    pair_table = both[:, :block_rows, latent + 16 : latent + 16 + 2 * choices]
     pair_table = pair_table.reshape(pair_rows, 2 * choices).astype(jnp.int32)
     pair_routes, pair_slots = pair_table[:, :choices], pair_table[:, choices:]
 
@@ -251,29 +308,11 @@
     summed = jnp.sum(partial.astype(f32), axis=0).reshape(sections, block_rows, width_local)
     is_mine = (jnp.arange(sections) == section)[:, None, None]
     summed = summed + jnp.where(is_mine, resid.astype(f32)[None], 0.0)
-    hidden = jnp.sum(lax.all_gather(summed, "sec", axis=0), axis=0)
-    hidden_mine = lax.dynamic_index_in_dim(hidden, section, 0, False)
-    hidden = hidden.reshape(pair_rows, width_local)
-
-    gained = hidden * norm_gain
-    square_high, square_low = split_2(jnp.sum(hidden * hidden, axis=-1, keepdims=True))
-    logit_high, logit_low = split_2(jnp.dot(gained, router, precision=lax.Precision.HIGHEST))
+    summed = lax.all_gather(summed.reshape(pair_rows, width_local), "sec", axis=0)
+
     expert_ids = jnp.arange(expert_total, dtype=jnp.int32)
     named = jnp.any(pair_routes[:, :, None] == expert_ids[None, None, :], axis=1)
-    extra = 3 * expert_total + 2
-    tail = -(width_local + extra) % 128
-    content = jnp.concatenate(
-        [
-            gained.astype(bf16),
-            logit_high,
-            logit_low,
-            named.astype(bf16),
-            square_high,
-            square_low,
-            jnp.zeros((pair_rows, tail), bf16),
-        ],
-        axis=1,
-    )
+    named = jnp.pad(named.astype(f32), ((0, 0), (0, 128 - expert_total)))
     chunk = 16
     block_of_row = jnp.arange(pair_rows, dtype=jnp.int32)[:, None] // block_rows
     kept = pair_slots < capacity
@@ -281,14 +320,23 @@
     slot_index = jnp.where(kept, slot_index, -1)
     slot_ids = jnp.arange(expert_total * chunk, dtype=jnp.int32)
     placement = jnp.any(slot_index[:, :, None] == slot_ids[None, None, :], axis=1).astype(bf16)
-    buffer = jnp.einsum("be,bd->ed", placement, content, preferred_element_type=f32).astype(bf16)
-    buffer = buffer.reshape(expert_total, chunk, content.shape[1])
+    padded_width = width_local + -width_local % 128
+    buffer, hidden = pl.pallas_call(
+        functools.partial(dispatch_kernel, expert_total),
+        out_shape=(
+            jax.ShapeDtypeStruct((expert_total, chunk, padded_width), bf16),
+            jax.ShapeDtypeStruct((pair_rows, width_local), f32),
+        ),
+        in_specs=in_vmem(5),
+        out_specs=tuple(in_vmem(2)),
+        compiler_params=vmem,
+    )(summed, norm_gain[None], router.T, named, placement.T)
     received = lax.all_to_all(buffer, "grp", split_axis=0, concat_axis=0, tiled=True)
 
     unit = w_gateup.shape[3]
     weight = jnp.pad(
-        w_gateup[0].transpose(1, 0, 2), ((0, 0), (0, content.shape[1] - width_local), (0, 0))
-    ).reshape(2 * content.shape[1], unit)
+        w_gateup[0].transpose(1, 0, 2), ((0, 0), (0, padded_width - width_local), (0, 0))
+    ).reshape(2 * padded_width, unit)
     sums = pl.pallas_call(
         gate_up_kernel,
         out_shape=jax.ShapeDtypeStruct((members, 24 * unit // 128 + 8, 128), bf16),
@@ -322,6 +370,7 @@
     )
     from_other = lax.dynamic_index_in_dim(both_halves, other, 0, False)
     mine = lax.dynamic_index_in_dim(mixture, section, 0, False)
+    hidden_mine = lax.dynamic_slice_in_dim(hidden, section * block_rows, block_rows, 0)
     return (hidden_mine + mine + from_other).astype(bf16)
 
 

time: 153 us -> 154 us (level)
  matrix products: 4.39 us -> 0.32 us
  Pallas kernels: 4.03 us -> 7.53 us
  local copies, waits for them, and re-layouts: 3.93 us -> 6.27 us
    dot_general x5 -> x0, matrix products: 4.07 us -> none  [the longest x1 1.48 us: body(): jnp.einsum('hc,pc->hp', query, cache_latent[0], preferred_element_type=f32)]
    unnamed x25, local copies, waits for them, and re-layouts: 1.77 us -> 4.95 us
    pallas_call x0 -> x2, Pallas kernels: none -> 2.59 us  [the longest x1 1.44 us: body(): pl.pallas_call(attend_kernel, out_shape=(jax.ShapeDtypeStruct((half_heads...]
where the time goes in v3:
time: 154 us; the launch traced here: 153 us
  waiting for transfers between devices  56.3 us (37%)
  blocking collectives  52.1 us (34%)
  starting transfers between devices  27.5 us (18%)
  Pallas kernels  7.53 us (5%)
  local copies, waits for them, and re-layouts  6.27 us (4%)
  other arithmetic  2.36 us (2%)
    all_to_all x1, waiting for transfers between devices, body(): sums = lax.all_to_all(sums, 'dev', split_axis=0, concat_axis=0, tiled=True)  18.9 us
    all_to_all x1, blocking collectives, body(): lax.all_to_all(packed, 'dev', split_axis=0, concat_axis=0, tiled=True)  17.5 us
    all_to_all x1, blocking collectives, body(): lax.all_to_all(outgoing_heads, 'grp', split_axis=0, concat_axis=0, tiled=...  12.7 us
    all_to_all x1, starting transfers between devices, spread(): return lax.all_to_all(copies, axis, split_axis=0, concat_axis=0, tiled=True)  10.3 us
    all_to_all x1, waiting for transfers between devices, body(): lax.all_to_all(buffer, 'grp', split_axis=0, concat_axis=0, tiled=True)  9.98 us
    all_to_all x1, waiting for transfers between devices, body(): lax.all_to_all(partial, 'grp', split_axis=0, concat_axis=0, tiled=True)  9.98 us
    all_to_all x1, waiting for transfers between devices, body(): lax.all_to_all(down, 'grp', split_axis=0, concat_axis=0, tiled=True)  9.97 us
    all_gather x1, blocking collectives, body(): both = lax.all_gather(sent, 'sec', axis=0)  8.45 us
  transfers between devices with their start and end apart: 5, of which 5 were waited for; matrix products, arithmetic and copies ran while one was open for 1% of the time, Pallas kernels for 0%

profile of v3, /device:TPU:1, one launch (start us, length us, event | category | flops | bytes accessed | tf_op | source)
XLA Modules:
  0.0 153.3 jit_solution(7405445677294626905)
XLA Ops:
  0.0 0.0 copy-start
  0.7 0.8 reduce
  1.6 0.1 reshape.109.rope_ref
  1.6 0.1 pad_add_fusion.place_ref
  1.7 1.2 copy-done.1
  3.0 0.9 copy-done.4
  3.9 0.9 copy-done.5
  4.8 0.7 copy-done.7
  5.5 0.7 copy-done.8
  6.1 1.4 shard_map.136
  7.6 8.4 %all-gather = bf16[128,640]{1,0:T(8,128)(2,1)S(1)} all-gather(bf16[64,640]{1,0:T(8,128)(2,1)S(1)} %get-tuple-element.10), channel_id=2, replica_groups=mesh['sec'=2,'grp'=16,'dev'=16] {'sec'}, dimensions={0}, use_global_device_ids=true | all-gather | bytes 245760 | tf_op jit(solution)/shard_map/all_gather | solution.py:274
  16.0 0.2 fusion.8
  16.2 0.1 divide_convert_fusion
  16.4 12.7 %all_to_all.35 = bf16[16,4,512]{2,1,0:T(4,128)(2,1)S(1)} all-to-all(bf16[16,4,512]{2,1,0:T(4,128)(2,1)S(1)} %reshape.110), channel_id=1, replica_groups=mesh['sec'=2,'grp'=16,'dev'=16] {'grp'}, dimensions={0} | all-to-all | bytes 131072 | tf_op jit(solution)/shard_map/all_to_all | solution.py:296
  29.1 0.0 copy-done
  29.1 0.2 fusion
  29.3 0.0 copy-start.10
  29.3 0.7 broadcast_in_dim.48
  30.1 10.3 %all-to-all-start.1 = ((bf16[16,16,512]{2,1,0:T(8,128)(2,1)}), bf16[16,16,512]{2,1,0:T(8,128)(2,1)S(1)}, u32[]{:S(2)}, u32[]{:S(2)}) async-start(bf16[16,16,512]{2,1,0:T(8,128)(2,1)} %broadcast_in_dim.48), calls=%async_computation.1 | async-start | bytes 524288 | tf_op jit(solution)/shard_map/all_to_all | solution.py:20
  40.3 0.1 fusion.12
  40.4 0.1 add_select_fusion
  40.5 7.5 %all-to-all-done.1.gathered_ref = bf16[16,16,512]{2,1,0:T(8,128)(2,1)S(1)} async-done(((bf16[16,16,512]{2,1,0:T(8,128)(2,1)}), bf16[16,16,512]{2,1,0:T(8,128)(2,1)S(1)}, u32[]{:S(2)}, u32[]{:S(2)}) %all-to-all-start.1) | async-done | bytes 262176 | tf_op jit(solution)/shard_map/all_to_all | solution.py:20
  48.0 1.1 shard_map.137
  49.1 3.5 %all-to-all-start.2 = ((bf16[16,16,448]{2,1,0:T(8,128)(2,1)}), bf16[16,16,448]{2,1,0:T(8,128)(2,1)S(1)}, u32[]{:S(2)}, u32[]{:S(2)}) async-start(bf16[16,16,448]{2,1,0:T(8,128)(2,1)} %shard_map.137), calls=%async_computation.2 | async-start | bytes 524288 | tf_op jit(solution)/shard_map/all_to_all | solution.py:307
  52.7 0.1 broadcast_in_dim.49
  52.8 0.1 broadcast_in_dim.50
  52.9 0.1 fusion.1
  53.0 0.1 copy.31
  53.1 0.1 fusion.3
  53.2 10.0 %all-to-all-done.2 = bf16[16,16,448]{2,1,0:T(8,128)(2,1)S(1)} async-done(((bf16[16,16,448]{2,1,0:T(8,128)(2,1)}), bf16[16,16,448]{2,1,0:T(8,128)(2,1)S(1)}, u32[]{:S(2)}, u32[]{:S(2)}) %all-to-all-start.2) | async-done | bytes 229408 | tf_op jit(solution)/shard_map/all_to_all | solution.py:307
  63.3 0.1 fusion.6
  63.3 6.1 %all_gather.15.sums_ref = f32[2,16,448]{2,1,0:T(8,128)S(1)} all-gather(f32[1,16,448]{2,1,0:T(8,128)S(1)} %fusion.6), channel_id=1, replica_groups=mesh['sec'=2,'grp'=16,'dev'=16] {'sec'}, dimensions={0}, use_global_device_ids=true | all-gather | bytes 86016 | tf_op jit(solution)/shard_map/all_gather | solution.py:311
  69.4 1.1 shard_map.138
  70.6 3.5 %all-to-all-start.3 = ((bf16[16,16,512]{2,1,0:T(8,128)(2,1)}), bf16[16,16,512]{2,1,0:T(8,128)(2,1)S(1)}, u32[]{:S(2)}, u32[]{:S(2)}) async-start(bf16[16,16,512]{2,1,0:T(8,128)(2,1)} %get-tuple-element.12), calls=%async_computation.3 | async-start | bytes 524288 | tf_op jit(solution)/shard_map/all_to_all | solution.py:334
  74.1 0.5 copy.36
  74.6 0.2 pad.12.clone
  74.8 10.0 %all-to-all-done.3.received_ref = bf16[16,16,512]{2,1,0:T(8,128)(2,1)S(1)} async-done(((bf16[16,16,512]{2,1,0:T(8,128)(2,1)}), bf16[16,16,512]{2,1,0:T(8,128)(2,1)S(1)}, u32[]{:S(2)}, u32[]{:S(2)}) %all-to-all-start.3) | async-done | bytes 262176 | tf_op jit(solution)/shard_map/all_to_all | solution.py:334
  84.8 2.1 %shard_map.139 = bf16[16,200,128]{2,1,0:T(8,128)(2,1)} custom-call(bf16[16,16,512]{2,1,0:T(8,128)(2,1)S(1)} %all-to-all-done.3.received_ref, bf16[1024,1024]{1,0:T(8,128)(2,1)S(1)} %bitcast.55), custom_call_target="tpu_custom_call" | custom-call | tf_op jit(solution)/shard_map/pallas_call | solution.py:340
  86.9 6.5 %all-to-all-start.4 = ((bf16[16,200,128]{2,1,0:T(8,128)(2,1)}), bf16[16,200,128]{2,1,0:T(8,128)(2,1)S(1)}, u32[]{:S(2)}, u32[]{:S(2)}) async-start(bf16[16,200,128]{2,1,0:T(8,128)(2,1)} %shard_map.139), calls=%async_computation.4 | async-start | bytes 1638400 | tf_op jit(solution)/shard_map/all_to_all | solution.py:347
  93.4 18.9 %all-to-all-done.4.sums_ref = bf16[16,200,128]{2,1,0:T(8,128)(2,1)S(1)} async-done(((bf16[16,200,128]{2,1,0:T(8,128)(2,1)}), bf16[16,200,128]{2,1,0:T(8,128)(2,1)S(1)}, u32[]{:S(2)}, u32[]{:S(2)}) %all-to-all-start.4) | async-done | bytes 819232 | tf_op jit(solution)/shard_map/all_to_all | solution.py:347
  112.3 0.3 shard_map.140
  112.6 17.5 %all_to_all.36.packed_ref = bf16[16,24,512]{2,1,0:T(8,128)(2,1)S(1)} all-to-all(bf16[16,24,512]{2,1,0:T(8,128)(2,1)S(1)} %shard_map.140), channel_id=1, replica_groups=mesh['sec'=2,'grp'=16,'dev'=16] {'dev'}, dimensions={0} | all-to-all | bytes 786432 | tf_op jit(solution)/shard_map/all_to_all | solution.py:356
  130.1 1.4 shard_map.141
  131.5 3.7 %all-to-all-start.6 = ((bf16[16,16,448]{2,1,0:T(8,128)(2,1)}), bf16[16,16,448]{2,1,0:T(8,128)(2,1)S(1)}, u32[]{:S(2)}, u32[]{:S(2)}) async-start(bf16[16,16,448]{2,1,0:T(8,128)(2,1)} %shard_map.141), calls=%async_computation.6 | async-start | bytes 524288 | tf_op jit(solution)/shard_map/all_to_all | solution.py:364
  135.2 10.0 %all-to-all-done.6 = bf16[16,16,448]{2,1,0:T(8,128)(2,1)S(1)} async-done(((bf16[16,16,448]{2,1,0:T(8,128)(2,1)}), bf16[16,16,448]{2,1,0:T(8,128)(2,1)S(1)}, u32[]{:S(2)}, u32[]{:S(2)}) %all-to-all-start.6) | async-done | bytes 229408 | tf_op jit(solution)/shard_map/all_to_all | solution.py:364
  145.2 0.1 fusion.10
  145.4 7.4 %all_gather.16 = f32[2,8,448]{2,1,0:T(8,128)S(1)} all-gather(f32[1,8,448]{2,1,0:T(8,128)S(1)} %constant_dynamic-slice_fusion), channel_id=1, replica_groups=mesh['sec'=2,'grp'=16,'dev'=16] {'sec'}, dimensions={0}, use_global_device_ids=true | all-gather | bytes 43008 | tf_op jit(solution)/shard_map/all_gather | solution.py:368
  152.7 0.6 fusion.9
  (26 shorter events, 0.1 us)
Async XLA Ops:
  0.0 29.1 %copy-start = (bf16[4,512,128]{2,1,0:T(8,128)(2,1)S(1)}, bf16[4,512,128]{2,1,0:T(8,128)(2,1)}, u32[]{:S(2)}) copy-start(bf16[4,512,128]{2,1,0:T(8,128)(2,1)} %param.19) | copy-start | bytes 1572868
  1.7 1.2 copy-start.1
  3.0 0.9 copy-start.4
  3.9 0.9 copy-start.5
  4.8 0.7 copy-start.7
  5.4 0.7 copy-start.8
  6.1 41.9 %copy-start.3 = (bf16[512,448]{0,1:T(8,128)(2,1)S(1)}, bf16[512,448]{0,1:T(8,128)(2,1)}, u32[]{:S(2)}) copy-start(bf16[512,448]{0,1:T(8,128)(2,1)} %param.20) | copy-start | bytes 1376260
  16.0 36.8 %copy-start.11 = (bf16[8,448]{1,0:T(8,128)(2,1)S(1)}, bf16[8,448]{1,0:T(8,128)(2,1)}, u32[]{:S(2)}) copy-start(bf16[8,448]{1,0:T(8,128)(2,1)} %param.21) | copy-start | bytes 21508
  29.1 40.3 %copy-start.6 = (f32[448,16]{0,1:T(8,128)S(1)}, f32[448,16]{0,1:T(8,128)}, u32[]{:S(2)}) copy-start(f32[448,16]{0,1:T(8,128)} %param.23) | copy-start | bytes 86020
  29.1 40.3 %copy-start.9 = (f32[448]{0:T(512)S(1)}, f32[448]{0:T(512)}, u32[]{:S(2)}) copy-start(f32[448]{0:T(512)} %param.22) | copy-start | bytes 5380
  29.3 44.8 %copy-start.10 = (bf16[1,448,2,1024]{3,2,1,0:T(2,128)(2,1)S(1)}, bf16[1,448,2,1024]{3,2,1,0:T(2,128)(2,1)}, u32[]{:S(2)}) copy-start(bf16[1,448,2,1024]{3,2,1,0:T(2,128)(2,1)} %param.26) | copy-start | bytes 5505028
  30.1 17.9 %all-to-all-start.1 = ((bf16[16,16,512]{2,1,0:T(8,128)(2,1)}), bf16[16,16,512]{2,1,0:T(8,128)(2,1)S(1)}, u32[]{:S(2)}, u32[]{:S(2)}) async-start(bf16[16,16,512]{2,1,0:T(8,128)(2,1)} %broadcast_in_dim.48), calls=%async_computation.1 | async-start | bytes 524288 | tf_op jit(solution)/shard_map/all_to_all | solution.py:20
  49.1 14.1 %all-to-all-start.2 = ((bf16[16,16,448]{2,1,0:T(8,128)(2,1)}), bf16[16,16,448]{2,1,0:T(8,128)(2,1)S(1)}, u32[]{:S(2)}, u32[]{:S(2)}) async-start(bf16[16,16,448]{2,1,0:T(8,128)(2,1)} %shard_map.137), calls=%async_computation.2 | async-start | bytes 524288 | tf_op jit(solution)/shard_map/all_to_all | solution.py:307
  70.6 14.2 %all-to-all-start.3 = ((bf16[16,16,512]{2,1,0:T(8,128)(2,1)}), bf16[16,16,512]{2,1,0:T(8,128)(2,1)S(1)}, u32[]{:S(2)}, u32[]{:S(2)}) async-start(bf16[16,16,512]{2,1,0:T(8,128)(2,1)} %get-tuple-element.12), calls=%async_computation.3 | async-start | bytes 524288 | tf_op jit(solution)/shard_map/all_to_all | solution.py:334
  86.9 43.2 %copy-start.2 = (bf16[1,1024,448]{1,2,0:T(8,128)(2,1)S(1)}, bf16[1,1024,448]{1,2,0:T(8,128)(2,1)}, u32[]{:S(2)}) copy-start(bf16[1,1024,448]{1,2,0:T(8,128)(2,1)} %param.27) | copy-start | bytes 2752516
  86.9 25.4 %all-to-all-start.4 = ((bf16[16,200,128]{2,1,0:T(8,128)(2,1)}), bf16[16,200,128]{2,1,0:T(8,128)(2,1)S(1)}, u32[]{:S(2)}, u32[]{:S(2)}) async-start(bf16[16,200,128]{2,1,0:T(8,128)(2,1)} %shard_map.139), calls=%async_computation.4 | async-start | bytes 1638400 | tf_op jit(solution)/shard_map/all_to_all | solution.py:347
  131.5 13.7 %all-to-all-start.6 = ((bf16[16,16,448]{2,1,0:T(8,128)(2,1)}), bf16[16,16,448]{2,1,0:T(8,128)(2,1)S(1)}, u32[]{:S(2)}, u32[]{:S(2)}) async-start(bf16[16,16,448]{2,1,0:T(8,128)(2,1)} %shard_map.141), calls=%async_computation.6 | async-start | bytes 524288 | tf_op jit(solution)/shard_map/all_to_all | solution.py:364

commit v4 on v3

--- a/solution.py
+++ b/solution.py
@@ -41,21 +41,69 @@
 
 
 def attend_kernel(
-    place_ref, latent_ref, rope_ref, cache_ref, cache_rope_ref, routes_ref, slots_ref, sent_ref, kept_ref
+    place_ref,
+    latent_hbm,
+    rope_hbm,
+    cache_hbm,
+    cache_rope_hbm,
+    routes_ref,
+    slots_ref,
+    sent_ref,
+    kept_ref,
+    latent_ref,
+    rope_ref,
+    cache_ref,
+    cache_rope_ref,
+    sems,
 ):
-    heads = latent_ref.shape[0]
+    copies = [
+        pltpu.make_async_copy(source, target, sems.at[index])
+        for index, (source, target) in enumerate(
+            [
+                (rope_hbm, rope_ref),
+                (cache_rope_hbm, cache_rope_ref),
+                (latent_hbm, latent_ref),
+                (cache_hbm, cache_ref),
+            ]
+        )
+    ]
+    for copy in copies:
+        copy.start()
+    heads, latent = latent_ref.shape
     half = heads // 2
-    latent = latent_ref.shape[1]
+    width = cache_rope_ref.shape[0]
     mine = pl.multiple_of(place_ref[0] * half, half)
     other = pl.multiple_of(half - place_ref[0] * half, half)
 
-    def other_first(ref):
-        return jnp.concatenate([ref[pl.ds(other, half), :], ref[pl.ds(mine, half), :]], axis=0)
-
+    choices = routes_ref.shape[1]
+    spot = iota((choices, 128), 1) - iota((choices, 128), 0)
+    table = jnp.dot(
+        routes_ref[...].astype(f32), jnp.where(spot == 16, 1.0, 0.0), preferred_element_type=f32
+    ) + jnp.dot(
+        slots_ref[...].astype(f32), jnp.where(spot == 16 + choices, 1.0, 0.0), preferred_element_type=f32
+    )
+
+    copies[0].wait()
+    row = rope_ref[...].astype(f32)
+    pairs = jnp.concatenate(
+        [row[:, 128 * pair : 128 * pair + 128] for pair in range(heads * width // 128)], axis=0
+    )
+    head = iota((heads, heads // 2), 0) + jnp.where(
+        iota((heads, heads // 2), 0) < half, other, mine - half
+    )
+    picked = select_rows(one_hot(head >> 1 == iota((heads, heads // 2), 1)), pairs.astype(bf16))
+    lane_half = iota((heads, 128), 1) >> 6
+    picked = jnp.where(lane_half == (iota((heads, 128), 0) & 1), picked, jnp.zeros_like(picked))
+    copies[1].wait()
+    keys = cache_rope_ref[...]
+    rope_scores = jnp.dot(
+        picked, jnp.concatenate([keys, keys], axis=0), preferred_element_type=f32
+    )
+    copies[2].wait()
+    query = jnp.concatenate([latent_ref[pl.ds(other, half), :], latent_ref[pl.ds(mine, half), :]], axis=0)
+    copies[3].wait()
     cache = cache_ref[...]
-    scores = dot_nt(other_first(latent_ref), cache) + jnp.dot(
-        other_first(rope_ref), cache_rope_ref[...], preferred_element_type=f32
-    )
+    scores = dot_nt(query, cache) + rope_scores
     usable = iota(scores.shape, 1) < place_ref[1]
     masked = jnp.where(usable, scores * score_scale, masked_floor)
     top = jnp.max(masked, axis=1, keepdims=True).astype(bf16).astype(f32)
@@ -69,25 +117,52 @@
     side = jnp.where(lane == 2, mass - mass_high, side)
     kept_ref[:, :latent] = weighted[half:]
     kept_ref[:, latent:] = side[half:]
-    choices = routes_ref.shape[1]
-    spot = iota((choices, 128), 1) - iota((choices, 128), 0)
-    table = jnp.dot(
-        routes_ref[...].astype(f32), jnp.where(spot == 16, 1.0, 0.0), preferred_element_type=f32
-    ) + jnp.dot(
-        slots_ref[...].astype(f32), jnp.where(spot == 16 + choices, 1.0, 0.0), preferred_element_type=f32
-    )
     block_rows = table.shape[0]
     side = jnp.concatenate([side[:block_rows] + table, side[block_rows:half]], axis=0)
     sent_ref[:, :latent] = weighted[:half].astype(bf16)
     sent_ref[:, latent:] = side.astype(bf16)
 
 
+def block_sum_kernel(place_ref, partial_ref, resid_ref, out_ref):
+    total = partial_ref[0].astype(f32)
+    for group in range(1, partial_ref.shape[0]):
+        total = total + partial_ref[group].astype(f32)
+    block_rows = resid_ref.shape[0]
+    resid = resid_ref[...].astype(f32)
+    resid = jnp.concatenate([resid] * (total.shape[0] // block_rows), axis=0)
+    own = iota(total.shape, 0) // block_rows == place_ref[0]
+    out_ref[...] = total + jnp.where(own, resid, 0.0)
+
+
+def last_sum_kernel(place_ref, halves_ref, hidden_ref, out_ref):
+    block_rows = out_ref.shape[0]
+    own = pl.ds(pl.multiple_of(place_ref[0] * block_rows, block_rows), block_rows)
+    total = hidden_ref[own, :] + halves_ref[0, own, :] + halves_ref[1, own, :]
+    out_ref[...] = total.astype(bf16)
+
+
 def dispatch_kernel(
-    expert_total, sums_ref, gain_ref, router_ref, named_ref, placement_ref, buffer_ref, hidden_ref
+    expert_total, choices, capacity, sums_ref, gain_ref, router_ref, table_ref, buffer_ref, hidden_ref, placement_ref
 ):
+    table = table_ref[...].astype(f32).reshape(-1, 128)
+    rows = table.shape[0]
+    chunk = buffer_ref.shape[1]
+    slot_total = expert_total * chunk
+    lane = iota((rows, 128), 1)
+    block = jnp.where(iota((rows, 1), 0) < rows // 2, 0.0, 1.0 * capacity)
+    named = jnp.zeros((rows, 128), f32)
+    placement = jnp.zeros((rows, slot_total), f32)
+    spot = iota((rows, slot_total), 1).astype(f32)
+    for choice in range(choices):
+        route = table[:, 16 + choice : 17 + choice]
+        slot = table[:, 16 + choices + choice : 17 + choices + choice]
+        named = jnp.where(lane.astype(f32) == route, 1.0, named)
+        filled = jnp.where(slot < capacity, route * chunk + block + slot, -1.0)
+        placement = jnp.where(spot == filled, 1.0, placement)
+    placement_ref[...] = placement.astype(bf16)
     hidden = sums_ref[0] + sums_ref[1]
     hidden_ref[...] = hidden
-    rows, width = hidden.shape
+    width = hidden.shape[1]
     gained = hidden * gain_ref[...]
     squares = jnp.sum(hidden * hidden, axis=1, keepdims=True)
     square_high = squares.astype(bf16).astype(f32)
@@ -100,18 +175,22 @@
     )
     spread_out = jnp.concatenate([logits, jnp.zeros((rows, 128 - expert_total), f32)], axis=1)
     logit_high = spread_out.astype(bf16).astype(f32)
-    lane = iota((rows, 128), 1)
     first = width % 128
     side = pltpu.roll(logit_high, first, 1) + pltpu.roll(
         spread_out - logit_high, first + expert_total, 1
     )
-    side = side + pltpu.roll(named_ref[...], first + 2 * expert_total, 1)
+    side = side + pltpu.roll(named, first + 2 * expert_total, 1)
     side = jnp.where(lane == first + 3 * expert_total, square_high, side)
     side = jnp.where(lane == first + 3 * expert_total + 1, squares - square_high, side)
     full = width - first
     last = jnp.concatenate([gained[:, full:], jnp.zeros((rows, 128 - first), f32)], axis=1)
     content = jnp.concatenate([gained[:, :full], jnp.where(lane < first, last, side)], axis=1)
-    out = jnp.dot(placement_ref[...], content.astype(bf16), preferred_element_type=f32)
+    out = lax.dot_general(
+        placement.astype(bf16),
+        content.astype(bf16),
+        (((0,), (0,)), ((), ())),
+        preferred_element_type=f32,
+    )
     buffer_ref[...] = out.astype(bf16).reshape(buffer_ref.shape)
 
 
@@ -128,7 +207,7 @@
     out_ref[...] = out.reshape(out_ref.shape)
 
 
-def gate_up_kernel(received_ref, weight_ref, out_ref):
+def gate_up_kernel(expert_total, expert_ref, received_ref, weight_ref, out_ref):
     members, chunk, width = received_ref.shape
     total = members * chunk
     rows = received_ref[...].reshape(total, width)
@@ -144,6 +223,8 @@
     sums = jnp.dot(left, weight_ref[...], preferred_element_type=f32)
     side = received_ref[:, :, width - 128 :].astype(f32)
     first = iota((8, 128), 1) < 64
+    is_expert = (iota((8, 128), 1) & 63) == 3 * expert_total + 2
+    expert = expert_ref[0].astype(f32)
     columns = sums.shape[1] // 128
     for member in range(members):
         tiles = [
@@ -152,11 +233,12 @@
             for col in range(columns)
         ]
         turned = pltpu.roll(side[member, :8], 64, 1)
-        tiles.append(jnp.where(first, turned, side[member, 8:]))
+        last = jnp.where(first, turned, side[member, 8:])
+        tiles.append(jnp.where(is_expert, expert, last))
         out_ref[member] = jnp.concatenate(tiles, axis=0).astype(bf16)
 
 
-def activate_kernel(model_width, expert_total, sums_ref, expert_ref, out_ref):
+def activate_kernel(model_width, expert_total, sums_ref, out_ref):
     members, height, _ = sums_ref.shape
     columns = height // 24
     total = sums_ref[0].astype(f32)
@@ -180,7 +262,9 @@
     inverse_rms = lax.rsqrt(squares / model_width + norm_eps)
     scores = 1.0 / (1.0 + jnp.exp(-jnp.where(lane < expert_total, logits * inverse_rms, 0.0)))
     chosen = (named > 0.5) & (lane < expert_total)
-    picked = jnp.sum(jnp.where(lane == expert_ref[0], scores, 0.0), axis=1, keepdims=True)
+    expert = jnp.sum(jnp.where(lane == square_lane + 2, side, 0.0), axis=1, keepdims=True)
+    is_own = lane.astype(f32) * members == expert
+    picked = jnp.sum(jnp.where(is_own, scores, 0.0), axis=1, keepdims=True)
     denominator = jnp.sum(jnp.where(chosen, scores, 0.0), axis=1, keepdims=True)
     occupied = denominator > 0.0
     weight = route_scale * picked / jnp.where(occupied, denominator, 1.0)
@@ -248,6 +332,7 @@
     expert_total = router.shape[1]
     capacity = max(2, 3 * block_rows // 4)
     pair_rows = sections * block_rows
+    in_smem = pl.BlockSpec(memory_space=pltpu.SMEM)
     vmem = pltpu.CompilerParams(vmem_limit_bytes=32 * 2**20)
 
     place = jnp.stack([section, lengths[0] - section * hist_local]).astype(jnp.int32)
@@ -257,13 +342,20 @@
             jax.ShapeDtypeStruct((half_heads, latent + 128), bf16),
             jax.ShapeDtypeStruct((half_heads, latent + 128), f32),
         ),
-        in_specs=[pl.BlockSpec(memory_space=pltpu.SMEM)] + in_vmem(6),
+        in_specs=[in_smem] + [pl.BlockSpec(memory_space=pl.ANY)] * 4 + in_vmem(2),
         out_specs=tuple(in_vmem(2)),
+        scratch_shapes=[
+            pltpu.VMEM((head_total, latent), bf16),
+            pltpu.VMEM(q_rope.shape, bf16),
+            pltpu.VMEM(cache_latent.shape[1:], bf16),
+            pltpu.VMEM(cache_rope.shape[1:], bf16),
+            pltpu.SemaphoreType.DMA((4,)),
+        ],
         compiler_params=vmem,
     )(
         place,
         q_latent[0],
-        q_rope.reshape(head_total, rope_width),
+        q_rope,
         cache_latent[0],
         cache_rope[0],
         routes,
@@ -288,9 +380,7 @@
         kept_part[:, :latent] * factor_mine + theirs[:, :latent].astype(f32) * factor_theirs
     ) / mass_both
     latent_out = latent_out.astype(bf16)
-    pair_table = both[:, :block_rows, latent + 16 : latent + 16 + 2 * choices]
-    pair_table = pair_table.reshape(pair_rows, 2 * choices).astype(jnp.int32)
-    pair_routes, pair_slots = pair_table[:, :choices], pair_table[:, choices:]
+    tables = both[:, :block_rows, latent:]
 
     outgoing_heads = latent_out.reshape(groups, head_block, latent)
     arrived = lax.all_to_all(outgoing_heads, "grp", split_axis=0, concat_axis=0, tiled=True)
@@ -305,32 +395,28 @@
         compiler_params=vmem,
     )(gathered, w_out.T)
     partial = lax.all_to_all(partial, "grp", split_axis=0, concat_axis=0, tiled=True)
-    summed = jnp.sum(partial.astype(f32), axis=0).reshape(sections, block_rows, width_local)
-    is_mine = (jnp.arange(sections) == section)[:, None, None]
-    summed = summed + jnp.where(is_mine, resid.astype(f32)[None], 0.0)
-    summed = lax.all_gather(summed.reshape(pair_rows, width_local), "sec", axis=0)
-
-    expert_ids = jnp.arange(expert_total, dtype=jnp.int32)
-    named = jnp.any(pair_routes[:, :, None] == expert_ids[None, None, :], axis=1)
-    named = jnp.pad(named.astype(f32), ((0, 0), (0, 128 - expert_total)))
+    summed = pl.pallas_call(
+        block_sum_kernel,
+        out_shape=jax.ShapeDtypeStruct((pair_rows, width_local), f32),
+        in_specs=[in_smem] + in_vmem(2),
+        out_specs=in_vmem(1)[0],
+        compiler_params=vmem,
+    )(place, partial, resid)
+    summed = lax.all_gather(summed, "sec", axis=0)
+
     chunk = 16
-    block_of_row = jnp.arange(pair_rows, dtype=jnp.int32)[:, None] // block_rows
-    kept = pair_slots < capacity
-    slot_index = pair_routes * chunk + block_of_row * capacity + pair_slots
-    slot_index = jnp.where(kept, slot_index, -1)
-    slot_ids = jnp.arange(expert_total * chunk, dtype=jnp.int32)
-    placement = jnp.any(slot_index[:, :, None] == slot_ids[None, None, :], axis=1).astype(bf16)
     padded_width = width_local + -width_local % 128
-    buffer, hidden = pl.pallas_call(
-        functools.partial(dispatch_kernel, expert_total),
+    buffer, hidden, placement = pl.pallas_call(
+        functools.partial(dispatch_kernel, expert_total, choices, capacity),
         out_shape=(
             jax.ShapeDtypeStruct((expert_total, chunk, padded_width), bf16),
             jax.ShapeDtypeStruct((pair_rows, width_local), f32),
+            jax.ShapeDtypeStruct((pair_rows, expert_total * chunk), bf16),
         ),
-        in_specs=in_vmem(5),
-        out_specs=tuple(in_vmem(2)),
-        compiler_params=vmem,
-    )(summed, norm_gain[None], router.T, named, placement.T)
+        in_specs=in_vmem(4),
+        out_specs=tuple(in_vmem(3)),
+        compiler_params=vmem,
+    )(summed, norm_gain[None], router.T, tables)
     received = lax.all_to_all(buffer, "grp", split_axis=0, concat_axis=0, tiled=True)
 
     unit = w_gateup.shape[3]
@@ -338,20 +424,20 @@
         w_gateup[0].transpose(1, 0, 2), ((0, 0), (0, padded_width - width_local), (0, 0))
     ).reshape(2 * padded_width, unit)
     sums = pl.pallas_call(
-        gate_up_kernel,
+        functools.partial(gate_up_kernel, expert_total),
         out_shape=jax.ShapeDtypeStruct((members, 24 * unit // 128 + 8, 128), bf16),
-        in_specs=in_vmem(2),
-        out_specs=in_vmem(1)[0],
-        compiler_params=vmem,
-    )(received, weight)
+        in_specs=[in_smem] + in_vmem(2),
+        out_specs=in_vmem(1)[0],
+        compiler_params=vmem,
+    )(lax.axis_index("grp").reshape(1), received, weight)
     sums = lax.all_to_all(sums, "dev", split_axis=0, concat_axis=0, tiled=True)
     packed = pl.pallas_call(
         functools.partial(activate_kernel, width_local * members, expert_total),
         out_shape=jax.ShapeDtypeStruct((members, 24, unit // 2), bf16),
-        in_specs=[in_vmem(1)[0], pl.BlockSpec(memory_space=pltpu.SMEM)],
-        out_specs=in_vmem(1)[0],
-        compiler_params=vmem,
-    )(sums, lax.axis_index("grp").reshape(1))
+        in_specs=in_vmem(1),
+        out_specs=in_vmem(1)[0],
+        compiler_params=vmem,
+    )(sums)
 
     everyone = lax.all_to_all(packed, "dev", split_axis=0, concat_axis=0, tiled=True)
     down = pl.pallas_call(
@@ -364,14 +450,14 @@
     returned = lax.all_to_all(down, "grp", split_axis=0, concat_axis=0, tiled=True)
     returned = returned.reshape(expert_total * chunk, width_local)
     mixture = jnp.dot(placement, returned, preferred_element_type=f32)
-    mixture = mixture.reshape(sections, block_rows, width_local)
-    both_halves = lax.all_gather(
-        lax.dynamic_index_in_dim(mixture, other, 0, False), "sec", axis=0
-    )
-    from_other = lax.dynamic_index_in_dim(both_halves, other, 0, False)
-    mine = lax.dynamic_index_in_dim(mixture, section, 0, False)
-    hidden_mine = lax.dynamic_slice_in_dim(hidden, section * block_rows, block_rows, 0)
-    return (hidden_mine + mine + from_other).astype(bf16)
+    halves = lax.all_gather(mixture, "sec", axis=0)
+    return pl.pallas_call(
+        last_sum_kernel,
+        out_shape=jax.ShapeDtypeStruct((block_rows, width_local), bf16),
+        in_specs=[in_smem] + in_vmem(2),
+        out_specs=in_vmem(1)[0],
+        compiler_params=vmem,
+    )(place, halves, hidden)
 
 
 def solution(mesh):

time: 154 us -> 153 us (level)
  blocking collectives: 52.1 us -> 108 us
  waiting for transfers between devices: 56.3 us -> 20.5 us
  starting transfers between devices: 27.5 us -> 7.06 us
  other arithmetic: 2.36 us -> 0.38 us
    all_to_all x0 -> x3, blocking collectives: none -> 57.6 us  [the longest x1 26.2 us: body(): sums = lax.all_to_all(sums, 'dev', split_axis=0, concat_axis=0, tiled=True)]
    all_to_all x3 -> x0, waiting for transfers between devices: 36.4 us -> none  [the longest x1 18.9 us: body(): sums = lax.all_to_all(sums, 'dev', split_axis=0, concat_axis=0, tiled=True)]
    all_to_all x3 -> x0, starting transfers between devices: 20.5 us -> none  [the longest x1 10.3 us: spread(): return lax.all_to_all(copies, axis, split_axis=0, concat_axis=0, tiled=True)]
    all_to_all x1, blocking collectives: 17.5 us -> 15.8 us  [body(): lax.all_to_all(packed, 'dev', split_axis=0, concat_axis=0, tiled=True)]
    pallas_call x2 -> x4, Pallas kernels: 3.23 us -> 4.17 us  [the longest x1 1.23 us: body(): pl.pallas_call(functools.partial(dispatch_kernel, expert_total, choices,...]
    unnamed x25 -> x27, local copies, waits for them, and re-layouts: 4.95 us -> 5.72 us
  transfers between devices with their start and end apart: 5 -> 2, of which waited for: 5 -> 2; matrix products, arithmetic and copies ran while one was open for 1% -> 0% of each run, Pallas kernels for 0% -> 0%
where the time goes in v4:
time: 153 us; the launch traced here: 152 us
  blocking collectives  108 us (71%)
  waiting for transfers between devices  20.5 us (13%)
  Pallas kernels  8.59 us (6%)
  starting transfers between devices  7.06 us (5%)
  local copies, waits for them, and re-layouts  5.97 us (4%)
    all_to_all x1, blocking collectives, body(): sums = lax.all_to_all(sums, 'dev', split_axis=0, concat_axis=0, tiled=True)  26.2 us
    all_to_all x1, blocking collectives, spread(): return lax.all_to_all(copies, axis, split_axis=0, concat_axis=0, tiled=True)  17.9 us
    all_to_all x1, blocking collectives, body(): lax.all_to_all(packed, 'dev', split_axis=0, concat_axis=0, tiled=True)  15.8 us
    all_to_all x1, blocking collectives, body(): lax.all_to_all(down, 'grp', split_axis=0, concat_axis=0, tiled=True)  13.5 us
    all_to_all x1, blocking collectives, body(): lax.all_to_all(outgoing_heads, 'grp', split_axis=0, concat_axis=0, tiled=...  12.7 us
    all_to_all x1, waiting for transfers between devices, body(): lax.all_to_all(partial, 'grp', split_axis=0, concat_axis=0, tiled=True)  10.5 us
    all_to_all x1, waiting for transfers between devices, body(): lax.all_to_all(buffer, 'grp', split_axis=0, concat_axis=0, tiled=True)  9.98 us
    all_gather x1, blocking collectives, body(): both = lax.all_gather(sent, 'sec', axis=0)  8.46 us
  transfers between devices with their start and end apart: 2, of which 2 were waited for; matrix products, arithmetic and copies ran while one was open for 0% of the time, Pallas kernels for 0%

profile of v4, /device:TPU:1, one launch (start us, length us, event | category | flops | bytes accessed | tf_op | source)
XLA Modules:
  0.0 151.8 jit_solution(9855107231706924941)
XLA Ops:
  0.0 0.0 copy-start
  0.7 0.1 pad_add_fusion.place_ref
  0.8 0.0 copy-start.1
  0.8 1.2 copy-done.1
  2.0 0.0 copy-start.4
  2.0 0.9 copy-done.4
  2.9 0.0 copy-start.5
  2.9 0.9 copy-done.5
  3.8 0.0 copy-start.6
  3.8 0.8 copy-done.6
  4.6 0.7 copy-done.9
  5.3 0.7 copy-done.10
  6.0 2.3 %shard_map.136 = (bf16[64,640]{1,0:T(8,128)(2,1)S(1)}, f32[64,640]{1,0:T(8,128)S(1)}) custom-call(s32[2]{0:T(128)S(1)} %pad_add_fusion.place_ref, bf16[128,512]{1,0:T(8,128)(2,1)S(1)} %bitcast.39, bf16[1,8192]{1,0:T(2,128)(2,1)S(1)} %copy-done.6, bf16[1024,512]{1,0:T(8,128)(2,1)S(1)} %bitcast.34, bf16[64,1024]{1,0:T(8,128)(2,1)S(1)} %bitcast.40, ...), custom_call_target="tpu_custom_call" | custom-call | tf_op jit(solution)/shard_map/pallas_call | solution.py:339
  8.2 8.5 %all-gather = bf16[128,640]{1,0:T(8,128)(2,1)S(1)} all-gather(bf16[64,640]{1,0:T(8,128)(2,1)S(1)} %get-tuple-element.11), channel_id=2, replica_groups=mesh['sec'=2,'grp'=16,'dev'=16] {'sec'}, dimensions={0}, use_global_device_ids=true | all-gather | bytes 245760 | tf_op jit(solution)/shard_map/all_gather | solution.py:366
  16.7 0.2 fusion.5
  16.9 0.1 divide_convert_fusion
  17.0 0.0 copy-start.7
  17.0 0.0 copy-start.11
  17.1 12.7 %all_to_all.35 = bf16[16,4,512]{2,1,0:T(4,128)(2,1)S(1)} all-to-all(bf16[16,4,512]{2,1,0:T(4,128)(2,1)S(1)} %reshape.13), channel_id=1, replica_groups=mesh['sec'=2,'grp'=16,'dev'=16] {'grp'}, dimensions={0} | all-to-all | bytes 131072 | tf_op jit(solution)/shard_map/all_to_all | solution.py:386
  29.8 0.0 copy-done
  29.8 0.2 fusion
  30.0 17.9 %all_to_all.36.gathered_ref = bf16[16,16,512]{2,1,0:T(8,128)(2,1)S(1)} all-to-all(bf16[16,16,512]{2,1,0:T(8,128)(2,1)S(1)} %broadcast_in_dim.11), channel_id=1, replica_groups=mesh['sec'=2,'grp'=16,'dev'=16] {'dev'}, dimensions={0} | all-to-all | bytes 524288 | tf_op jit(solution)/shard_map/all_to_all | solution.py:20
  47.9 0.0 copy-done.3
  47.9 1.1 shard_map.137
  49.0 3.5 %all-to-all-start.2 = ((bf16[16,16,448]{2,1,0:T(8,128)(2,1)}), bf16[16,16,448]{2,1,0:T(8,128)(2,1)S(1)}, u32[]{:S(2)}, u32[]{:S(2)}) async-start(bf16[16,16,448]{2,1,0:T(8,128)(2,1)} %shard_map.137), calls=%async_computation.2 | async-start | bytes 524288 | tf_op jit(solution)/shard_map/all_to_all | solution.py:397
  52.6 10.5 %all-to-all-done.2.partial_ref = bf16[16,16,448]{2,1,0:T(8,128)(2,1)S(1)} async-done(((bf16[16,16,448]{2,1,0:T(8,128)(2,1)}), bf16[16,16,448]{2,1,0:T(8,128)(2,1)S(1)}, u32[]{:S(2)}, u32[]{:S(2)}) %all-to-all-start.2) | async-done | bytes 229408 | tf_op jit(solution)/shard_map/all_to_all | solution.py:397
  63.1 0.0 copy-done.8
  63.1 0.6 shard_map.138
  63.7 6.1 %all-gather.1 = f32[32,448]{1,0:T(8,128)S(1)} all-gather(f32[16,448]{1,0:T(8,128)S(1)} %shard_map.138), channel_id=3, replica_groups=mesh['sec'=2,'grp'=16,'dev'=16] {'sec'}, dimensions={0}, use_global_device_ids=true | all-gather | bytes 86016 | tf_op jit(solution)/shard_map/all_gather | solution.py:405
  69.8 0.0 copy-done.7
  69.8 0.0 copy-done.11
  69.8 1.2 shard_map.139
  71.0 3.5 %all-to-all-start.3 = ((bf16[16,16,512]{2,1,0:T(8,128)(2,1)}), bf16[16,16,512]{2,1,0:T(8,128)(2,1)S(1)}, u32[]{:S(2)}, u32[]{:S(2)}) async-start(bf16[16,16,512]{2,1,0:T(8,128)(2,1)} %get-tuple-element.13), calls=%async_computation.3 | async-start | bytes 524288 | tf_op jit(solution)/shard_map/all_to_all | solution.py:420
  74.6 0.0 copy-done.12
  74.6 0.5 copy.23
  75.1 0.2 pad.4.clone
  75.3 10.0 %all-to-all-done.3.received_ref = bf16[16,16,512]{2,1,0:T(8,128)(2,1)S(1)} async-done(((bf16[16,16,512]{2,1,0:T(8,128)(2,1)}), bf16[16,16,512]{2,1,0:T(8,128)(2,1)S(1)}, u32[]{:S(2)}, u32[]{:S(2)}) %all-to-all-start.3) | async-done | bytes 262176 | tf_op jit(solution)/shard_map/all_to_all | solution.py:420
  85.3 1.2 shard_map.140
  86.5 0.0 copy-start.2
  86.5 26.2 %all_to_all.37.sums_ref = bf16[16,200,128]{2,1,0:T(8,128)(2,1)S(1)} all-to-all(bf16[16,200,128]{2,1,0:T(8,128)(2,1)S(1)} %shard_map.140), channel_id=1, replica_groups=mesh['sec'=2,'grp'=16,'dev'=16] {'dev'}, dimensions={0} | all-to-all | bytes 1638400 | tf_op jit(solution)/shard_map/all_to_all | solution.py:433
  112.7 0.3 shard_map.141
  113.0 15.8 %all_to_all.38.packed_ref = bf16[16,24,512]{2,1,0:T(8,128)(2,1)S(1)} all-to-all(bf16[16,24,512]{2,1,0:T(8,128)(2,1)S(1)} %shard_map.141), channel_id=1, replica_groups=mesh['sec'=2,'grp'=16,'dev'=16] {'dev'}, dimensions={0} | all-to-all | bytes 786432 | tf_op jit(solution)/shard_map/all_to_all | solution.py:442
  128.8 0.0 copy-done.2
  128.8 0.7 shard_map.142
  129.5 13.5 %all_to_all.39 = bf16[16,16,448]{2,1,0:T(8,128)(2,1)S(1)} all-to-all(bf16[16,16,448]{2,1,0:T(8,128)(2,1)S(1)} %shard_map.142), channel_id=1, replica_groups=mesh['sec'=2,'grp'=16,'dev'=16] {'grp'}, dimensions={0} | all-to-all | bytes 458752 | tf_op jit(solution)/shard_map/all_to_all | solution.py:450
  143.1 0.1 fusion.6
  143.2 7.5 %all-gather.2 = f32[32,448]{1,0:T(8,128)S(1)} all-gather(f32[16,448]{1,0:T(8,128)S(1)} %fusion.6), channel_id=4, replica_groups=mesh['sec'=2,'grp'=16,'dev'=16] {'sec'}, dimensions={0}, use_global_device_ids=true | all-gather | bytes 86016 | tf_op jit(solution)/shard_map/all_gather | solution.py:453
  150.7 1.1 shard_map.143
  (10 shorter events, 0.1 us)
Async XLA Ops:
  0.0 29.8 %copy-start = (bf16[4,512,128]{2,1,0:T(8,128)(2,1)S(1)}, bf16[4,512,128]{2,1,0:T(8,128)(2,1)}, u32[]{:S(2)}) copy-start(bf16[4,512,128]{2,1,0:T(8,128)(2,1)} %param.19) | copy-start | bytes 1572868
  0.8 1.2 copy-start.1
  2.0 0.9 copy-start.4
  2.9 0.9 copy-start.5
  3.8 0.8 copy-start.6
  4.6 0.7 copy-start.9
  5.3 0.7 copy-start.10
  6.0 41.9 %copy-start.3 = (bf16[512,448]{0,1:T(8,128)(2,1)S(1)}, bf16[512,448]{0,1:T(8,128)(2,1)}, u32[]{:S(2)}) copy-start(bf16[512,448]{0,1:T(8,128)(2,1)} %param.20) | copy-start | bytes 1376260
  16.7 46.4 %copy-start.8 = (bf16[8,448]{1,0:T(8,128)(2,1)S(1)}, bf16[8,448]{1,0:T(8,128)(2,1)}, u32[]{:S(2)}) copy-start(bf16[8,448]{1,0:T(8,128)(2,1)} %resid_ref.1) | copy-start | bytes 21508
  17.0 52.8 %copy-start.7 = (f32[448,16]{0,1:T(8,128)S(1)}, f32[448,16]{0,1:T(8,128)}, u32[]{:S(2)}) copy-start(f32[448,16]{0,1:T(8,128)} %param.23) | copy-start | bytes 86020
  17.0 52.8 %copy-start.11 = (f32[448]{0:T(512)S(1)}, f32[448]{0:T(512)}, u32[]{:S(2)}) copy-start(f32[448]{0:T(512)} %param.22) | copy-start | bytes 5380
  30.0 44.6 %copy-start.12 = (bf16[1,448,2,1024]{3,2,1,0:T(2,128)(2,1)S(1)}, bf16[1,448,2,1024]{3,2,1,0:T(2,128)(2,1)}, u32[]{:S(2)}) copy-start(bf16[1,448,2,1024]{3,2,1,0:T(2,128)(2,1)} %param.26) | copy-start | bytes 5505028
  49.0 14.1 %all-to-all-start.2 = ((bf16[16,16,448]{2,1,0:T(8,128)(2,1)}), bf16[16,16,448]{2,1,0:T(8,128)(2,1)S(1)}, u32[]{:S(2)}, u32[]{:S(2)}) async-start(bf16[16,16,448]{2,1,0:T(8,128)(2,1)} %shard_map.137), calls=%async_computation.2 | async-start | bytes 524288 | tf_op jit(solution)/shard_map/all_to_all | solution.py:397
  71.0 14.3 %all-to-all-start.3 = ((bf16[16,16,512]{2,1,0:T(8,128)(2,1)}), bf16[16,16,512]{2,1,0:T(8,128)(2,1)S(1)}, u32[]{:S(2)}, u32[]{:S(2)}) async-start(bf16[16,16,512]{2,1,0:T(8,128)(2,1)} %get-tuple-element.13), calls=%async_computation.3 | async-start | bytes 524288 | tf_op jit(solution)/shard_map/all_to_all | solution.py:420
  86.5 42.3 %copy-start.2 = (bf16[1,1024,448]{1,2,0:T(8,128)(2,1)S(1)}, bf16[1,1024,448]{1,2,0:T(8,128)(2,1)}, u32[]{:S(2)}) copy-start(bf16[1,1024,448]{1,2,0:T(8,128)(2,1)} %param.27) | copy-start | bytes 2752516

commit v5 on v4

--- a/solution.py
+++ b/solution.py
@@ -40,16 +40,56 @@
     return lax.dot_general(left, right, (((1,), (1,)), ((), ())), preferred_element_type=f32)
 
 
+def pad_lanes(value):
+    spare = -value.shape[1] % 128
+    if spare == 0:
+        return value
+    return jnp.concatenate([value, jnp.zeros((value.shape[0], spare), value.dtype)], axis=1)
+
+
+def pack_pair(upper, lower):
+    full = upper.shape[1] // 128 * 128
+    tiles = [block[:, at : at + 128] for block in (upper, lower) for at in range(0, full, 128)]
+    tail = pad_lanes(upper[:, full:]) + pltpu.roll(pad_lanes(lower[:, full:]), 64, 1)
+    return jnp.concatenate(tiles + [tail], axis=0)
+
+
+def unpack_pair(packed):
+    full = packed.shape[0] // 16
+    tiles = [packed[8 * at : 8 * at + 8] for at in range(2 * full + 1)]
+    first = iota((8, 128), 1) < 64
+    upper = jnp.concatenate(tiles[:full] + [jnp.where(first, tiles[-1], 0.0)], axis=1)
+    turned = pltpu.roll(tiles[-1], 64, 1)
+    lower = jnp.concatenate(tiles[full:-1] + [jnp.where(first, turned, 0.0)], axis=1)
+    return jnp.concatenate([upper, lower], axis=0)
+
+
+def pack_slots(upper, lower):
+    half = upper.shape[1] // 2
+    last = jnp.where(
+        iota((8, half), 0) < 4, lower[:, :half], pltpu.roll(lower[:, half:], 4, 0)
+    )
+    return jnp.concatenate([upper[:, :half], upper[:, half:], last], axis=0)
+
+
+def unpack_slots(packed):
+    last = packed[16:]
+    upper = jnp.concatenate([packed[:8], packed[8:16]], axis=1)
+    return upper, jnp.concatenate([last, pltpu.roll(last, 4, 0)], axis=1)
+
+
 def attend_kernel(
     place_ref,
     latent_hbm,
     rope_hbm,
     cache_hbm,
     cache_rope_hbm,
+    routes_hbm,
+    slots_hbm,
+    sent_ref,
+    kept_ref,
     routes_ref,
     slots_ref,
-    sent_ref,
-    kept_ref,
     latent_ref,
     rope_ref,
     cache_ref,
@@ -64,11 +104,15 @@
                 (cache_rope_hbm, cache_rope_ref),
                 (latent_hbm, latent_ref),
                 (cache_hbm, cache_ref),
+                (routes_hbm, routes_ref),
+                (slots_hbm, slots_ref),
             ]
         )
     ]
     for copy in copies:
         copy.start()
+    copies[4].wait()
+    copies[5].wait()
     heads, latent = latent_ref.shape
     half = heads // 2
     width = cache_rope_ref.shape[0]
@@ -123,57 +167,68 @@
     sent_ref[:, latent:] = side.astype(bf16)
 
 
-def block_sum_kernel(place_ref, partial_ref, resid_ref, out_ref):
+def block_sum_kernel(section_ref, partial_ref, resid_ref, out_ref):
     total = partial_ref[0].astype(f32)
     for group in range(1, partial_ref.shape[0]):
         total = total + partial_ref[group].astype(f32)
-    block_rows = resid_ref.shape[0]
     resid = resid_ref[...].astype(f32)
-    resid = jnp.concatenate([resid] * (total.shape[0] // block_rows), axis=0)
-    own = iota(total.shape, 0) // block_rows == place_ref[0]
-    out_ref[...] = total + jnp.where(own, resid, 0.0)
-
-
-def last_sum_kernel(place_ref, halves_ref, hidden_ref, out_ref):
-    block_rows = out_ref.shape[0]
-    own = pl.ds(pl.multiple_of(place_ref[0] * block_rows, block_rows), block_rows)
-    total = hidden_ref[own, :] + halves_ref[0, own, :] + halves_ref[1, own, :]
-    out_ref[...] = total.astype(bf16)
+    section = section_ref[...]
+    upper = jnp.where(section == 0, resid, 0.0)
+    lower = jnp.where(section == 1, resid, 0.0)
+    out_ref[...] = total + pack_pair(upper, lower)
+
+
+def last_sum_kernel(section_ref, halves_ref, hidden_ref, out_ref):
+    block_rows, width = out_ref.shape
+    total = halves_ref[0] + halves_ref[1]
+    rows = total.shape[0] // 2
+    total = hidden_ref[...] + jnp.concatenate([total[:rows], total[rows:]], axis=1)
+    own = jnp.where(section_ref[...] == 0, total[:block_rows], total[block_rows:])
+    out_ref[...] = own[:, :width].astype(bf16)
 
 
 def dispatch_kernel(
-    expert_total, choices, capacity, sums_ref, gain_ref, router_ref, table_ref, buffer_ref, hidden_ref, placement_ref
+    expert_total, choices, capacity, sums_ref, gain_ref, router_ref, both_ref, buffer_ref, hidden_ref, placement_ref
 ):
-    table = table_ref[...].astype(f32).reshape(-1, 128)
+    latent = both_ref.shape[2] - 128
+    table = both_ref[:, :8, latent:].astype(f32).reshape(16, 128)
     rows = table.shape[0]
     chunk = buffer_ref.shape[1]
-    slot_total = expert_total * chunk
     lane = iota((rows, 128), 1)
     block = jnp.where(iota((rows, 1), 0) < rows // 2, 0.0, 1.0 * capacity)
     named = jnp.zeros((rows, 128), f32)
-    placement = jnp.zeros((rows, slot_total), f32)
-    spot = iota((rows, slot_total), 1).astype(f32)
+    spot = iota((rows, expert_total * chunk), 1).astype(f32)
+    low = jnp.zeros(spot.shape, f32)
+    high = jnp.zeros(spot.shape, f32)
     for choice in range(choices):
         route = table[:, 16 + choice : 17 + choice]
         slot = table[:, 16 + choices + choice : 17 + choices + choice]
         named = jnp.where(lane.astype(f32) == route, 1.0, named)
-        filled = jnp.where(slot < capacity, route * chunk + block + slot, -1.0)
-        placement = jnp.where(spot == filled, 1.0, placement)
-    placement_ref[...] = placement.astype(bf16)
-    hidden = sums_ref[0] + sums_ref[1]
+        packed = block + slot
+        early = packed < 8
+        kept = slot < capacity
+        start = route * chunk + packed
+        low_spot = jnp.where(kept, start + jnp.where(early, 0.0, 8.0), -1.0)
+        high_spot = jnp.where(kept, start + jnp.where(early, 8.0, 12.0), -1.0)
+        low = jnp.where(spot == low_spot, 1.0, low)
+        high = jnp.where(spot == high_spot, 1.0, high)
+    placement = jnp.concatenate([low, high], axis=0).astype(bf16)
+    placement_ref[...] = placement
+
+    hidden = unpack_pair(sums_ref[0] + sums_ref[1])
     hidden_ref[...] = hidden
-    width = hidden.shape[1]
-    gained = hidden * gain_ref[...]
+    width = gain_ref.shape[1]
+    gained = hidden * pad_lanes(gain_ref[...])
     squares = jnp.sum(hidden * hidden, axis=1, keepdims=True)
     square_high = squares.astype(bf16).astype(f32)
     logits = lax.dot_general(
-        gained,
+        gained[:, :width],
         router_ref[...],
         (((1,), (1,)), ((), ())),
         preferred_element_type=f32,
         precision=lax.Precision.HIGHEST,
     )
-    spread_out = jnp.concatenate([logits, jnp.zeros((rows, 128 - expert_total), f32)], axis=1)
+    spread_out = pad_lanes(logits)
     logit_high = spread_out.astype(bf16).astype(f32)
     first = width % 128
     side = pltpu.roll(logit_high, first, 1) + pltpu.roll(
@@ -183,13 +238,12 @@
     side = jnp.where(lane == first + 3 * expert_total, square_high, side)
     side = jnp.where(lane == first + 3 * expert_total + 1, squares - square_high, side)
     full = width - first
-    last = jnp.concatenate([gained[:, full:], jnp.zeros((rows, 128 - first), f32)], axis=1)
-    content = jnp.concatenate([gained[:, :full], jnp.where(lane < first, last, side)], axis=1)
+    last = jnp.where(lane < first, gained[:, full:], side)
+    content = jnp.concatenate([gained[:, :full], last], axis=1)
+    half = content.shape[1] // 2
+    content = jnp.concatenate([content[:, :half], content[:, half:]], axis=0)
     out = lax.dot_general(
-        placement.astype(bf16),
-        content.astype(bf16),
-        (((0,), (0,)), ((), ())),
-        preferred_element_type=f32,
+        placement, content.astype(bf16), (((0,), (0,)), ((), ())), preferred_element_type=f32
     )
     buffer_ref[...] = out.astype(bf16).reshape(buffer_ref.shape)
 
@@ -203,28 +257,34 @@
     wanted = (target >> 3 & 1) * (total // 2) + (target >> 4) * 8 + (target & 7)
     found = (source & (groups - 1)) * members + (source >> 4)
     rows = select_rows(one_hot(wanted == found), rows)
-    out = dot_nt(rows, weight_ref[...]).astype(bf16)
-    out_ref[...] = out.reshape(out_ref.shape)
+    out = dot_nt(rows, weight_ref[...])
+    for owner in range(out_ref.shape[0]):
+        start = 16 * owner
+        packed = pack_pair(out[start : start + 8], out[start + 8 : start + 16])
+        out_ref[owner] = packed.astype(bf16)
 
 
 def gate_up_kernel(expert_total, expert_ref, received_ref, weight_ref, out_ref):
-    members, chunk, width = received_ref.shape
-    total = members * chunk
-    rows = received_ref[...].reshape(total, width)
-    shape = (24 * members, total)
-    target = iota(shape, 0)
-    source = iota(shape, 1)
-    base = 24 * (source >> 4)
-    slot = source & 15
-    gate_rows = select_rows(one_hot((target == base + slot) & (slot < 12)), rows)
-    place = base + jnp.where(slot < 8, slot + 16, slot + 4)
-    up_rows = select_rows(one_hot((target == place) & (slot < 12)), rows)
-    left = jnp.concatenate([gate_rows, up_rows], axis=1)
-    sums = jnp.dot(left, weight_ref[...], preferred_element_type=f32)
-    side = received_ref[:, :, width - 128 :].astype(f32)
+    members = received_ref.shape[0]
+    width = 2 * received_ref.shape[2]
+    zeros = jnp.zeros((8, width), f32)
+    upside = iota((8, width), 0) < 4
+    gate_rows, up_rows, side = [], [], []
     first = iota((8, 128), 1) < 64
     is_expert = (iota((8, 128), 1) & 63) == 3 * expert_total + 2
-    expert = expert_ref[0].astype(f32)
+    expert = expert_ref[...].astype(f32)
+    for member in range(members):
+        early, late = unpack_slots(received_ref[member].astype(f32))
+        late = jnp.where(upside, late, 0.0)
+        gate_rows += [early, late, zeros]
+        up_rows += [zeros, pltpu.roll(late, 4, 0), early]
+        turned = pltpu.roll(early[:, width - 128 :], 64, 1)
+        last = jnp.where(first, turned, late[:, width - 128 :])
+        side.append(jnp.where(is_expert, expert, last))
+    left = jnp.concatenate(
+        [jnp.concatenate(gate_rows, axis=0), jnp.concatenate(up_rows, axis=0)], axis=1
+    ).astype(bf16)
+    sums = jnp.dot(left, weight_ref[...], preferred_element_type=f32)
     columns = sums.shape[1] // 128
     for member in range(members):
         tiles = [
@@ -232,10 +292,7 @@
             for row in range(3)
             for col in range(columns)
         ]
-        turned = pltpu.roll(side[member, :8], 64, 1)
-        last = jnp.where(first, turned, side[member, 8:])
-        tiles.append(jnp.where(is_expert, expert, last))
-        out_ref[member] = jnp.concatenate(tiles, axis=0).astype(bf16)
+        out_ref[member] = jnp.concatenate(tiles + [side[member]], axis=0).astype(bf16)
 
 
 def activate_kernel(model_width, expert_total, sums_ref, out_ref):
@@ -277,29 +334,21 @@
     early = activation(block(0), block(2), inverse_rms[:8], weight[:8])
     mixed = block(1)
     late = activation(mixed, pltpu.roll(mixed, 4, 0), inverse_rms[8:], weight[8:])
-    half = early.shape[1] // 2
-    last = jnp.where(
-        iota((8, half), 0) < 4, late[:, :half], pltpu.roll(late[:, half:], 4, 0)
-    )
-    packed = jnp.concatenate([early[:, :half], early[:, half:], last], axis=0).astype(bf16)
+    packed = pack_slots(early, late).astype(bf16)
     for member in range(out_ref.shape[0]):
         out_ref[member] = packed
 
 
 def down_kernel(packed_ref, weight_ref, out_ref):
-    members, height, half = packed_ref.shape
-    rows = packed_ref[...].reshape(members * height, half)
-    shape = (16 * members, members * height)
-    target = iota(shape, 0)
-    source = iota(shape, 1)
-    base = 24 * (target >> 4)
-    slot = target & 15
-    low_place = base + jnp.where(slot < 8, slot, slot + 8)
-    high_place = base + jnp.where(slot < 8, slot + 8, slot + 12)
-    low = select_rows(one_hot((source == low_place) & (slot < 12)), rows)
-    high = select_rows(one_hot((source == high_place) & (slot < 12)), rows)
-    out = dot_nt(jnp.concatenate([low, high], axis=1), weight_ref[...]).astype(bf16)
-    out_ref[...] = out.reshape(out_ref.shape)
+    rows = []
+    for member in range(packed_ref.shape[0]):
+        rows += unpack_slots(packed_ref[member].astype(f32))
+    left = jnp.concatenate(rows, axis=0).astype(bf16)
+    out = pad_lanes(dot_nt(left, weight_ref[...]))
+    for group in range(out_ref.shape[0]):
+        start = 16 * group
+        packed = pack_slots(out[start : start + 8], out[start + 8 : start + 16])
+        out_ref[group] = packed.astype(bf16)
 
 
 def body(
@@ -332,9 +381,12 @@
     expert_total = router.shape[1]
     capacity = max(2, 3 * block_rows // 4)
     pair_rows = sections * block_rows
+    pair_tiles = 8 * (2 * (width_local // 128) + 1)
+    padded_width = width_local + -width_local % 128
     in_smem = pl.BlockSpec(memory_space=pltpu.SMEM)
     vmem = pltpu.CompilerParams(vmem_limit_bytes=32 * 2**20)
 
+    own_section = section.reshape(1, 1)
     place = jnp.stack([section, lengths[0] - section * hist_local]).astype(jnp.int32)
     sent, kept_part = pl.pallas_call(
         attend_kernel,
@@ -342,16 +394,18 @@
             jax.ShapeDtypeStruct((half_heads, latent + 128), bf16),
             jax.ShapeDtypeStruct((half_heads, latent + 128), f32),
         ),
-        in_specs=[in_smem] + [pl.BlockSpec(memory_space=pl.ANY)] * 4 + in_vmem(2),
+        in_specs=[in_smem] + [pl.BlockSpec(memory_space=pltpu.HBM)] * 6,
         out_specs=tuple(in_vmem(2)),
         scratch_shapes=[
+            pltpu.VMEM(routes.shape, jnp.int32),
+            pltpu.VMEM(slots.shape, jnp.int32),
             pltpu.VMEM((head_total, latent), bf16),
             pltpu.VMEM(q_rope.shape, bf16),
             pltpu.VMEM(cache_latent.shape[1:], bf16),
             pltpu.VMEM(cache_rope.shape[1:], bf16),
-            pltpu.SemaphoreType.DMA((4,)),
+            pltpu.SemaphoreType.DMA((6,)),
         ],
-        compiler_params=vmem,
+        compiler_params=pltpu.CompilerParams(vmem_limit_bytes=60 * 2**20),
     )(
         place,
         q_latent[0],
@@ -380,7 +434,6 @@
         kept_part[:, :latent] * factor_mine + theirs[:, :latent].astype(f32) * factor_theirs
     ) / mass_both
     latent_out = latent_out.astype(bf16)
-    tables = both[:, :block_rows, latent:]
 
     outgoing_heads = latent_out.reshape(groups, head_block, latent)
     arrived = lax.all_to_all(outgoing_heads, "grp", split_axis=0, concat_axis=0, tiled=True)
@@ -389,7 +442,7 @@
     gathered = spread(values.reshape(groups, width_heads), "dev")
     partial = pl.pallas_call(
         project_kernel,
-        out_shape=jax.ShapeDtypeStruct((groups, pair_rows, width_local), bf16),
+        out_shape=jax.ShapeDtypeStruct((groups, pair_tiles, 128), bf16),
         in_specs=in_vmem(2),
         out_specs=in_vmem(1)[0],
         compiler_params=vmem,
@@ -397,26 +450,25 @@
     partial = lax.all_to_all(partial, "grp", split_axis=0, concat_axis=0, tiled=True)
     summed = pl.pallas_call(
         block_sum_kernel,
-        out_shape=jax.ShapeDtypeStruct((pair_rows, width_local), f32),
-        in_specs=[in_smem] + in_vmem(2),
+        out_shape=jax.ShapeDtypeStruct((pair_tiles, 128), f32),
+        in_specs=in_vmem(3),
         out_specs=in_vmem(1)[0],
         compiler_params=vmem,
-    )(place, partial, resid)
+    )(own_section, partial, resid)
     summed = lax.all_gather(summed, "sec", axis=0)
 
-    chunk = 16
-    padded_width = width_local + -width_local % 128
+    chunk = 24
     buffer, hidden, placement = pl.pallas_call(
         functools.partial(dispatch_kernel, expert_total, choices, capacity),
         out_shape=(
-            jax.ShapeDtypeStruct((expert_total, chunk, padded_width), bf16),
-            jax.ShapeDtypeStruct((pair_rows, width_local), f32),
-            jax.ShapeDtypeStruct((pair_rows, expert_total * chunk), bf16),
+            jax.ShapeDtypeStruct((expert_total, chunk, padded_width // 2), bf16),
+            jax.ShapeDtypeStruct((pair_rows, padded_width), f32),
+            jax.ShapeDtypeStruct((2 * pair_rows, expert_total * chunk), bf16),
         ),
         in_specs=in_vmem(4),
         out_specs=tuple(in_vmem(3)),
         compiler_params=vmem,
-    )(summed, norm_gain[None], router.T, tables)
+    )(summed, norm_gain[None], router.T, both)
     received = lax.all_to_all(buffer, "grp", split_axis=0, concat_axis=0, tiled=True)
 
     unit = w_gateup.shape[3]
@@ -426,10 +478,10 @@
     sums = pl.pallas_call(
         functools.partial(gate_up_kernel, expert_total),
         out_shape=jax.ShapeDtypeStruct((members, 24 * unit // 128 + 8, 128), bf16),
-        in_specs=[in_smem] + in_vmem(2),
+        in_specs=in_vmem(3),
         out_specs=in_vmem(1)[0],
         compiler_params=vmem,
-    )(lax.axis_index("grp").reshape(1), received, weight)
+    )(lax.axis_index("grp").reshape(1, 1), received, weight)
     sums = lax.all_to_all(sums, "dev", split_axis=0, concat_axis=0, tiled=True)
     packed = pl.pallas_call(
         functools.partial(activate_kernel, width_local * members, expert_total),
@@ -442,22 +494,22 @@
     everyone = lax.all_to_all(packed, "dev", split_axis=0, concat_axis=0, tiled=True)
     down = pl.pallas_call(
         down_kernel,
-        out_shape=jax.ShapeDtypeStruct((groups, chunk, width_local), bf16),
+        out_shape=jax.ShapeDtypeStruct((groups, chunk, padded_width // 2), bf16),
         in_specs=in_vmem(2),
         out_specs=in_vmem(1)[0],
         compiler_params=vmem,
     )(everyone, w_down[0].T)
     returned = lax.all_to_all(down, "grp", split_axis=0, concat_axis=0, tiled=True)
-    returned = returned.reshape(expert_total * chunk, width_local)
+    returned = returned.reshape(expert_total * chunk, padded_width // 2)
     mixture = jnp.dot(placement, returned, preferred_element_type=f32)
     halves = lax.all_gather(mixture, "sec", axis=0)
     return pl.pallas_call(
         last_sum_kernel,
         out_shape=jax.ShapeDtypeStruct((block_rows, width_local), bf16),
-        in_specs=[in_smem] + in_vmem(2),
+        in_specs=in_vmem(3),
         out_specs=in_vmem(1)[0],
         compiler_params=vmem,
-    )(place, halves, hidden)
+    )(own_section, halves, hidden)
 
 
 def solution(mesh):

time: 153 us -> 147 us (0.961)
  blocking collectives: 108 us -> 121 us
  waiting for transfers between devices: 20.5 us -> 9.01 us
  local copies, waits for them, and re-layouts: 5.97 us -> 0.85 us
  starting transfers between devices: 7.06 us -> 3.53 us
  other arithmetic: 0.38 us -> 2.79 us
    all_to_all x0 -> x1, blocking collectives: none -> 13.1 us  [body(): lax.all_to_all(partial, 'grp', split_axis=0, concat_axis=0, tiled=True)]
    all_to_all x1 -> x0, waiting for transfers between devices: 10.5 us -> none  [body(): lax.all_to_all(partial, 'grp', split_axis=0, concat_axis=0, tiled=True)]
    unnamed x27 -> x15, local copies, waits for them, and re-layouts: 5.72 us -> 0.55 us
    all_to_all x1 -> x0, starting transfers between devices: 3.53 us -> none  [body(): lax.all_to_all(partial, 'grp', split_axis=0, concat_axis=0, tiled=True)]
    pallas_call x1, Pallas kernels: 2.25 us -> 4.05 us  [body(): pl.pallas_call(attend_kernel, out_shape=(jax.ShapeDtypeStruct((half_heads...]
  transfers between devices with their start and end apart: 2 -> 1, of which waited for: 2 -> 1; matrix products, arithmetic and copies ran while one was open for 0% -> 1% of each run, Pallas kernels for 0% -> 0%
where the time goes in v5:
time: 147 us; the launch traced here: 146 us
  blocking collectives  121 us (82%)
  waiting for transfers between devices  9.01 us (6%)
  Pallas kernels  8.34 us (6%)
  starting transfers between devices  3.53 us (2%)
  other arithmetic  2.79 us (2%)
    all_to_all x1, blocking collectives, body(): sums = lax.all_to_all(sums, 'dev', split_axis=0, concat_axis=0, tiled=True)  25.9 us
    all_to_all x1, blocking collectives, spread(): return lax.all_to_all(copies, axis, split_axis=0, concat_axis=0, tiled=True)  17.9 us
    all_to_all x1, blocking collectives, body(): lax.all_to_all(packed, 'dev', split_axis=0, concat_axis=0, tiled=True)  15.7 us
    all_to_all x1, blocking collectives, body(): lax.all_to_all(partial, 'grp', split_axis=0, concat_axis=0, tiled=True)  13.1 us
    all_to_all x1, blocking collectives, body(): lax.all_to_all(down, 'grp', split_axis=0, concat_axis=0, tiled=True)  13 us
    all_to_all x1, blocking collectives, body(): lax.all_to_all(outgoing_heads, 'grp', split_axis=0, concat_axis=0, tiled=...  12.7 us
    all_to_all x1, waiting for transfers between devices, body(): lax.all_to_all(buffer, 'grp', split_axis=0, concat_axis=0, tiled=True)  9.01 us
    all_gather x1, blocking collectives, body(): both = lax.all_gather(sent, 'sec', axis=0)  8.66 us
  transfers between devices with their start and end apart: 1, of which 1 were waited for; matrix products, arithmetic and copies ran while one was open for 1% of the time, Pallas kernels for 0%

profile of v5, /device:TPU:1, one launch (start us, length us, event | category | flops | bytes accessed | tf_op | source)
XLA Modules:
  0.0 146.3 jit_solution(653250217486933818)
XLA Ops:
  0.0 0.0 copy-start
  0.7 0.7 pad_add_fusion.place_ref
  1.4 0.0 copy-start.2
  1.4 4.1 %shard_map.136 = (bf16[64,640]{1,0:T(8,128)(2,1)}, f32[64,640]{1,0:T(8,128)}) custom-call(s32[2]{0:T(128)} %pad_add_fusion.place_ref, bf16[128,512]{1,0:T(8,128)(2,1)} %bitcast.46, bf16[1,8192]{1,0:T(2,128)(2,1)} %rope_hbm.1, bf16[1024,512]{1,0:T(8,128)(2,1)} %bitcast.44, bf16[64,1024]{1,0:T(8,128)(2,1)} %bitcast.47, s32[8,8]{1,0:T(8,128)} %routes_hbm.1, ...), custom_call_target="tpu_custom_call" | custom-call | tf_op jit(solution)/shard_map/pallas_call | solution.py:391
  5.4 8.7 %all-gather = bf16[128,640]{1,0:T(8,128)(2,1)S(1)} all-gather(bf16[64,640]{1,0:T(8,128)(2,1)} %get-tuple-element.11), channel_id=2, replica_groups=mesh['sec'=2,'grp'=16,'dev'=16] {'sec'}, dimensions={0}, use_global_device_ids=true | all-gather | bytes 245760 | tf_op jit(solution)/shard_map/all_gather | solution.py:420
  14.1 0.0 copy-start.4
  14.1 1.1 fusion.5
  15.2 0.0 copy-start.3
  15.2 0.0 copy-start.5
  15.3 1.0 divide_convert_fusion
  16.3 12.7 %all_to_all.35 = bf16[16,4,512]{2,1,0:T(4,128)(2,1)S(1)} all-to-all(bf16[16,4,512]{2,1,0:T(4,128)(2,1)S(1)} %reshape.17), channel_id=1, replica_groups=mesh['sec'=2,'grp'=16,'dev'=16] {'grp'}, dimensions={0} | all-to-all | bytes 131072 | tf_op jit(solution)/shard_map/all_to_all | solution.py:439
  29.0 0.0 copy-done
  29.0 0.0 copy-start.6
  29.0 0.2 fusion
  29.3 17.9 %all_to_all.36.gathered_ref = bf16[16,16,512]{2,1,0:T(8,128)(2,1)S(1)} all-to-all(bf16[16,16,512]{2,1,0:T(8,128)(2,1)S(1)} %broadcast_in_dim.11), channel_id=1, replica_groups=mesh['sec'=2,'grp'=16,'dev'=16] {'dev'}, dimensions={0} | all-to-all | bytes 524288 | tf_op jit(solution)/shard_map/all_to_all | solution.py:20
  47.1 0.0 copy-done.2
  47.1 0.5 shard_map.137
  47.6 13.1 %all_to_all.37.partial_ref = bf16[16,56,128]{2,1,0:T(8,128)(2,1)S(1)} all-to-all(bf16[16,56,128]{2,1,0:T(8,128)(2,1)S(1)} %shard_map.137), channel_id=1, replica_groups=mesh['sec'=2,'grp'=16,'dev'=16] {'grp'}, dimensions={0} | all-to-all | bytes 458752 | tf_op jit(solution)/shard_map/all_to_all | solution.py:450
  60.7 0.0 copy-done.4
  60.7 0.1 shard_map.138
  60.9 6.3 %all-gather.1 = f32[112,128]{1,0:T(8,128)S(1)} all-gather(f32[56,128]{1,0:T(8,128)S(1)} %shard_map.138), channel_id=3, replica_groups=mesh['sec'=2,'grp'=16,'dev'=16] {'sec'}, dimensions={0}, use_global_device_ids=true | all-gather | bytes 86016 | tf_op jit(solution)/shard_map/all_gather | solution.py:458
  67.1 0.0 copy-done.3
  67.1 0.0 copy-done.5
  67.1 1.2 shard_map.139
  68.3 3.5 %all-to-all-start.3 = ((bf16[16,24,256]{2,1,0:T(8,128)(2,1)}), bf16[16,24,256]{2,1,0:T(8,128)(2,1)S(1)}, u32[]{:S(2)}, u32[]{:S(2)}) async-start(bf16[16,24,256]{2,1,0:T(8,128)(2,1)} %get-tuple-element.13), calls=%async_computation.3 | async-start | bytes 393216 | tf_op jit(solution)/shard_map/all_to_all | solution.py:472
  71.9 0.0 copy-done.6
  71.9 0.5 copy.23
  72.4 0.2 pad.4.clone
  72.6 9.0 %all-to-all-done.3.received_ref = bf16[16,24,256]{2,1,0:T(8,128)(2,1)S(1)} async-done(((bf16[16,24,256]{2,1,0:T(8,128)(2,1)}), bf16[16,24,256]{2,1,0:T(8,128)(2,1)S(1)}, u32[]{:S(2)}, u32[]{:S(2)}) %all-to-all-start.3) | async-done | bytes 196640 | tf_op jit(solution)/shard_map/all_to_all | solution.py:472
  81.7 1.0 shard_map.140
  82.6 0.0 copy-start.1
  82.7 25.9 %all_to_all.38.sums_ref = bf16[16,200,128]{2,1,0:T(8,128)(2,1)S(1)} all-to-all(bf16[16,200,128]{2,1,0:T(8,128)(2,1)S(1)} %shard_map.140), channel_id=1, replica_groups=mesh['sec'=2,'grp'=16,'dev'=16] {'dev'}, dimensions={0} | all-to-all | bytes 1638400 | tf_op jit(solution)/shard_map/all_to_all | solution.py:485
  108.6 0.3 shard_map.141
  108.9 15.7 %all_to_all.39.packed_ref = bf16[16,24,512]{2,1,0:T(8,128)(2,1)S(1)} all-to-all(bf16[16,24,512]{2,1,0:T(8,128)(2,1)S(1)} %shard_map.141), channel_id=1, replica_groups=mesh['sec'=2,'grp'=16,'dev'=16] {'dev'}, dimensions={0} | all-to-all | bytes 786432 | tf_op jit(solution)/shard_map/all_to_all | solution.py:494
  124.6 0.0 copy-done.1
  124.6 0.5 shard_map.142
  125.0 13.0 %all_to_all.40 = bf16[16,24,256]{2,1,0:T(8,128)(2,1)S(1)} all-to-all(bf16[16,24,256]{2,1,0:T(8,128)(2,1)S(1)} %shard_map.142), channel_id=1, replica_groups=mesh['sec'=2,'grp'=16,'dev'=16] {'grp'}, dimensions={0} | all-to-all | bytes 393216 | tf_op jit(solution)/shard_map/all_to_all | solution.py:502
  138.1 0.1 fusion.6
  138.2 7.4 %all-gather.2 = f32[64,256]{1,0:T(8,128)S(1)} all-gather(f32[32,256]{1,0:T(8,128)S(1)} %fusion.6), channel_id=4, replica_groups=mesh['sec'=2,'grp'=16,'dev'=16] {'sec'}, dimensions={0}, use_global_device_ids=true | all-gather | bytes 98304 | tf_op jit(solution)/shard_map/all_gather | solution.py:505
  145.6 0.7 shard_map.143
  (4 shorter events, 0.1 us)
Async XLA Ops:
  0.0 29.0 %copy-start = (bf16[4,512,128]{2,1,0:T(8,128)(2,1)S(1)}, bf16[4,512,128]{2,1,0:T(8,128)(2,1)}, u32[]{:S(2)}) copy-start(bf16[4,512,128]{2,1,0:T(8,128)(2,1)} %param.19) | copy-start | bytes 1572868
  1.4 45.8 %copy-start.2 = (bf16[512,448]{0,1:T(8,128)(2,1)S(1)}, bf16[512,448]{0,1:T(8,128)(2,1)}, u32[]{:S(2)}) copy-start(bf16[512,448]{0,1:T(8,128)(2,1)} %param.20) | copy-start | bytes 1376260
  14.1 46.6 %copy-start.4 = (bf16[8,448]{1,0:T(8,128)(2,1)S(1)}, bf16[8,448]{1,0:T(8,128)(2,1)}, u32[]{:S(2)}) copy-start(bf16[8,448]{1,0:T(8,128)(2,1)} %resid_ref.1) | copy-start | bytes 21508
  15.2 51.9 %copy-start.3 = (f32[448,16]{0,1:T(8,128)S(1)}, f32[448,16]{0,1:T(8,128)}, u32[]{:S(2)}) copy-start(f32[448,16]{0,1:T(8,128)} %param.23) | copy-start | bytes 86020
  15.2 51.9 %copy-start.5 = (f32[448]{0:T(512)S(1)}, f32[448]{0:T(512)}, u32[]{:S(2)}) copy-start(f32[448]{0:T(512)} %param.22) | copy-start | bytes 5380
  29.0 42.8 %copy-start.6 = (bf16[1,448,2,1024]{3,2,1,0:T(2,128)(2,1)S(1)}, bf16[1,448,2,1024]{3,2,1,0:T(2,128)(2,1)}, u32[]{:S(2)}) copy-start(bf16[1,448,2,1024]{3,2,1,0:T(2,128)(2,1)} %param.26) | copy-start | bytes 5505028
  68.3 13.3 %all-to-all-start.3 = ((bf16[16,24,256]{2,1,0:T(8,128)(2,1)}), bf16[16,24,256]{2,1,0:T(8,128)(2,1)S(1)}, u32[]{:S(2)}, u32[]{:S(2)}) async-start(bf16[16,24,256]{2,1,0:T(8,128)(2,1)} %get-tuple-element.13), calls=%async_computation.3 | async-start | bytes 393216 | tf_op jit(solution)/shard_map/all_to_all | solution.py:472
  82.6 41.9 %copy-start.1 = (bf16[1,1024,448]{1,2,0:T(8,128)(2,1)S(1)}, bf16[1,1024,448]{1,2,0:T(8,128)(2,1)}, u32[]{:S(2)}) copy-start(bf16[1,1024,448]{1,2,0:T(8,128)(2,1)} %param.27) | copy-start | bytes 2752516

commit v6 on v5

--- a/solution.py
+++ b/solution.py
@@ -405,15 +405,13 @@
             pltpu.VMEM(cache_rope.shape[1:], bf16),
             pltpu.SemaphoreType.DMA((6,)),
         ],
-        compiler_params=pltpu.CompilerParams(vmem_limit_bytes=60 * 2**20),
+        compiler_params=vmem,
     )(
         place,
-        q_latent[0],
-        q_rope,
-        cache_latent[0],
-        cache_rope[0],
-        routes,
-        slots,
+        *[
+            pltpu.with_memory_space_constraint(operand, pltpu.HBM)
+            for operand in (q_latent[0], q_rope, cache_latent[0], cache_rope[0], routes, slots)
+        ],
     )
 
     other = 1 - section

time: 147 us -> 143 us (0.973)
  other arithmetic: 2.79 us -> 0.37 us
where the time goes in v6:
time: 143 us
  blocking collectives  120 us (84%)
  waiting for transfers between devices  9.03 us (6%)
  Pallas kernels  7.43 us (5%)
  starting transfers between devices  3.53 us (2%)
    all_to_all x1, blocking collectives, body(): sums = lax.all_to_all(sums, 'dev', split_axis=0, concat_axis=0, tiled=True)  25.9 us
    all_to_all x1, blocking collectives, spread(): return lax.all_to_all(copies, axis, split_axis=0, concat_axis=0, tiled=True)  17.9 us
    all_to_all x1, blocking collectives, body(): lax.all_to_all(packed, 'dev', split_axis=0, concat_axis=0, tiled=True)  15.7 us
    all_to_all x1, blocking collectives, body(): lax.all_to_all(partial, 'grp', split_axis=0, concat_axis=0, tiled=True)  13.1 us
    all_to_all x1, blocking collectives, body(): lax.all_to_all(down, 'grp', split_axis=0, concat_axis=0, tiled=True)  13 us
    all_to_all x1, blocking collectives, body(): lax.all_to_all(outgoing_heads, 'grp', split_axis=0, concat_axis=0, tiled=...  12.7 us
    all_to_all x1, waiting for transfers between devices, body(): lax.all_to_all(buffer, 'grp', split_axis=0, concat_axis=0, tiled=True)  9.03 us
    all_gather x1, blocking collectives, body(): both = lax.all_gather(sent, 'sec', axis=0)  8.45 us
  transfers between devices with their start and end apart: 1, of which 1 were waited for; matrix products, arithmetic and copies ran while one was open for 1% of the time, Pallas kernels for 0%

profile of v6, /device:TPU:1, one launch (start us, length us, event | category | flops | bytes accessed | tf_op | source)
XLA Modules:
  0.0 142.8 jit_solution(2153486657499377157)
XLA Ops:
  0.0 0.0 copy-start
  0.7 0.1 pad_add_fusion.place_ref
  0.8 0.0 copy-start.2
  0.8 3.1 %shard_map.136 = (bf16[64,640]{1,0:T(8,128)(2,1)S(1)}, f32[64,640]{1,0:T(8,128)S(1)}) custom-call(s32[2]{0:T(128)S(1)} %pad_add_fusion.place_ref, bf16[128,512]{1,0:T(8,128)(2,1)} %bitcast.46, bf16[1,8192]{1,0:T(2,128)(2,1)} %rope_hbm.1, bf16[1024,512]{1,0:T(8,128)(2,1)} %bitcast.44, bf16[64,1024]{1,0:T(8,128)(2,1)} %bitcast.47, s32[8,8]{1,0:T(8,128)} %routes_hbm.1, ...), custom_call_target="tpu_custom_call" | custom-call | tf_op jit(solution)/shard_map/pallas_call | solution.py:391
  3.9 8.4 %all-gather = bf16[128,640]{1,0:T(8,128)(2,1)S(1)} all-gather(bf16[64,640]{1,0:T(8,128)(2,1)S(1)} %get-tuple-element.11), channel_id=2, replica_groups=mesh['sec'=2,'grp'=16,'dev'=16] {'sec'}, dimensions={0}, use_global_device_ids=true | all-gather | bytes 245760 | tf_op jit(solution)/shard_map/all_gather | solution.py:418
  12.4 0.0 copy-start.4
  12.4 0.2 fusion.5
  12.6 0.0 copy-start.3
  12.6 0.0 copy-start.5
  12.6 0.1 divide_convert_fusion
  12.8 12.7 %all_to_all.35 = bf16[16,4,512]{2,1,0:T(4,128)(2,1)S(1)} all-to-all(bf16[16,4,512]{2,1,0:T(4,128)(2,1)S(1)} %reshape.17), channel_id=1, replica_groups=mesh['sec'=2,'grp'=16,'dev'=16] {'grp'}, dimensions={0} | all-to-all | bytes 131072 | tf_op jit(solution)/shard_map/all_to_all | solution.py:437
  25.5 0.0 copy-done
  25.5 0.0 copy-start.6
  25.5 0.2 fusion
  25.7 17.9 %all_to_all.36.gathered_ref = bf16[16,16,512]{2,1,0:T(8,128)(2,1)S(1)} all-to-all(bf16[16,16,512]{2,1,0:T(8,128)(2,1)S(1)} %broadcast_in_dim.11), channel_id=1, replica_groups=mesh['sec'=2,'grp'=16,'dev'=16] {'dev'}, dimensions={0} | all-to-all | bytes 524288 | tf_op jit(solution)/shard_map/all_to_all | solution.py:20
  43.6 0.0 copy-done.2
  43.6 0.5 shard_map.137
  44.1 13.1 %all_to_all.37.partial_ref = bf16[16,56,128]{2,1,0:T(8,128)(2,1)S(1)} all-to-all(bf16[16,56,128]{2,1,0:T(8,128)(2,1)S(1)} %shard_map.137), channel_id=1, replica_groups=mesh['sec'=2,'grp'=16,'dev'=16] {'grp'}, dimensions={0} | all-to-all | bytes 458752 | tf_op jit(solution)/shard_map/all_to_all | solution.py:448
  57.2 0.0 copy-done.4
  57.2 0.1 shard_map.138
  57.3 6.2 %all-gather.1 = f32[112,128]{1,0:T(8,128)S(1)} all-gather(f32[56,128]{1,0:T(8,128)S(1)} %shard_map.138), channel_id=3, replica_groups=mesh['sec'=2,'grp'=16,'dev'=16] {'sec'}, dimensions={0}, use_global_device_ids=true | all-gather | bytes 86016 | tf_op jit(solution)/shard_map/all_gather | solution.py:456
  63.6 0.0 copy-done.3
  63.6 0.0 copy-done.5
  63.6 1.2 shard_map.139
  64.8 3.5 %all-to-all-start.3 = ((bf16[16,24,256]{2,1,0:T(8,128)(2,1)}), bf16[16,24,256]{2,1,0:T(8,128)(2,1)S(1)}, u32[]{:S(2)}, u32[]{:S(2)}) async-start(bf16[16,24,256]{2,1,0:T(8,128)(2,1)} %get-tuple-element.13), calls=%async_computation.3 | async-start | bytes 393216 | tf_op jit(solution)/shard_map/all_to_all | solution.py:470
  68.3 0.0 copy-done.6
  68.3 0.5 copy.23
  68.9 0.2 pad.4.clone
  69.1 9.0 %all-to-all-done.3.received_ref = bf16[16,24,256]{2,1,0:T(8,128)(2,1)S(1)} async-done(((bf16[16,24,256]{2,1,0:T(8,128)(2,1)}), bf16[16,24,256]{2,1,0:T(8,128)(2,1)S(1)}, u32[]{:S(2)}, u32[]{:S(2)}) %all-to-all-start.3) | async-done | bytes 196640 | tf_op jit(solution)/shard_map/all_to_all | solution.py:470
  78.1 1.0 shard_map.140
  79.1 0.0 copy-start.1
  79.1 25.9 %all_to_all.38.sums_ref = bf16[16,200,128]{2,1,0:T(8,128)(2,1)S(1)} all-to-all(bf16[16,200,128]{2,1,0:T(8,128)(2,1)S(1)} %shard_map.140), channel_id=1, replica_groups=mesh['sec'=2,'grp'=16,'dev'=16] {'dev'}, dimensions={0} | all-to-all | bytes 1638400 | tf_op jit(solution)/shard_map/all_to_all | solution.py:483
  105.1 0.3 shard_map.141
  105.4 15.7 %all_to_all.39.packed_ref = bf16[16,24,512]{2,1,0:T(8,128)(2,1)S(1)} all-to-all(bf16[16,24,512]{2,1,0:T(8,128)(2,1)S(1)} %shard_map.141), channel_id=1, replica_groups=mesh['sec'=2,'grp'=16,'dev'=16] {'dev'}, dimensions={0} | all-to-all | bytes 786432 | tf_op jit(solution)/shard_map/all_to_all | solution.py:492
  121.0 0.0 copy-done.1
  121.1 0.5 shard_map.142
  121.5 13.0 %all_to_all.40 = bf16[16,24,256]{2,1,0:T(8,128)(2,1)S(1)} all-to-all(bf16[16,24,256]{2,1,0:T(8,128)(2,1)S(1)} %shard_map.142), channel_id=1, replica_groups=mesh['sec'=2,'grp'=16,'dev'=16] {'grp'}, dimensions={0} | all-to-all | bytes 393216 | tf_op jit(solution)/shard_map/all_to_all | solution.py:500
  134.5 0.1 fusion.6
  134.7 7.4 %all-gather.2 = f32[64,256]{1,0:T(8,128)S(1)} all-gather(f32[32,256]{1,0:T(8,128)S(1)} %fusion.6), channel_id=4, replica_groups=mesh['sec'=2,'grp'=16,'dev'=16] {'sec'}, dimensions={0}, use_global_device_ids=true | all-gather | bytes 98304 | tf_op jit(solution)/shard_map/all_gather | solution.py:503
  142.1 0.7 shard_map.143
  (4 shorter events, 0.1 us)
Async XLA Ops:
  0.0 25.5 %copy-start = (bf16[4,512,128]{2,1,0:T(8,128)(2,1)S(1)}, bf16[4,512,128]{2,1,0:T(8,128)(2,1)}, u32[]{:S(2)}) copy-start(bf16[4,512,128]{2,1,0:T(8,128)(2,1)} %param.19) | copy-start | bytes 1572868
  0.8 42.8 %copy-start.2 = (bf16[512,448]{0,1:T(8,128)(2,1)S(1)}, bf16[512,448]{0,1:T(8,128)(2,1)}, u32[]{:S(2)}) copy-start(bf16[512,448]{0,1:T(8,128)(2,1)} %param.20) | copy-start | bytes 1376260
  12.4 44.8 %copy-start.4 = (bf16[8,448]{1,0:T(8,128)(2,1)S(1)}, bf16[8,448]{1,0:T(8,128)(2,1)}, u32[]{:S(2)}) copy-start(bf16[8,448]{1,0:T(8,128)(2,1)} %resid_ref.1) | copy-start | bytes 21508
  12.6 51.0 %copy-start.3 = (f32[448,16]{0,1:T(8,128)S(1)}, f32[448,16]{0,1:T(8,128)}, u32[]{:S(2)}) copy-start(f32[448,16]{0,1:T(8,128)} %param.23) | copy-start | bytes 86020
  12.6 50.9 %copy-start.5 = (f32[448]{0:T(512)S(1)}, f32[448]{0:T(512)}, u32[]{:S(2)}) copy-start(f32[448]{0:T(512)} %param.22) | copy-start | bytes 5380
  25.5 42.8 %copy-start.6 = (bf16[1,448,2,1024]{3,2,1,0:T(2,128)(2,1)S(1)}, bf16[1,448,2,1024]{3,2,1,0:T(2,128)(2,1)}, u32[]{:S(2)}) copy-start(bf16[1,448,2,1024]{3,2,1,0:T(2,128)(2,1)} %param.26) | copy-start | bytes 5505028
  64.8 13.4 %all-to-all-start.3 = ((bf16[16,24,256]{2,1,0:T(8,128)(2,1)}), bf16[16,24,256]{2,1,0:T(8,128)(2,1)S(1)}, u32[]{:S(2)}, u32[]{:S(2)}) async-start(bf16[16,24,256]{2,1,0:T(8,128)(2,1)} %get-tuple-element.13), calls=%async_computation.3 | async-start | bytes 393216 | tf_op jit(solution)/shard_map/all_to_all | solution.py:470
  79.1 41.9 %copy-start.1 = (bf16[1,1024,448]{1,2,0:T(8,128)(2,1)S(1)}, bf16[1,1024,448]{1,2,0:T(8,128)(2,1)}, u32[]{:S(2)}) copy-start(bf16[1,1024,448]{1,2,0:T(8,128)(2,1)} %param.27) | copy-start | bytes 2752516

commit v7 on v6

--- a/solution.py
+++ b/solution.py
@@ -96,6 +96,9 @@
     cache_rope_ref,
     sems,
 ):
+    positions = cache_ref.shape[0]
+    step = positions // 4
+    blocks = [pl.ds(step * index, step) for index in range(4)]
     copies = [
         pltpu.make_async_copy(source, target, sems.at[index])
         for index, (source, target) in enumerate(
@@ -103,16 +106,16 @@
                 (rope_hbm, rope_ref),
                 (cache_rope_hbm, cache_rope_ref),
                 (latent_hbm, latent_ref),
-                (cache_hbm, cache_ref),
                 (routes_hbm, routes_ref),
                 (slots_hbm, slots_ref),
             ]
+            + [(cache_hbm.at[block], cache_ref.at[block]) for block in blocks]
         )
     ]
     for copy in copies:
         copy.start()
+    copies[3].wait()
     copies[4].wait()
-    copies[5].wait()
     heads, latent = latent_ref.shape
     half = heads // 2
     width = cache_rope_ref.shape[0]
@@ -145,15 +148,17 @@
     )
     copies[2].wait()
     query = jnp.concatenate([latent_ref[pl.ds(other, half), :], latent_ref[pl.ds(mine, half), :]], axis=0)
-    copies[3].wait()
-    cache = cache_ref[...]
-    scores = dot_nt(query, cache) + rope_scores
+    parts = []
+    for index, block in enumerate(blocks):
+        copies[5 + index].wait()
+        parts.append(dot_nt(query, cache_ref[block, :]))
+    scores = jnp.concatenate(parts, axis=1) + rope_scores
     usable = iota(scores.shape, 1) < place_ref[1]
     masked = jnp.where(usable, scores * score_scale, masked_floor)
     top = jnp.max(masked, axis=1, keepdims=True).astype(bf16).astype(f32)
     expon = jnp.where(usable, jnp.exp(masked - top), 0.0)
     mass = jnp.sum(expon, axis=1, keepdims=True)
-    weighted = jnp.dot(expon.astype(bf16), cache, preferred_element_type=f32)
+    weighted = jnp.dot(expon.astype(bf16), cache_ref[...], preferred_element_type=f32)
     mass_high = mass.astype(bf16).astype(f32)
     lane = iota((heads, 128), 1)
     side = jnp.where(lane == 0, top, 0.0)
@@ -267,31 +272,32 @@
 def gate_up_kernel(expert_total, expert_ref, received_ref, weight_ref, out_ref):
     members = received_ref.shape[0]
     width = 2 * received_ref.shape[2]
-    zeros = jnp.zeros((8, width), f32)
     upside = iota((8, width), 0) < 4
-    gate_rows, up_rows, side = [], [], []
+    rows, side = [], []
     first = iota((8, 128), 1) < 64
     is_expert = (iota((8, 128), 1) & 63) == 3 * expert_total + 2
     expert = expert_ref[...].astype(f32)
     for member in range(members):
         early, late = unpack_slots(received_ref[member].astype(f32))
         late = jnp.where(upside, late, 0.0)
-        gate_rows += [early, late, zeros]
-        up_rows += [zeros, pltpu.roll(late, 4, 0), early]
+        rows += [early, late]
         turned = pltpu.roll(early[:, width - 128 :], 64, 1)
         last = jnp.where(first, turned, late[:, width - 128 :])
         side.append(jnp.where(is_expert, expert, last))
-    left = jnp.concatenate(
-        [jnp.concatenate(gate_rows, axis=0), jnp.concatenate(up_rows, axis=0)], axis=1
-    ).astype(bf16)
-    sums = jnp.dot(left, weight_ref[...], preferred_element_type=f32)
-    columns = sums.shape[1] // 128
+    left = jnp.concatenate(rows, axis=0).astype(bf16)
+    gate = jnp.dot(left, weight_ref[:width, :], preferred_element_type=f32)
+    up = jnp.dot(left, weight_ref[width:, :], preferred_element_type=f32)
+    unit = gate.shape[1]
+    over = iota((8, unit), 0) < 4
     for member in range(members):
-        tiles = [
-            sums[24 * member + 8 * row : 24 * member + 8 * row + 8, 128 * col : 128 * col + 128]
-            for row in range(3)
-            for col in range(columns)
+        start = 16 * member
+        late_up = pltpu.roll(up[start + 8 : start + 16], 4, 0)
+        blocks = [
+            gate[start : start + 8],
+            jnp.where(over, gate[start + 8 : start + 16], late_up),
+            up[start : start + 8],
         ]
+        tiles = [block[:, at : at + 128] for block in blocks for at in range(0, unit, 128)]
         out_ref[member] = jnp.concatenate(tiles + [side[member]], axis=0).astype(bf16)
 
 
@@ -403,7 +409,7 @@
             pltpu.VMEM(q_rope.shape, bf16),
             pltpu.VMEM(cache_latent.shape[1:], bf16),
             pltpu.VMEM(cache_rope.shape[1:], bf16),
-            pltpu.SemaphoreType.DMA((6,)),
+            pltpu.SemaphoreType.DMA((9,)),
         ],
         compiler_params=vmem,
     )(

time: 143 us -> 143 us (level)
  no operation moved by 1% of the time
where the time goes in v7:
time: 143 us
  blocking collectives  120 us (84%)
  waiting for transfers between devices  9.01 us (6%)
  Pallas kernels  7.37 us (5%)
  starting transfers between devices  3.53 us (2%)
    all_to_all x1, blocking collectives, body(): sums = lax.all_to_all(sums, 'dev', split_axis=0, concat_axis=0, tiled=True)  25.9 us
    all_to_all x1, blocking collectives, spread(): return lax.all_to_all(copies, axis, split_axis=0, concat_axis=0, tiled=True)  17.9 us
    all_to_all x1, blocking collectives, body(): lax.all_to_all(packed, 'dev', split_axis=0, concat_axis=0, tiled=True)  15.7 us
    all_to_all x1, blocking collectives, body(): lax.all_to_all(partial, 'grp', split_axis=0, concat_axis=0, tiled=True)  13.1 us
    all_to_all x1, blocking collectives, body(): lax.all_to_all(down, 'grp', split_axis=0, concat_axis=0, tiled=True)  13 us
    all_to_all x1, blocking collectives, body(): lax.all_to_all(outgoing_heads, 'grp', split_axis=0, concat_axis=0, tiled=...  12.8 us
    all_to_all x1, waiting for transfers between devices, body(): lax.all_to_all(buffer, 'grp', split_axis=0, concat_axis=0, tiled=True)  9.01 us
    all_gather x1, blocking collectives, body(): both = lax.all_gather(sent, 'sec', axis=0)  8.45 us
  transfers between devices with their start and end apart: 1, of which 1 were waited for; matrix products, arithmetic and copies ran while one was open for 1% of the time, Pallas kernels for 0%

profile of v7, /device:TPU:1, one launch (start us, length us, event | category | flops | bytes accessed | tf_op | source)
XLA Modules:
  0.0 142.7 jit_solution(13165886820001721560)
XLA Ops:
  0.0 0.0 copy-start
  0.7 0.1 pad_add_fusion.place_ref
  0.8 0.0 copy-start.2
  0.8 3.4 %shard_map.136 = (bf16[64,640]{1,0:T(8,128)(2,1)S(1)}, f32[64,640]{1,0:T(8,128)S(1)}) custom-call(s32[2]{0:T(128)S(1)} %pad_add_fusion.place_ref, bf16[128,512]{1,0:T(8,128)(2,1)} %bitcast.46, bf16[1,8192]{1,0:T(2,128)(2,1)} %rope_hbm.1, bf16[1024,512]{1,0:T(8,128)(2,1)} %bitcast.44, bf16[64,1024]{1,0:T(8,128)(2,1)} %bitcast.47, s32[8,8]{1,0:T(8,128)} %routes_hbm.1, ...), custom_call_target="tpu_custom_call" | custom-call | tf_op jit(solution)/shard_map/pallas_call | solution.py:397
  4.2 8.4 %all-gather = bf16[128,640]{1,0:T(8,128)(2,1)S(1)} all-gather(bf16[64,640]{1,0:T(8,128)(2,1)S(1)} %get-tuple-element.11), channel_id=2, replica_groups=mesh['sec'=2,'grp'=16,'dev'=16] {'sec'}, dimensions={0}, use_global_device_ids=true | all-gather | bytes 245760 | tf_op jit(solution)/shard_map/all_gather | solution.py:424
  12.6 0.0 copy-start.4
  12.6 0.2 fusion.5
  12.8 0.0 copy-start.3
  12.8 0.0 copy-start.5
  12.8 0.1 divide_convert_fusion
  13.0 12.8 %all_to_all.35 = bf16[16,4,512]{2,1,0:T(4,128)(2,1)S(1)} all-to-all(bf16[16,4,512]{2,1,0:T(4,128)(2,1)S(1)} %reshape.17), channel_id=1, replica_groups=mesh['sec'=2,'grp'=16,'dev'=16] {'grp'}, dimensions={0} | all-to-all | bytes 131072 | tf_op jit(solution)/shard_map/all_to_all | solution.py:443
  25.7 0.0 copy-done
  25.7 0.0 copy-start.6
  25.7 0.2 fusion
  26.0 17.9 %all_to_all.36.gathered_ref = bf16[16,16,512]{2,1,0:T(8,128)(2,1)S(1)} all-to-all(bf16[16,16,512]{2,1,0:T(8,128)(2,1)S(1)} %broadcast_in_dim.11), channel_id=1, replica_groups=mesh['sec'=2,'grp'=16,'dev'=16] {'dev'}, dimensions={0} | all-to-all | bytes 524288 | tf_op jit(solution)/shard_map/all_to_all | solution.py:20
  43.8 0.0 copy-done.2
  43.8 0.5 shard_map.137
  44.3 13.1 %all_to_all.37.partial_ref = bf16[16,56,128]{2,1,0:T(8,128)(2,1)S(1)} all-to-all(bf16[16,56,128]{2,1,0:T(8,128)(2,1)S(1)} %shard_map.137), channel_id=1, replica_groups=mesh['sec'=2,'grp'=16,'dev'=16] {'grp'}, dimensions={0} | all-to-all | bytes 458752 | tf_op jit(solution)/shard_map/all_to_all | solution.py:454
  57.4 0.0 copy-done.4
  57.4 0.1 shard_map.138
  57.5 6.2 %all-gather.1 = f32[112,128]{1,0:T(8,128)S(1)} all-gather(f32[56,128]{1,0:T(8,128)S(1)} %shard_map.138), channel_id=3, replica_groups=mesh['sec'=2,'grp'=16,'dev'=16] {'sec'}, dimensions={0}, use_global_device_ids=true | all-gather | bytes 86016 | tf_op jit(solution)/shard_map/all_gather | solution.py:462
  63.8 0.0 copy-done.3
  63.8 0.0 copy-done.5
  63.8 1.2 shard_map.139
  65.0 3.5 %all-to-all-start.3 = ((bf16[16,24,256]{2,1,0:T(8,128)(2,1)}), bf16[16,24,256]{2,1,0:T(8,128)(2,1)S(1)}, u32[]{:S(2)}, u32[]{:S(2)}) async-start(bf16[16,24,256]{2,1,0:T(8,128)(2,1)} %get-tuple-element.13), calls=%async_computation.3 | async-start | bytes 393216 | tf_op jit(solution)/shard_map/all_to_all | solution.py:476
  68.5 0.0 copy-done.6
  68.5 0.5 copy.23
  69.1 0.2 pad.4.clone
  69.3 9.0 %all-to-all-done.3.received_ref = bf16[16,24,256]{2,1,0:T(8,128)(2,1)S(1)} async-done(((bf16[16,24,256]{2,1,0:T(8,128)(2,1)}), bf16[16,24,256]{2,1,0:T(8,128)(2,1)S(1)}, u32[]{:S(2)}, u32[]{:S(2)}) %all-to-all-start.3) | async-done | bytes 196640 | tf_op jit(solution)/shard_map/all_to_all | solution.py:476
  78.3 0.7 shard_map.140
  79.0 0.0 copy-start.1
  79.1 25.9 %all_to_all.38.sums_ref = bf16[16,200,128]{2,1,0:T(8,128)(2,1)S(1)} all-to-all(bf16[16,200,128]{2,1,0:T(8,128)(2,1)S(1)} %shard_map.140), channel_id=1, replica_groups=mesh['sec'=2,'grp'=16,'dev'=16] {'dev'}, dimensions={0} | all-to-all | bytes 1638400 | tf_op jit(solution)/shard_map/all_to_all | solution.py:489
  105.0 0.3 shard_map.141
  105.3 15.7 %all_to_all.39.packed_ref = bf16[16,24,512]{2,1,0:T(8,128)(2,1)S(1)} all-to-all(bf16[16,24,512]{2,1,0:T(8,128)(2,1)S(1)} %shard_map.141), channel_id=1, replica_groups=mesh['sec'=2,'grp'=16,'dev'=16] {'dev'}, dimensions={0} | all-to-all | bytes 786432 | tf_op jit(solution)/shard_map/all_to_all | solution.py:498
  121.0 0.0 copy-done.1
  121.0 0.5 shard_map.142
  121.4 13.0 %all_to_all.40 = bf16[16,24,256]{2,1,0:T(8,128)(2,1)S(1)} all-to-all(bf16[16,24,256]{2,1,0:T(8,128)(2,1)S(1)} %shard_map.142), channel_id=1, replica_groups=mesh['sec'=2,'grp'=16,'dev'=16] {'grp'}, dimensions={0} | all-to-all | bytes 393216 | tf_op jit(solution)/shard_map/all_to_all | solution.py:506
  134.4 0.1 fusion.6
  134.6 7.4 %all-gather.2 = f32[64,256]{1,0:T(8,128)S(1)} all-gather(f32[32,256]{1,0:T(8,128)S(1)} %fusion.6), channel_id=4, replica_groups=mesh['sec'=2,'grp'=16,'dev'=16] {'sec'}, dimensions={0}, use_global_device_ids=true | all-gather | bytes 98304 | tf_op jit(solution)/shard_map/all_gather | solution.py:509
  142.0 0.7 shard_map.143
  (4 shorter events, 0.1 us)
Async XLA Ops:
  0.0 25.7 %copy-start = (bf16[4,512,128]{2,1,0:T(8,128)(2,1)S(1)}, bf16[4,512,128]{2,1,0:T(8,128)(2,1)}, u32[]{:S(2)}) copy-start(bf16[4,512,128]{2,1,0:T(8,128)(2,1)} %param.19) | copy-start | bytes 1572868
  0.8 43.0 %copy-start.2 = (bf16[512,448]{0,1:T(8,128)(2,1)S(1)}, bf16[512,448]{0,1:T(8,128)(2,1)}, u32[]{:S(2)}) copy-start(bf16[512,448]{0,1:T(8,128)(2,1)} %param.20) | copy-start | bytes 1376260
  12.6 44.8 %copy-start.4 = (bf16[8,448]{1,0:T(8,128)(2,1)S(1)}, bf16[8,448]{1,0:T(8,128)(2,1)}, u32[]{:S(2)}) copy-start(bf16[8,448]{1,0:T(8,128)(2,1)} %resid_ref.1) | copy-start | bytes 21508
  12.8 51.0 %copy-start.3 = (f32[448,16]{0,1:T(8,128)S(1)}, f32[448,16]{0,1:T(8,128)}, u32[]{:S(2)}) copy-start(f32[448,16]{0,1:T(8,128)} %param.23) | copy-start | bytes 86020
  12.8 50.9 %copy-start.5 = (f32[448]{0:T(512)S(1)}, f32[448]{0:T(512)}, u32[]{:S(2)}) copy-start(f32[448]{0:T(512)} %param.22) | copy-start | bytes 5380
  25.7 42.8 %copy-start.6 = (bf16[1,448,2,1024]{3,2,1,0:T(2,128)(2,1)S(1)}, bf16[1,448,2,1024]{3,2,1,0:T(2,128)(2,1)}, u32[]{:S(2)}) copy-start(bf16[1,448,2,1024]{3,2,1,0:T(2,128)(2,1)} %param.26) | copy-start | bytes 5505028
  65.0 13.3 %all-to-all-start.3 = ((bf16[16,24,256]{2,1,0:T(8,128)(2,1)}), bf16[16,24,256]{2,1,0:T(8,128)(2,1)S(1)}, u32[]{:S(2)}, u32[]{:S(2)}) async-start(bf16[16,24,256]{2,1,0:T(8,128)(2,1)} %get-tuple-element.13), calls=%async_computation.3 | async-start | bytes 393216 | tf_op jit(solution)/shard_map/all_to_all | solution.py:476
  79.0 41.9 %copy-start.1 = (bf16[1,1024,448]{1,2,0:T(8,128)(2,1)S(1)}, bf16[1,1024,448]{1,2,0:T(8,128)(2,1)}, u32[]{:S(2)}) copy-start(bf16[1,1024,448]{1,2,0:T(8,128)(2,1)} %param.27) | copy-start | bytes 2752516

commit v8 on v7

--- a/solution.py
+++ b/solution.py
@@ -76,6 +76,18 @@
     last = packed[16:]
     upper = jnp.concatenate([packed[:8], packed[8:16]], axis=1)
     return upper, jnp.concatenate([last, pltpu.roll(last, 4, 0)], axis=1)
+
+
+def pack_block(value):
+    row = iota((8, 128), 0)
+    tail = value[:, 384:]
+    return jnp.concatenate(
+        [
+            jnp.where(row < 6, value[:, 128 * at : 128 * at + 128], pltpu.roll(tail, 6 - 2 * at, 0))
+            for at in range(3)
+        ],
+        axis=0,
+    )
 
 
 def attend_kernel(
@@ -96,9 +108,6 @@
     cache_rope_ref,
     sems,
 ):
-    positions = cache_ref.shape[0]
-    step = positions // 4
-    blocks = [pl.ds(step * index, step) for index in range(4)]
     copies = [
         pltpu.make_async_copy(source, target, sems.at[index])
         for index, (source, target) in enumerate(
@@ -106,16 +115,16 @@
                 (rope_hbm, rope_ref),
                 (cache_rope_hbm, cache_rope_ref),
                 (latent_hbm, latent_ref),
+                (cache_hbm, cache_ref),
                 (routes_hbm, routes_ref),
                 (slots_hbm, slots_ref),
             ]
-            + [(cache_hbm.at[block], cache_ref.at[block]) for block in blocks]
         )
     ]
     for copy in copies:
         copy.start()
-    copies[3].wait()
     copies[4].wait()
+    copies[5].wait()
     heads, latent = latent_ref.shape
     half = heads // 2
     width = cache_rope_ref.shape[0]
@@ -148,17 +157,15 @@
     )
     copies[2].wait()
     query = jnp.concatenate([latent_ref[pl.ds(other, half), :], latent_ref[pl.ds(mine, half), :]], axis=0)
-    parts = []
-    for index, block in enumerate(blocks):
-        copies[5 + index].wait()
-        parts.append(dot_nt(query, cache_ref[block, :]))
-    scores = jnp.concatenate(parts, axis=1) + rope_scores
+    copies[3].wait()
+    cache = cache_ref[...]
+    scores = dot_nt(query, cache) + rope_scores
     usable = iota(scores.shape, 1) < place_ref[1]
     masked = jnp.where(usable, scores * score_scale, masked_floor)
     top = jnp.max(masked, axis=1, keepdims=True).astype(bf16).astype(f32)
     expon = jnp.where(usable, jnp.exp(masked - top), 0.0)
     mass = jnp.sum(expon, axis=1, keepdims=True)
-    weighted = jnp.dot(expon.astype(bf16), cache_ref[...], preferred_element_type=f32)
+    weighted = jnp.dot(expon.astype(bf16), cache, preferred_element_type=f32)
     mass_high = mass.astype(bf16).astype(f32)
     lane = iota((heads, 128), 1)
     side = jnp.where(lane == 0, top, 0.0)
@@ -183,17 +190,21 @@
     out_ref[...] = total + pack_pair(upper, lower)
 
 
-def last_sum_kernel(section_ref, halves_ref, hidden_ref, out_ref):
-    block_rows, width = out_ref.shape
-    total = halves_ref[0] + halves_ref[1]
-    rows = total.shape[0] // 2
-    total = hidden_ref[...] + jnp.concatenate([total[:rows], total[rows:]], axis=1)
-    own = jnp.where(section_ref[...] == 0, total[:block_rows], total[block_rows:])
-    out_ref[...] = own[:, :width].astype(bf16)
+def half_sum_kernel(section_ref, both_ref, kept_ref, out_ref):
+    theirs = jnp.where(section_ref[...] == 0, both_ref[1].astype(f32), both_ref[0].astype(f32))
+    out_ref[...] = (kept_ref[...] + theirs).astype(bf16)
+
+
+def last_sum_kernel(returned_ref, placement_ref, hidden_ref, out_ref):
+    width = out_ref.shape[1]
+    returned = returned_ref[...].reshape(-1, 128)
+    tiles = jnp.dot(placement_ref[...], returned, preferred_element_type=f32)
+    mixture = jnp.concatenate([tiles[8 * at : 8 * at + 8] for at in range(4)], axis=1)
+    out_ref[...] = (hidden_ref[...] + mixture)[:, :width].astype(bf16)
 
 
 def dispatch_kernel(
-    expert_total, choices, capacity, sums_ref, gain_ref, router_ref, both_ref, buffer_ref, hidden_ref, placement_ref
+    expert_total, choices, capacity, section_ref, sums_ref, gain_ref, router_ref, both_ref, buffer_ref, hidden_ref, placement_ref
 ):
     latent = both_ref.shape[2] - 128
     table = both_ref[:, :8, latent:].astype(f32).reshape(16, 128)
@@ -218,10 +229,28 @@
         low = jnp.where(spot == low_spot, 1.0, low)
         high = jnp.where(spot == high_spot, 1.0, high)
     placement = jnp.concatenate([low, high], axis=0).astype(bf16)
-    placement_ref[...] = placement
+
+    is_first = section_ref[...] == 0
+    own = jnp.where(is_first, table[:8], table[8:])
+    own_spot = iota((8, expert_total * chunk), 1).astype(f32)
+    sources = []
+    for tile in range(4):
+        source = jnp.zeros(own_spot.shape, f32)
+        for choice in range(choices):
+            route = own[:, 16 + choice : 17 + choice]
+            slot = own[:, 16 + choices + choice : 17 + choices + choice]
+            if tile < 3:
+                wanted = 8.0 * tile + slot
+            else:
+                pair = jnp.floor(slot * 0.5)
+                wanted = 8.0 * pair + 6.0 + (slot - 2.0 * pair)
+            wanted = jnp.where(slot < capacity, route * chunk + wanted, -1.0)
+            source = jnp.where(own_spot == wanted, 1.0, source)
+        sources.append(source)
+    placement_ref[...] = jnp.concatenate(sources, axis=0).astype(bf16)
 
     hidden = unpack_pair(sums_ref[0] + sums_ref[1])
-    hidden_ref[...] = hidden
+    hidden_ref[...] = jnp.where(is_first, hidden[:8], hidden[8:])
     width = gain_ref.shape[1]
     gained = hidden * pad_lanes(gain_ref[...])
     squares = jnp.sum(hidden * hidden, axis=1, keepdims=True)
@@ -345,16 +374,21 @@
         out_ref[member] = packed
 
 
-def down_kernel(packed_ref, weight_ref, out_ref):
+def down_kernel(section_ref, packed_ref, weight_ref, sent_ref, kept_ref):
     rows = []
     for member in range(packed_ref.shape[0]):
         rows += unpack_slots(packed_ref[member].astype(f32))
     left = jnp.concatenate(rows, axis=0).astype(bf16)
     out = pad_lanes(dot_nt(left, weight_ref[...]))
-    for group in range(out_ref.shape[0]):
+    is_first = section_ref[...] == 0
+    for group in range(sent_ref.shape[0]):
         start = 16 * group
-        packed = pack_slots(out[start : start + 8], out[start + 8 : start + 16])
-        out_ref[group] = packed.astype(bf16)
+        early, late = out[start : start + 8], out[start + 8 : start + 16]
+        row = iota(early.shape, 0)
+        second = jnp.where(row < 2, pltpu.roll(early, 2, 0), pltpu.roll(late, 2, 0))
+        first, second = pack_block(early), pack_block(second)
+        sent_ref[group] = jnp.where(is_first, second, first).astype(bf16)
+        kept_ref[group] = jnp.where(is_first, first, second)
 
 
 def body(
@@ -409,7 +443,7 @@
             pltpu.VMEM(q_rope.shape, bf16),
             pltpu.VMEM(cache_latent.shape[1:], bf16),
             pltpu.VMEM(cache_rope.shape[1:], bf16),
-            pltpu.SemaphoreType.DMA((9,)),
+            pltpu.SemaphoreType.DMA((6,)),
         ],
         compiler_params=vmem,
     )(
@@ -466,13 +500,13 @@
         functools.partial(dispatch_kernel, expert_total, choices, capacity),
         out_shape=(
             jax.ShapeDtypeStruct((expert_total, chunk, padded_width // 2), bf16),
-            jax.ShapeDtypeStruct((pair_rows, padded_width), f32),
-            jax.ShapeDtypeStruct((2 * pair_rows, expert_total * chunk), bf16),
+            jax.ShapeDtypeStruct((block_rows, padded_width), f32),
+            jax.ShapeDtypeStruct((4 * block_rows, expert_total * chunk), bf16),
         ),
-        in_specs=in_vmem(4),
+        in_specs=in_vmem(5),
         out_specs=tuple(in_vmem(3)),
         compiler_params=vmem,
-    )(summed, norm_gain[None], router.T, both)
+    )(own_section, summed, norm_gain[None], router.T, both)
     received = lax.all_to_all(buffer, "grp", split_axis=0, concat_axis=0, tiled=True)
 
     unit = w_gateup.shape[3]
@@ -496,24 +530,32 @@
     )(sums)
 
     everyone = lax.all_to_all(packed, "dev", split_axis=0, concat_axis=0, tiled=True)
+    sent, kept = pl.pallas_call(
+        down_kernel,
+        out_shape=(
+            jax.ShapeDtypeStruct((groups, 24, 128), bf16),
+            jax.ShapeDtypeStruct((groups, 24, 128), f32),
+        ),
+        in_specs=in_vmem(3),
+        out_specs=tuple(in_vmem(2)),
+        compiler_params=vmem,
+    )(own_section, everyone, w_down[0].T)
+    halves = lax.all_gather(sent, "sec", axis=0)
     down = pl.pallas_call(
-        down_kernel,
-        out_shape=jax.ShapeDtypeStruct((groups, chunk, padded_width // 2), bf16),
-        in_specs=in_vmem(2),
+        half_sum_kernel,
+        out_shape=jax.ShapeDtypeStruct((groups, 24, 128), bf16),
+        in_specs=in_vmem(3),
         out_specs=in_vmem(1)[0],
         compiler_params=vmem,
-    )(everyone, w_down[0].T)
+    )(own_section, halves, kept)
     returned = lax.all_to_all(down, "grp", split_axis=0, concat_axis=0, tiled=True)
-    returned = returned.reshape(expert_total * chunk, padded_width // 2)
-    mixture = jnp.dot(placement, returned, preferred_element_type=f32)
-    halves = lax.all_gather(mixture, "sec", axis=0)
     return pl.pallas_call(
         last_sum_kernel,
         out_shape=jax.ShapeDtypeStruct((block_rows, width_local), bf16),
         in_specs=in_vmem(3),
         out_specs=in_vmem(1)[0],
         compiler_params=vmem,
-    )(own_section, halves, hidden)
+    )(returned, placement, hidden)
 
 
 def solution(mesh):

time: 143 us -> 141 us (0.986)
  blocking collectives: 120 us -> 118 us
    all_gather x1, blocking collectives: 7.41 us -> 5.72 us  [body(): halves = lax.all_gather(sent, 'sec', axis=0)]
where the time goes in v8:
time: 141 us
  blocking collectives  118 us (84%)
  waiting for transfers between devices  9.07 us (6%)
  Pallas kernels  7.34 us (5%)
  starting transfers between devices  3.53 us (3%)
    all_to_all x1, blocking collectives, body(): sums = lax.all_to_all(sums, 'dev', split_axis=0, concat_axis=0, tiled=True)  25.9 us
    all_to_all x1, blocking collectives, spread(): return lax.all_to_all(copies, axis, split_axis=0, concat_axis=0, tiled=True)  17.9 us
    all_to_all x1, blocking collectives, body(): lax.all_to_all(packed, 'dev', split_axis=0, concat_axis=0, tiled=True)  15.7 us
    all_to_all x1, blocking collectives, body(): lax.all_to_all(partial, 'grp', split_axis=0, concat_axis=0, tiled=True)  13.1 us
    all_to_all x1, blocking collectives, body(): lax.all_to_all(down, 'grp', split_axis=0, concat_axis=0, tiled=True)  12.8 us
    all_to_all x1, blocking collectives, body(): lax.all_to_all(outgoing_heads, 'grp', split_axis=0, concat_axis=0, tiled=...  12.7 us
    all_to_all x1, waiting for transfers between devices, body(): lax.all_to_all(buffer, 'grp', split_axis=0, concat_axis=0, tiled=True)  9.07 us
    all_gather x1, blocking collectives, body(): both = lax.all_gather(sent, 'sec', axis=0)  8.45 us
  transfers between devices with their start and end apart: 1, of which 1 were waited for; matrix products, arithmetic and copies ran while one was open for 1% of the time, Pallas kernels for 0%

profile of v8, /device:TPU:1, one launch (start us, length us, event | category | flops | bytes accessed | tf_op | source)
XLA Modules:
  0.0 140.6 jit_solution(7692992277117893321)
XLA Ops:
  0.0 0.0 copy-start
  0.7 0.1 pad_add_fusion.place_ref
  0.8 0.0 copy-start.2
  0.8 3.1 %shard_map.136 = (bf16[64,640]{1,0:T(8,128)(2,1)S(1)}, f32[64,640]{1,0:T(8,128)S(1)}) custom-call(s32[2]{0:T(128)S(1)} %pad_add_fusion.place_ref, bf16[128,512]{1,0:T(8,128)(2,1)} %bitcast.42, bf16[1,8192]{1,0:T(2,128)(2,1)} %rope_hbm.1, bf16[1024,512]{1,0:T(8,128)(2,1)} %bitcast.41, bf16[64,1024]{1,0:T(8,128)(2,1)} %bitcast.43, s32[8,8]{1,0:T(8,128)} %routes_hbm.1, ...), custom_call_target="tpu_custom_call" | custom-call | tf_op jit(solution)/shard_map/pallas_call | solution.py:431
  3.9 8.4 %all-gather = bf16[128,640]{1,0:T(8,128)(2,1)S(1)} all-gather(bf16[64,640]{1,0:T(8,128)(2,1)S(1)} %get-tuple-element.13), channel_id=2, replica_groups=mesh['sec'=2,'grp'=16,'dev'=16] {'sec'}, dimensions={0}, use_global_device_ids=true | all-gather | bytes 245760 | tf_op jit(solution)/shard_map/all_gather | solution.py:458
  12.4 0.0 copy-start.4
  12.4 0.2 fusion.5
  12.6 0.0 copy-start.3
  12.6 0.0 copy-start.5
  12.6 0.1 divide_convert_fusion
  12.8 12.7 %all_to_all.35 = bf16[16,4,512]{2,1,0:T(4,128)(2,1)S(1)} all-to-all(bf16[16,4,512]{2,1,0:T(4,128)(2,1)S(1)} %reshape.15), channel_id=1, replica_groups=mesh['sec'=2,'grp'=16,'dev'=16] {'grp'}, dimensions={0} | all-to-all | bytes 131072 | tf_op jit(solution)/shard_map/all_to_all | solution.py:477
  25.5 0.0 copy-done
  25.5 0.0 copy-start.6
  25.5 0.2 fusion
  25.7 17.9 %all_to_all.36.gathered_ref = bf16[16,16,512]{2,1,0:T(8,128)(2,1)S(1)} all-to-all(bf16[16,16,512]{2,1,0:T(8,128)(2,1)S(1)} %broadcast_in_dim.11), channel_id=1, replica_groups=mesh['sec'=2,'grp'=16,'dev'=16] {'dev'}, dimensions={0} | all-to-all | bytes 524288 | tf_op jit(solution)/shard_map/all_to_all | solution.py:20
  43.6 0.0 copy-done.2
  43.6 0.5 shard_map.137
  44.1 13.1 %all_to_all.37.partial_ref = bf16[16,56,128]{2,1,0:T(8,128)(2,1)S(1)} all-to-all(bf16[16,56,128]{2,1,0:T(8,128)(2,1)S(1)} %shard_map.137), channel_id=1, replica_groups=mesh['sec'=2,'grp'=16,'dev'=16] {'grp'}, dimensions={0} | all-to-all | bytes 458752 | tf_op jit(solution)/shard_map/all_to_all | solution.py:488
  57.2 0.0 copy-done.4
  57.2 0.1 shard_map.138
  57.3 6.2 %all-gather.1 = f32[112,128]{1,0:T(8,128)S(1)} all-gather(f32[56,128]{1,0:T(8,128)S(1)} %shard_map.138), channel_id=3, replica_groups=mesh['sec'=2,'grp'=16,'dev'=16] {'sec'}, dimensions={0}, use_global_device_ids=true | all-gather | bytes 86016 | tf_op jit(solution)/shard_map/all_gather | solution.py:496
  63.6 0.0 copy-done.3
  63.6 0.0 copy-done.5
  63.6 1.2 shard_map.139
  64.8 3.5 %all-to-all-start.3 = ((bf16[16,24,256]{2,1,0:T(8,128)(2,1)}), bf16[16,24,256]{2,1,0:T(8,128)(2,1)S(1)}, u32[]{:S(2)}, u32[]{:S(2)}) async-start(bf16[16,24,256]{2,1,0:T(8,128)(2,1)} %get-tuple-element.14), calls=%async_computation.3 | async-start | bytes 393216 | tf_op jit(solution)/shard_map/all_to_all | solution.py:510
  68.3 0.0 copy-done.6
  68.3 0.5 copy.23
  68.9 0.2 pad.4.clone
  69.1 9.1 %all-to-all-done.3.received_ref = bf16[16,24,256]{2,1,0:T(8,128)(2,1)S(1)} async-done(((bf16[16,24,256]{2,1,0:T(8,128)(2,1)}), bf16[16,24,256]{2,1,0:T(8,128)(2,1)S(1)}, u32[]{:S(2)}, u32[]{:S(2)}) %all-to-all-start.3) | async-done | bytes 196640 | tf_op jit(solution)/shard_map/all_to_all | solution.py:510
  78.1 0.7 shard_map.140
  78.9 0.0 copy-start.1
  78.9 25.9 %all_to_all.38.sums_ref = bf16[16,200,128]{2,1,0:T(8,128)(2,1)S(1)} all-to-all(bf16[16,200,128]{2,1,0:T(8,128)(2,1)S(1)} %shard_map.140), channel_id=1, replica_groups=mesh['sec'=2,'grp'=16,'dev'=16] {'dev'}, dimensions={0} | all-to-all | bytes 1638400 | tf_op jit(solution)/shard_map/all_to_all | solution.py:523
  104.8 0.3 shard_map.141
  105.1 15.7 %all_to_all.39.packed_ref = bf16[16,24,512]{2,1,0:T(8,128)(2,1)S(1)} all-to-all(bf16[16,24,512]{2,1,0:T(8,128)(2,1)S(1)} %shard_map.141), channel_id=1, replica_groups=mesh['sec'=2,'grp'=16,'dev'=16] {'dev'}, dimensions={0} | all-to-all | bytes 786432 | tf_op jit(solution)/shard_map/all_to_all | solution.py:532
  120.8 0.0 copy-done.1
  120.8 0.5 shard_map.142
  121.2 5.7 %all-gather.2 = bf16[32,24,128]{2,1,0:T(8,128)(2,1)S(1)} all-gather(bf16[16,24,128]{2,1,0:T(8,128)(2,1)S(1)} %get-tuple-element.15), channel_id=4, replica_groups=mesh['sec'=2,'grp'=16,'dev'=16] {'sec'}, dimensions={0}, use_global_device_ids=true | all-gather | bytes 294912 | tf_op jit(solution)/shard_map/all_gather | solution.py:543
  127.0 0.1 shard_map.143
  127.1 12.8 %all_to_all.40.returned_ref = bf16[16,24,128]{2,1,0:T(8,128)(2,1)S(1)} all-to-all(bf16[16,24,128]{2,1,0:T(8,128)(2,1)S(1)} %shard_map.143), channel_id=1, replica_groups=mesh['sec'=2,'grp'=16,'dev'=16] {'grp'}, dimensions={0} | all-to-all | bytes 196608 | tf_op jit(solution)/shard_map/all_to_all | solution.py:551
  139.9 0.7 shard_map.144
  (4 shorter events, 0.1 us)
Async XLA Ops:
  0.0 25.5 %copy-start = (bf16[4,512,128]{2,1,0:T(8,128)(2,1)S(1)}, bf16[4,512,128]{2,1,0:T(8,128)(2,1)}, u32[]{:S(2)}) copy-start(bf16[4,512,128]{2,1,0:T(8,128)(2,1)} %param.19) | copy-start | bytes 1572868
  0.8 42.8 %copy-start.2 = (bf16[512,448]{0,1:T(8,128)(2,1)S(1)}, bf16[512,448]{0,1:T(8,128)(2,1)}, u32[]{:S(2)}) copy-start(bf16[512,448]{0,1:T(8,128)(2,1)} %param.20) | copy-start | bytes 1376260
  12.4 44.8 %copy-start.4 = (bf16[8,448]{1,0:T(8,128)(2,1)S(1)}, bf16[8,448]{1,0:T(8,128)(2,1)}, u32[]{:S(2)}) copy-start(bf16[8,448]{1,0:T(8,128)(2,1)} %resid_ref.1) | copy-start | bytes 21508
  12.6 51.0 %copy-start.3 = (f32[448,16]{0,1:T(8,128)S(1)}, f32[448,16]{0,1:T(8,128)}, u32[]{:S(2)}) copy-start(f32[448,16]{0,1:T(8,128)} %param.23) | copy-start | bytes 86020
  12.6 50.9 %copy-start.5 = (f32[448]{0:T(512)S(1)}, f32[448]{0:T(512)}, u32[]{:S(2)}) copy-start(f32[448]{0:T(512)} %param.22) | copy-start | bytes 5380
  25.5 42.8 %copy-start.6 = (bf16[1,448,2,1024]{3,2,1,0:T(2,128)(2,1)S(1)}, bf16[1,448,2,1024]{3,2,1,0:T(2,128)(2,1)}, u32[]{:S(2)}) copy-start(bf16[1,448,2,1024]{3,2,1,0:T(2,128)(2,1)} %param.26) | copy-start | bytes 5505028
  64.8 13.4 %all-to-all-start.3 = ((bf16[16,24,256]{2,1,0:T(8,128)(2,1)}), bf16[16,24,256]{2,1,0:T(8,128)(2,1)S(1)}, u32[]{:S(2)}, u32[]{:S(2)}) async-start(bf16[16,24,256]{2,1,0:T(8,128)(2,1)} %get-tuple-element.14), calls=%async_computation.3 | async-start | bytes 393216 | tf_op jit(solution)/shard_map/all_to_all | solution.py:510
  78.9 41.9 %copy-start.1 = (bf16[1,1024,448]{1,2,0:T(8,128)(2,1)S(1)}, bf16[1,1024,448]{1,2,0:T(8,128)(2,1)}, u32[]{:S(2)}) copy-start(bf16[1,1024,448]{1,2,0:T(8,128)(2,1)} %param.27) | copy-start | bytes 2752516

commit v9 on v8

--- a/solution.py
+++ b/solution.py
@@ -45,23 +45,6 @@
     if spare == 0:
         return value
     return jnp.concatenate([value, jnp.zeros((value.shape[0], spare), value.dtype)], axis=1)
-
-
-def pack_pair(upper, lower):
-    full = upper.shape[1] // 128 * 128
-    tiles = [block[:, at : at + 128] for block in (upper, lower) for at in range(0, full, 128)]
-    tail = pad_lanes(upper[:, full:]) + pltpu.roll(pad_lanes(lower[:, full:]), 64, 1)
-    return jnp.concatenate(tiles + [tail], axis=0)
-
-
-def unpack_pair(packed):
-    full = packed.shape[0] // 16
-    tiles = [packed[8 * at : 8 * at + 8] for at in range(2 * full + 1)]
-    first = iota((8, 128), 1) < 64
-    upper = jnp.concatenate(tiles[:full] + [jnp.where(first, tiles[-1], 0.0)], axis=1)
-    turned = pltpu.roll(tiles[-1], 64, 1)
-    lower = jnp.concatenate(tiles[full:-1] + [jnp.where(first, turned, 0.0)], axis=1)
-    return jnp.concatenate([upper, lower], axis=0)
 
 
 def pack_slots(upper, lower):
@@ -90,18 +73,22 @@
     )
 
 
+def unpack_block(packed):
+    row = iota((8, 128), 0)
+    tiles = [packed[:8], packed[8:16], packed[16:]]
+    turned = [pltpu.roll(tile, 2 * at + 2, 0) for at, tile in enumerate(tiles)]
+    tail = jnp.where(row < 2, turned[0], jnp.where(row < 4, turned[1], turned[2]))
+    return jnp.concatenate(tiles + [tail], axis=1)
+
+
 def attend_kernel(
     place_ref,
     latent_hbm,
     rope_hbm,
     cache_hbm,
     cache_rope_hbm,
-    routes_hbm,
-    slots_hbm,
     sent_ref,
     kept_ref,
-    routes_ref,
-    slots_ref,
     latent_ref,
     rope_ref,
     cache_ref,
@@ -116,28 +103,16 @@
                 (cache_rope_hbm, cache_rope_ref),
                 (latent_hbm, latent_ref),
                 (cache_hbm, cache_ref),
-                (routes_hbm, routes_ref),
-                (slots_hbm, slots_ref),
             ]
         )
     ]
     for copy in copies:
         copy.start()
-    copies[4].wait()
-    copies[5].wait()
     heads, latent = latent_ref.shape
     half = heads // 2
     width = cache_rope_ref.shape[0]
     mine = pl.multiple_of(place_ref[0] * half, half)
     other = pl.multiple_of(half - place_ref[0] * half, half)
-
-    choices = routes_ref.shape[1]
-    spot = iota((choices, 128), 1) - iota((choices, 128), 0)
-    table = jnp.dot(
-        routes_ref[...].astype(f32), jnp.where(spot == 16, 1.0, 0.0), preferred_element_type=f32
-    ) + jnp.dot(
-        slots_ref[...].astype(f32), jnp.where(spot == 16 + choices, 1.0, 0.0), preferred_element_type=f32
-    )
 
     copies[0].wait()
     row = rope_ref[...].astype(f32)
@@ -173,21 +148,8 @@
     side = jnp.where(lane == 2, mass - mass_high, side)
     kept_ref[:, :latent] = weighted[half:]
     kept_ref[:, latent:] = side[half:]
-    block_rows = table.shape[0]
-    side = jnp.concatenate([side[:block_rows] + table, side[block_rows:half]], axis=0)
     sent_ref[:, :latent] = weighted[:half].astype(bf16)
-    sent_ref[:, latent:] = side.astype(bf16)
-
-
-def block_sum_kernel(section_ref, partial_ref, resid_ref, out_ref):
-    total = partial_ref[0].astype(f32)
-    for group in range(1, partial_ref.shape[0]):
-        total = total + partial_ref[group].astype(f32)
-    resid = resid_ref[...].astype(f32)
-    section = section_ref[...]
-    upper = jnp.where(section == 0, resid, 0.0)
-    lower = jnp.where(section == 1, resid, 0.0)
-    out_ref[...] = total + pack_pair(upper, lower)
+    sent_ref[:, latent:] = side[:half].astype(bf16)
 
 
 def half_sum_kernel(section_ref, both_ref, kept_ref, out_ref):
@@ -204,53 +166,32 @@
 
 
 def dispatch_kernel(
-    expert_total, choices, capacity, section_ref, sums_ref, gain_ref, router_ref, both_ref, buffer_ref, hidden_ref, placement_ref
+    expert_total, capacity, partial_ref, resid_ref, gain_ref, router_ref, routes_ref, slots_ref, buffer_ref, hidden_ref, placement_ref
 ):
-    latent = both_ref.shape[2] - 128
-    table = both_ref[:, :8, latent:].astype(f32).reshape(16, 128)
-    rows = table.shape[0]
+    routes = routes_ref[...].astype(f32)
+    slots = slots_ref[...].astype(f32)
+    rows, choices = routes.shape
     chunk = buffer_ref.shape[1]
     lane = iota((rows, 128), 1)
-    block = jnp.where(iota((rows, 1), 0) < rows // 2, 0.0, 1.0 * capacity)
+    spot = iota((rows, expert_total * chunk), 1).astype(f32)
     named = jnp.zeros((rows, 128), f32)
-    spot = iota((rows, expert_total * chunk), 1).astype(f32)
-    low = jnp.zeros(spot.shape, f32)
-    high = jnp.zeros(spot.shape, f32)
+    sources = [jnp.zeros(spot.shape, f32) for _ in range(4)]
     for choice in range(choices):
-        route = table[:, 16 + choice : 17 + choice]
-        slot = table[:, 16 + choices + choice : 17 + choices + choice]
+        route = routes[:, choice : choice + 1]
+        slot = slots[:, choice : choice + 1]
         named = jnp.where(lane.astype(f32) == route, 1.0, named)
-        packed = block + slot
-        early = packed < 8
-        kept = slot < capacity
-        start = route * chunk + packed
-        low_spot = jnp.where(kept, start + jnp.where(early, 0.0, 8.0), -1.0)
-        high_spot = jnp.where(kept, start + jnp.where(early, 8.0, 12.0), -1.0)
-        low = jnp.where(spot == low_spot, 1.0, low)
-        high = jnp.where(spot == high_spot, 1.0, high)
-    placement = jnp.concatenate([low, high], axis=0).astype(bf16)
-
-    is_first = section_ref[...] == 0
-    own = jnp.where(is_first, table[:8], table[8:])
-    own_spot = iota((8, expert_total * chunk), 1).astype(f32)
-    sources = []
-    for tile in range(4):
-        source = jnp.zeros(own_spot.shape, f32)
-        for choice in range(choices):
-            route = own[:, 16 + choice : 17 + choice]
-            slot = own[:, 16 + choices + choice : 17 + choices + choice]
-            if tile < 3:
-                wanted = 8.0 * tile + slot
-            else:
-                pair = jnp.floor(slot * 0.5)
-                wanted = 8.0 * pair + 6.0 + (slot - 2.0 * pair)
-            wanted = jnp.where(slot < capacity, route * chunk + wanted, -1.0)
-            source = jnp.where(own_spot == wanted, 1.0, source)
-        sources.append(source)
-    placement_ref[...] = jnp.concatenate(sources, axis=0).astype(bf16)
-
-    hidden = unpack_pair(sums_ref[0] + sums_ref[1])
-    hidden_ref[...] = jnp.where(is_first, hidden[:8], hidden[8:])
+        pair = jnp.floor(slot * 0.5)
+        wanted = [8.0 * at + slot for at in range(3)] + [6.0 * pair + 6.0 + slot]
+        for at in range(4):
+            place = jnp.where(slot < capacity, route * chunk + wanted[at], -1.0)
+            sources[at] = jnp.where(spot == place, 1.0, sources[at])
+    placement = jnp.concatenate(sources, axis=0).astype(bf16)
+    placement_ref[...] = placement
+
+    hidden = pad_lanes(resid_ref[...].astype(f32))
+    for group in range(partial_ref.shape[0]):
+        hidden = hidden + partial_ref[group].astype(f32)
+    hidden_ref[...] = hidden
     width = gain_ref.shape[1]
     gained = hidden * pad_lanes(gain_ref[...])
     squares = jnp.sum(hidden * hidden, axis=1, keepdims=True)
@@ -274,15 +215,14 @@
     full = width - first
     last = jnp.where(lane < first, gained[:, full:], side)
     content = jnp.concatenate([gained[:, :full], last], axis=1)
-    half = content.shape[1] // 2
-    content = jnp.concatenate([content[:, :half], content[:, half:]], axis=0)
+    content = jnp.concatenate([content[:, 128 * at : 128 * at + 128] for at in range(4)], axis=0)
     out = lax.dot_general(
         placement, content.astype(bf16), (((0,), (0,)), ((), ())), preferred_element_type=f32
     )
     buffer_ref[...] = out.astype(bf16).reshape(buffer_ref.shape)
 
 
-def project_kernel(gathered_ref, weight_ref, out_ref):
+def project_kernel(section_ref, gathered_ref, weight_ref, sent_ref, kept_ref):
     members, groups, width = gathered_ref.shape
     total = members * groups
     rows = gathered_ref[...].reshape(total, width)
@@ -292,23 +232,28 @@
     found = (source & (groups - 1)) * members + (source >> 4)
     rows = select_rows(one_hot(wanted == found), rows)
     out = dot_nt(rows, weight_ref[...])
-    for owner in range(out_ref.shape[0]):
+    is_first = section_ref[...] == 0
+    for owner in range(sent_ref.shape[0]):
         start = 16 * owner
-        packed = pack_pair(out[start : start + 8], out[start + 8 : start + 16])
-        out_ref[owner] = packed.astype(bf16)
+        first = pad_lanes(out[start : start + 8])
+        second = pad_lanes(out[start + 8 : start + 16])
+        sent_ref[owner] = jnp.where(is_first, second, first).astype(bf16)
+        kept_ref[owner] = jnp.where(is_first, first, second)
 
 
 def gate_up_kernel(expert_total, expert_ref, received_ref, weight_ref, out_ref):
-    members = received_ref.shape[0]
-    width = 2 * received_ref.shape[2]
-    upside = iota((8, width), 0) < 4
+    members = received_ref.shape[1]
+    width = 4 * received_ref.shape[3]
+    row = iota((8, width), 0)
     rows, side = [], []
     first = iota((8, 128), 1) < 64
     is_expert = (iota((8, 128), 1) & 63) == 3 * expert_total + 2
     expert = expert_ref[...].astype(f32)
     for member in range(members):
-        early, late = unpack_slots(received_ref[member].astype(f32))
-        late = jnp.where(upside, late, 0.0)
+        first_block = unpack_block(received_ref[0, member].astype(f32))
+        turned = pltpu.roll(unpack_block(received_ref[1, member].astype(f32)), 6, 0)
+        early = jnp.where(row < 6, first_block, turned)
+        late = jnp.where(row < 4, turned, 0.0)
         rows += [early, late]
         turned = pltpu.roll(early[:, width - 128 :], 64, 1)
         last = jnp.where(first, turned, late[:, width - 128 :])
@@ -417,11 +362,8 @@
     half_heads = head_total // sections
     head_block, _, value_width = w_uv.shape
     block_rows, width_local = resid.shape
-    choices = routes.shape[1]
     expert_total = router.shape[1]
     capacity = max(2, 3 * block_rows // 4)
-    pair_rows = sections * block_rows
-    pair_tiles = 8 * (2 * (width_local // 128) + 1)
     padded_width = width_local + -width_local % 128
     in_smem = pl.BlockSpec(memory_space=pltpu.SMEM)
     vmem = pltpu.CompilerParams(vmem_limit_bytes=32 * 2**20)
@@ -434,23 +376,21 @@
             jax.ShapeDtypeStruct((half_heads, latent + 128), bf16),
             jax.ShapeDtypeStruct((half_heads, latent + 128), f32),
         ),
-        in_specs=[in_smem] + [pl.BlockSpec(memory_space=pltpu.HBM)] * 6,
+        in_specs=[in_smem] + [pl.BlockSpec(memory_space=pltpu.HBM)] * 4,
         out_specs=tuple(in_vmem(2)),
         scratch_shapes=[
-            pltpu.VMEM(routes.shape, jnp.int32),
-            pltpu.VMEM(slots.shape, jnp.int32),
             pltpu.VMEM((head_total, latent), bf16),
             pltpu.VMEM(q_rope.shape, bf16),
             pltpu.VMEM(cache_latent.shape[1:], bf16),
             pltpu.VMEM(cache_rope.shape[1:], bf16),
-            pltpu.SemaphoreType.DMA((6,)),
+            pltpu.SemaphoreType.DMA((4,)),
         ],
         compiler_params=vmem,
     )(
         place,
         *[
             pltpu.with_memory_space_constraint(operand, pltpu.HBM)
-            for operand in (q_latent[0], q_rope, cache_latent[0], cache_rope[0], routes, slots)
+            for operand in (q_latent[0], q_rope, cache_latent[0], cache_rope[0])
         ],
     )
 
@@ -478,36 +418,42 @@
     values = jnp.einsum("nhc,hcv->nhv", arrived, w_uv, preferred_element_type=f32).astype(bf16)
     width_heads = head_block * value_width
     gathered = spread(values.reshape(groups, width_heads), "dev")
-    partial = pl.pallas_call(
+    sent, kept = pl.pallas_call(
         project_kernel,
-        out_shape=jax.ShapeDtypeStruct((groups, pair_tiles, 128), bf16),
-        in_specs=in_vmem(2),
-        out_specs=in_vmem(1)[0],
-        compiler_params=vmem,
-    )(gathered, w_out.T)
+        out_shape=(
+            jax.ShapeDtypeStruct((groups, block_rows, padded_width), bf16),
+            jax.ShapeDtypeStruct((groups, block_rows, padded_width), f32),
+        ),
+        in_specs=in_vmem(3),
+        out_specs=tuple(in_vmem(2)),
+        compiler_params=vmem,
+    )(own_section, gathered, w_out.T)
+
+    def sum_halves(sent, kept):
+        return pl.pallas_call(
+            half_sum_kernel,
+            out_shape=jax.ShapeDtypeStruct(sent.shape, bf16),
+            in_specs=in_vmem(3),
+            out_specs=in_vmem(1)[0],
+            compiler_params=vmem,
+        )(own_section, lax.all_gather(sent, "sec", axis=0), kept)
+
+    partial = sum_halves(sent, kept)
     partial = lax.all_to_all(partial, "grp", split_axis=0, concat_axis=0, tiled=True)
-    summed = pl.pallas_call(
-        block_sum_kernel,
-        out_shape=jax.ShapeDtypeStruct((pair_tiles, 128), f32),
-        in_specs=in_vmem(3),
-        out_specs=in_vmem(1)[0],
-        compiler_params=vmem,
-    )(own_section, partial, resid)
-    summed = lax.all_gather(summed, "sec", axis=0)
-
-    chunk = 24
+
     buffer, hidden, placement = pl.pallas_call(
-        functools.partial(dispatch_kernel, expert_total, choices, capacity),
+        functools.partial(dispatch_kernel, expert_total, capacity),
         out_shape=(
-            jax.ShapeDtypeStruct((expert_total, chunk, padded_width // 2), bf16),
+            jax.ShapeDtypeStruct((expert_total, 24, 128), bf16),
             jax.ShapeDtypeStruct((block_rows, padded_width), f32),
-            jax.ShapeDtypeStruct((4 * block_rows, expert_total * chunk), bf16),
+            jax.ShapeDtypeStruct((4 * block_rows, expert_total * 24), bf16),
         ),
-        in_specs=in_vmem(5),
+        in_specs=in_vmem(6),
         out_specs=tuple(in_vmem(3)),
         compiler_params=vmem,
-    )(own_section, summed, norm_gain[None], router.T, both)
+    )(partial, resid, norm_gain[None], router.T, routes, slots)
     received = lax.all_to_all(buffer, "grp", split_axis=0, concat_axis=0, tiled=True)
+    received = lax.all_gather(received, "sec", axis=0)
 
     unit = w_gateup.shape[3]
     weight = jnp.pad(
@@ -540,14 +486,7 @@
         out_specs=tuple(in_vmem(2)),
         compiler_params=vmem,
     )(own_section, everyone, w_down[0].T)
-    halves = lax.all_gather(sent, "sec", axis=0)
-    down = pl.pallas_call(
-        half_sum_kernel,
-        out_shape=jax.ShapeDtypeStruct((groups, 24, 128), bf16),
-        in_specs=in_vmem(3),
-        out_specs=in_vmem(1)[0],
-        compiler_params=vmem,
-    )(own_section, halves, kept)
+    down = sum_halves(sent, kept)
     returned = lax.all_to_all(down, "grp", split_axis=0, concat_axis=0, tiled=True)
     return pl.pallas_call(
         last_sum_kernel,

time: 141 us -> 140 us (level)
    all_gather x2 -> x3, blocking collectives: 12 us -> 15 us  [the longest x2 10.9 us: sum_halves(): lax.all_gather(sent, 'sec', axis=0)]
    all_to_all x1, blocking collectives: 25.9 us -> 24 us  [body(): sums = lax.all_to_all(sums, 'dev', split_axis=0, concat_axis=0, tiled=True)]
where the time goes in v9:
time: 140 us
  blocking collectives  118 us (84%)
  waiting for transfers between devices  8.5 us (6%)
  Pallas kernels  6.79 us (5%)
  starting transfers between devices  4.3 us (3%)
    all_to_all x1, blocking collectives, body(): sums = lax.all_to_all(sums, 'dev', split_axis=0, concat_axis=0, tiled=True)  24 us
    all_to_all x1, blocking collectives, spread(): return lax.all_to_all(copies, axis, split_axis=0, concat_axis=0, tiled=True)  17.9 us
    all_to_all x1, blocking collectives, body(): lax.all_to_all(packed, 'dev', split_axis=0, concat_axis=0, tiled=True)  15.4 us
    all_to_all x1, blocking collectives, body(): lax.all_to_all(outgoing_heads, 'grp', split_axis=0, concat_axis=0, tiled=...  12.9 us
    all_to_all x1, blocking collectives, body(): lax.all_to_all(partial, 'grp', split_axis=0, concat_axis=0, tiled=True)  12.4 us
    all_to_all x1, blocking collectives, body(): lax.all_to_all(down, 'grp', split_axis=0, concat_axis=0, tiled=True)  11.7 us
    all_gather x2, blocking collectives, sum_halves(): lax.all_gather(sent, 'sec', axis=0)  10.9 us
    all_to_all x1, waiting for transfers between devices, body(): lax.all_to_all(buffer, 'grp', split_axis=0, concat_axis=0, tiled=True)  8.5 us
  transfers between devices with their start and end apart: 1, of which 1 were waited for; matrix products, arithmetic and copies ran while one was open for 1% of the time, Pallas kernels for 0%

profile of v9, /device:TPU:1, one launch (start us, length us, event | category | flops | bytes accessed | tf_op | source)
XLA Modules:
  0.0 139.6 jit_solution(1282149085755572452)
XLA Ops:
  0.0 0.0 copy-start
  0.7 0.1 pad_add_fusion.place_ref
  0.8 0.0 copy-start.2
  0.8 2.8 %shard_map.136 = (bf16[64,640]{1,0:T(8,128)(2,1)S(1)}, f32[64,640]{1,0:T(8,128)S(1)}) custom-call(s32[2]{0:T(128)S(1)} %pad_add_fusion.place_ref, bf16[128,512]{1,0:T(8,128)(2,1)} %bitcast.43, bf16[1,8192]{1,0:T(2,128)(2,1)} %rope_hbm.1, bf16[1024,512]{1,0:T(8,128)(2,1)} %bitcast.41, bf16[64,1024]{1,0:T(8,128)(2,1)} %bitcast.44), custom_call_target="tpu_custom_call" | custom-call | tf_op jit(solution)/shard_map/pallas_call | solution.py:373
  3.6 8.4 %all-gather = bf16[128,640]{1,0:T(8,128)(2,1)S(1)} all-gather(bf16[64,640]{1,0:T(8,128)(2,1)S(1)} %get-tuple-element.15), channel_id=2, replica_groups=mesh['sec'=2,'grp'=16,'dev'=16] {'sec'}, dimensions={0}, use_global_device_ids=true | all-gather | bytes 245760 | tf_op jit(solution)/shard_map/all_gather | solution.py:398
  12.1 0.2 fusion.5
  12.3 0.1 divide_convert_fusion
  12.4 0.0 copy-start.3
  12.4 0.0 copy-start.4
  12.4 0.0 copy-start.5
  12.4 0.0 copy-start.6
  12.5 0.0 copy-start.7
  12.5 12.9 %all_to_all.35 = bf16[16,4,512]{2,1,0:T(4,128)(2,1)S(1)} all-to-all(bf16[16,4,512]{2,1,0:T(4,128)(2,1)S(1)} %reshape.15), channel_id=1, replica_groups=mesh['sec'=2,'grp'=16,'dev'=16] {'grp'}, dimensions={0} | all-to-all | bytes 131072 | tf_op jit(solution)/shard_map/all_to_all | solution.py:417
  25.3 0.0 copy-done
  25.3 0.0 copy-start.8
  25.3 0.2 fusion
  25.6 17.9 %all_to_all.36.gathered_ref = bf16[16,16,512]{2,1,0:T(8,128)(2,1)S(1)} all-to-all(bf16[16,16,512]{2,1,0:T(8,128)(2,1)S(1)} %broadcast_in_dim.11), channel_id=1, replica_groups=mesh['sec'=2,'grp'=16,'dev'=16] {'dev'}, dimensions={0} | all-to-all | bytes 524288 | tf_op jit(solution)/shard_map/all_to_all | solution.py:20
  43.4 0.0 copy-done.2
  43.4 0.4 shard_map.137
  43.9 4.9 %all-gather.1 = bf16[32,8,512]{2,1,0:T(8,128)(2,1)S(1)} all-gather(bf16[16,8,512]{2,1,0:T(8,128)(2,1)S(1)} %get-tuple-element.16), channel_id=3, replica_groups=mesh['sec'=2,'grp'=16,'dev'=16] {'sec'}, dimensions={0}, use_global_device_ids=true | all-gather | bytes 393216 | tf_op jit(solution)/shard_map/all_gather | solution.py:439
  48.8 0.1 shard_map.138
  48.9 12.4 %all_to_all.37.partial_ref = bf16[16,8,512]{2,1,0:T(8,128)(2,1)S(1)} all-to-all(bf16[16,8,512]{2,1,0:T(8,128)(2,1)S(1)} %shard_map.138), channel_id=1, replica_groups=mesh['sec'=2,'grp'=16,'dev'=16] {'grp'}, dimensions={0} | all-to-all | bytes 262144 | tf_op jit(solution)/shard_map/all_to_all | solution.py:442
  61.3 0.0 copy-done.3
  61.4 0.0 copy-done.4
  61.4 0.0 copy-done.5
  61.4 0.0 copy-done.6
  61.4 0.0 copy-done.7
  61.4 1.1 shard_map.139
  62.5 4.3 %all-to-all-start.3 = ((bf16[16,24,128]{2,1,0:T(8,128)(2,1)}), bf16[16,24,128]{2,1,0:T(8,128)(2,1)S(1)}, u32[]{:S(2)}, u32[]{:S(2)}) async-start(bf16[16,24,128]{2,1,0:T(8,128)(2,1)} %get-tuple-element.18), calls=%async_computation.3 | async-start | bytes 196608 | tf_op jit(solution)/shard_map/all_to_all | solution.py:455
  66.8 0.0 copy-done.8
  66.8 0.5 copy.23
  67.3 0.2 pad.4.clone
  67.5 8.5 %all-to-all-done.3 = bf16[16,24,128]{2,1,0:T(8,128)(2,1)S(1)} async-done(((bf16[16,24,128]{2,1,0:T(8,128)(2,1)}), bf16[16,24,128]{2,1,0:T(8,128)(2,1)S(1)}, u32[]{:S(2)}, u32[]{:S(2)}) %all-to-all-start.3) | async-done | bytes 98336 | tf_op jit(solution)/shard_map/all_to_all | solution.py:455
  76.0 4.1 %all-gather.2 = bf16[32,24,128]{2,1,0:T(8,128)(2,1)S(1)} all-gather(bf16[16,24,128]{2,1,0:T(8,128)(2,1)S(1)} %all-to-all-done.3), channel_id=4, replica_groups=mesh['sec'=2,'grp'=16,'dev'=16] {'sec'}, dimensions={0}, use_global_device_ids=true | all-gather | bytes 294912 | tf_op jit(solution)/shard_map/all_gather | solution.py:456
  80.1 0.7 shard_map.140
  80.8 0.0 copy-start.1
  80.8 24.0 %all_to_all.38.sums_ref = bf16[16,200,128]{2,1,0:T(8,128)(2,1)S(1)} all-to-all(bf16[16,200,128]{2,1,0:T(8,128)(2,1)S(1)} %shard_map.140), channel_id=1, replica_groups=mesh['sec'=2,'grp'=16,'dev'=16] {'dev'}, dimensions={0} | all-to-all | bytes 1638400 | tf_op jit(solution)/shard_map/all_to_all | solution.py:469
  104.9 0.3 shard_map.141
  105.2 15.4 %all_to_all.39.packed_ref = bf16[16,24,512]{2,1,0:T(8,128)(2,1)S(1)} all-to-all(bf16[16,24,512]{2,1,0:T(8,128)(2,1)S(1)} %shard_map.141), channel_id=1, replica_groups=mesh['sec'=2,'grp'=16,'dev'=16] {'dev'}, dimensions={0} | all-to-all | bytes 786432 | tf_op jit(solution)/shard_map/all_to_all | solution.py:478
  120.6 0.0 copy-done.1
  120.6 0.5 shard_map.142
  121.1 6.0 %all-gather.3 = bf16[32,24,128]{2,1,0:T(8,128)(2,1)S(1)} all-gather(bf16[16,24,128]{2,1,0:T(8,128)(2,1)S(1)} %get-tuple-element.19), channel_id=5, replica_groups=mesh['sec'=2,'grp'=16,'dev'=16] {'sec'}, dimensions={0}, use_global_device_ids=true | all-gather | bytes 294912 | tf_op jit(solution)/shard_map/all_gather | solution.py:439
  127.0 0.1 shard_map.143
  127.1 11.7 %all_to_all.40.returned_ref = bf16[16,24,128]{2,1,0:T(8,128)(2,1)S(1)} all-to-all(bf16[16,24,128]{2,1,0:T(8,128)(2,1)S(1)} %shard_map.143), channel_id=1, replica_groups=mesh['sec'=2,'grp'=16,'dev'=16] {'grp'}, dimensions={0} | all-to-all | bytes 196608 | tf_op jit(solution)/shard_map/all_to_all | solution.py:490
  138.9 0.7 shard_map.144
  (4 shorter events, 0.1 us)
Async XLA Ops:
  0.0 25.3 %copy-start = (bf16[4,512,128]{2,1,0:T(8,128)(2,1)S(1)}, bf16[4,512,128]{2,1,0:T(8,128)(2,1)}, u32[]{:S(2)}) copy-start(bf16[4,512,128]{2,1,0:T(8,128)(2,1)} %param.19) | copy-start | bytes 1572868
  0.8 42.7 %copy-start.2 = (bf16[512,448]{0,1:T(8,128)(2,1)S(1)}, bf16[512,448]{0,1:T(8,128)(2,1)}, u32[]{:S(2)}) copy-start(bf16[512,448]{0,1:T(8,128)(2,1)} %param.20) | copy-start | bytes 1376260
  12.4 48.9 %copy-start.3 = (f32[448,16]{0,1:T(8,128)S(1)}, f32[448,16]{0,1:T(8,128)}, u32[]{:S(2)}) copy-start(f32[448,16]{0,1:T(8,128)} %param.23) | copy-start | bytes 86020
  12.4 48.9 %copy-start.4 = (bf16[8,448]{1,0:T(8,128)(2,1)S(1)}, bf16[8,448]{1,0:T(8,128)(2,1)}, u32[]{:S(2)}) copy-start(bf16[8,448]{1,0:T(8,128)(2,1)} %resid_ref.1) | copy-start | bytes 21508
  12.4 48.9 %copy-start.5 = (s32[8,8]{1,0:T(8,128)S(1)}, s32[8,8]{1,0:T(8,128)}, u32[]{:S(2)}) copy-start(s32[8,8]{1,0:T(8,128)} %routes_ref.1) | copy-start | bytes 772
  12.4 48.9 %copy-start.6 = (s32[8,8]{1,0:T(8,128)S(1)}, s32[8,8]{1,0:T(8,128)}, u32[]{:S(2)}) copy-start(s32[8,8]{1,0:T(8,128)} %slots_ref.1) | copy-start | bytes 772
  12.5 48.9 %copy-start.7 = (f32[448]{0:T(512)S(1)}, f32[448]{0:T(512)}, u32[]{:S(2)}) copy-start(f32[448]{0:T(512)} %param.22) | copy-start | bytes 5380
  25.3 41.4 %copy-start.8 = (bf16[1,448,2,1024]{3,2,1,0:T(2,128)(2,1)S(1)}, bf16[1,448,2,1024]{3,2,1,0:T(2,128)(2,1)}, u32[]{:S(2)}) copy-start(bf16[1,448,2,1024]{3,2,1,0:T(2,128)(2,1)} %param.26) | copy-start | bytes 5505028
  62.5 13.6 %all-to-all-start.3 = ((bf16[16,24,128]{2,1,0:T(8,128)(2,1)}), bf16[16,24,128]{2,1,0:T(8,128)(2,1)S(1)}, u32[]{:S(2)}, u32[]{:S(2)}) async-start(bf16[16,24,128]{2,1,0:T(8,128)(2,1)} %get-tuple-element.18), calls=%async_computation.3 | async-start | bytes 196608 | tf_op jit(solution)/shard_map/all_to_all | solution.py:455
  80.8 39.8 %copy-start.1 = (bf16[1,1024,448]{1,2,0:T(8,128)(2,1)S(1)}, bf16[1,1024,448]{1,2,0:T(8,128)(2,1)}, u32[]{:S(2)}) copy-start(bf16[1,1024,448]{1,2,0:T(8,128)(2,1)} %param.27) | copy-start | bytes 2752516
